TPU v7x, 128 devices: a whole 4x4x4 slice. The times are simulated.
128 devices in a mesh: dp: 8 (over x_hi, z), mp: 16 (over x_lo, y, core).
Axes of the slice: x: 4 (x_hi: 2, x_lo: 2; x = x_hi * 2 + x_lo), y: 4, z: 4, core: 2. Of those that a mesh axis runs over, the one named last changes fastest.
Arguments:
- tokens: bfloat16 [4096, 6144], P('dp'), may hold values from -6 to 6, as said below
- norm_gain: float32 [6144], replicated, may hold values from 0.5 to 1.5
- qkv_weight: bfloat16 [6144, 3, 4096], P('dp', None, 'mp'), as said below
- qk_gains: float32 [2, 128], replicated, may hold values from 0.6 to 6, as said below
- in_weight: bfloat16 [6144, 12288], P('dp', 'mp'), may hold values from -0.078125 to 0.078125
- in_bias: float32 [12288], P('mp'), may hold values from -3 to 3
- out_weight: bfloat16 [4096, 6144], P('mp', 'dp'), may hold values from -0.09375 to 0.09375
- mlp_out_weight: bfloat16 [12288, 6144], P('mp', 'dp'), may hold values from -0.0546875 to 0.0546875
- out_bias: float32 [6144], replicated, may hold values from -3 to 3
- targets: bfloat16 [4096, 3072], P('dp'), may hold values from -6 to 6
Outputs:
- gram_matrix: float32 [6144, 6144], P('mp', 'dp')
- cross_matrix: float32 [6144, 3072], P('mp', 'dp')
Inputs may be any that keep to these rules, and one draw needn't show every extreme that they name: `tokens`: activations of order one. `qkv_weight`: entries of order one over the square root of 6144. `qk_gains`: positive gains.
All inputs are finite; a program needn't handle non-finite values.
Results may differ from a plain program's by a relative error of at most 0.025.
Values may be sent and summed in bfloat16 or wider, within the bound.
No kernel may reach another device: no remote copies, remote signals or barrier semaphores. Data moves between devices by JAX's collectives and lax.ppermute only.
A program may use at most 128 MiB of HBM per device.

v0:
```python
import functools

import jax
import jax.numpy as jnp
from jax import lax
from jax.experimental import pallas as pl
from jax.experimental.pallas import tpu as pltpu
from jax.sharding import Mesh, PartitionSpec as P

HEAD = 128
BF = jnp.bfloat16
F32 = jnp.float32
LOG2E = 1.4426950408889634


def layer_norm(inputs, norm_scale):
    center = jnp.mean(inputs, axis=-1, keepdims=True)
    spread = jnp.mean(jnp.square(inputs - center), axis=-1, keepdims=True)
    return (inputs - center) * lax.rsqrt(spread + 1e-06) * norm_scale


def swap(x, axis, mask=1):
    size = lax.axis_size(axis)
    return lax.ppermute(x, axis, [(i, i ^ mask) for i in range(size)])


def dyn(x, start, size, axis):
    return lax.dynamic_slice_in_dim(x, start, size, axis)


def dot(a, b):
    return jnp.dot(a, b, preferred_element_type=F32)


def after(x, *others):
    return lax.optimization_barrier((x,) + others)[0]


def near(x, axis):
    return swap(x, axis, 1), swap(x, axis, 3)


def opposite(one, three, axis):
    half = one.shape[0] // 2
    return swap(one[:half], axis, 3), swap(three[half:], axis, 1)


def ring_gather(x, axis):
    one, three = near(x, axis)
    return [x, one, jnp.concatenate(opposite(one, three, axis)), three]


def in_order(blocks, index):
    laid = [lax.select_n(index ^ i, *blocks) for i in range(len(blocks))]
    return jnp.concatenate(laid)


def both(flag, first, second, axis=0):
    return jnp.where(
        flag == 0,
        jnp.concatenate([first, second], axis=axis),
        jnp.concatenate([second, first], axis=axis),
    )


def norm_kernel(place, tokens_ref, gain_ref, *out_refs):
    block = tokens_ref.shape[1] // 8
    values = tokens_ref[...].astype(F32)
    center = jnp.mean(values, axis=-1, keepdims=True)
    spread = jnp.mean(jnp.square(values - center), axis=-1, keepdims=True)
    scale = lax.rsqrt(spread + 1e-06)
    for relative in range(4):
        column = pl.multiple_of((place[1] * 4 + (place[2] ^ relative)) * block, 128)
        part = tokens_ref[:, pl.ds(column, block)].astype(F32)
        normed = ((part - center) * scale * gain_ref[:, pl.ds(column, block)]).astype(BF)
        out_refs[relative][...] = normed


def norm_rows(tokens, gain, place, count, piece):
    width = tokens.shape[1]
    block = width // 8
    out = jax.ShapeDtypeStruct((count * piece, block), BF)
    return pl.pallas_call(
        norm_kernel,
        grid_spec=pltpu.PrefetchScalarGridSpec(
            num_scalar_prefetch=1,
            grid=(count,),
            in_specs=[
                pl.BlockSpec((piece, width), lambda i, place: (i ^ place[0], 0)),
                pl.BlockSpec((1, width), lambda i, place: (0, 0)),
            ],
            out_specs=[pl.BlockSpec((piece, block), lambda i, place: (i, 0))] * 4,
        ),
        out_shape=[out] * 4,
        compiler_params=pltpu.CompilerParams(vmem_limit_bytes=24 * 2**20),
        name="norm_rows",
    )(place, tokens, gain.reshape(1, width))


def attend_kernel(q_ref, *refs):
    kv_refs, out_ref = refs[:-1], refs[-1]
    queries = q_ref[...]
    scores = [
        lax.dot_general(queries, kv[:, :HEAD], (((1,), (1,)), ((), ())), preferred_element_type=F32)
        for kv in kv_refs
    ]
    top = functools.reduce(jnp.maximum, [jnp.max(s, axis=-1, keepdims=True) for s in scores])
    factor = HEAD ** (-0.5) * LOG2E
    total, mixed = 0.0, 0.0
    for part, kv in zip(scores, kv_refs):
        weights = jnp.exp2((part - top) * factor)
        total = total + jnp.sum(weights, axis=-1, keepdims=True)
        mixed = mixed + dot(weights.astype(BF), kv[:, HEAD:])
    out_ref[...] = (mixed / total).astype(BF)


def attend(queries, kv_parts):
    rows = queries.shape[0]
    step = min(256, rows)
    keys = sum(part.shape[0] for part in kv_parts)
    return pl.pallas_call(
        attend_kernel,
        grid=(rows // step,),
        in_specs=[pl.BlockSpec((step, HEAD), lambda i: (i, 0))]
        + [pl.BlockSpec(part.shape, lambda i: (0, 0), pipeline_mode=pl.Buffered(1)) for part in kv_parts],
        out_specs=pl.BlockSpec((step, HEAD), lambda i: (i, 0)),
        out_shape=jax.ShapeDtypeStruct((rows, HEAD), BF),
        compiler_params=pltpu.CompilerParams(vmem_limit_bytes=24 * 2**20),
        name="attend",
    )(queries, *kv_parts)


def pieces_dot(parts, weights, part=None):
    w0, w1, low, high, w3 = weights
    n0, n1, n2, n3 = parts
    half = n2.shape[1] // 2
    pairs = [(n0[...], w0), (n1[...], w1), (n3[...], w3), (n2[:, :half], low), (n2[:, half:], high)]
    total = None
    for rows, w in pairs:
        term = dot(rows, w[...] if part is None else w[part])
        total = term if total is None else total + term
    return total


def qkv_kernel(place, *refs):
    own, far, weights = refs[0:4], refs[4:8], refs[8:13]
    give_ref, keep_ref, hold = refs[13:]
    rows = own[0].shape[0]
    hold[:rows] = pieces_dot(own, weights, 0)
    hold[rows:] = pieces_dot(far, weights, 0)
    mine = pl.ds(pl.multiple_of(place[0] * HEAD, HEAD), HEAD)
    other = pl.ds(pl.multiple_of((1 - place[0]) * HEAD, HEAD), HEAD)
    keep_ref[...] = hold[:, mine]
    give_ref[:rows] = hold[rows:, other].astype(BF)
    give_ref[rows:] = hold[:rows, other].astype(BF)


def project_qkv(own, far, weights, xh):
    rows, block = own[0].shape

    def whole(x):
        return pl.BlockSpec(x.shape, lambda i, place: (0, 0), pipeline_mode=pl.Buffered(1))

    def third(w):
        return pl.BlockSpec((1,) + w.shape[1:], lambda i, place: (i, 0, 0))

    column = pl.BlockSpec((2 * rows, HEAD), lambda i, place: (0, i))
    return pl.pallas_call(
        qkv_kernel,
        grid_spec=pltpu.PrefetchScalarGridSpec(
            num_scalar_prefetch=1,
            grid=(3,),
            in_specs=[whole(x) for x in (*own, *far)] + [third(w) for w in weights],
            out_specs=[column, column],
            scratch_shapes=[pltpu.VMEM((2 * rows, 2 * HEAD), F32)],
        ),
        out_shape=[
            jax.ShapeDtypeStruct((2 * rows, 3 * HEAD), BF),
            jax.ShapeDtypeStruct((2 * rows, 3 * HEAD), F32),
        ],
        compiler_params=pltpu.CompilerParams(vmem_limit_bytes=32 * 2**20),
        name="project_qkv",
    )(jnp.reshape(xh, (1,)), *own, *far, *weights)


def mlp_kernel(*refs):
    refs[9][...] = pieces_dot(refs[0:4], refs[4:9]).astype(refs[9].dtype)


def project_mlp(parts, weights, dtype):
    rows, block = parts[0].shape
    wide = weights[0].shape[1]
    step = wide // 3
    return pl.pallas_call(
        mlp_kernel,
        grid=(3,),
        in_specs=[pl.BlockSpec(x.shape, lambda i: (0, 0), pipeline_mode=pl.Buffered(1)) for x in parts]
        + [pl.BlockSpec((w.shape[0], step), lambda i: (0, i)) for w in weights],
        out_specs=pl.BlockSpec((rows, step), lambda i: (0, i)),
        out_shape=jax.ShapeDtypeStruct((rows, wide), dtype),
        compiler_params=pltpu.CompilerParams(vmem_limit_bytes=48 * 2**20),
        name="project_mlp",
    )(*parts, *weights)


def output_kernel(place, *refs):
    attended, hidden, w_ref, out_ref = refs[0:4], refs[4:8], refs[8], refs[9]
    first = w_ref[0, pl.ds(pl.multiple_of(place[0] * HEAD, HEAD), HEAD)]
    second = w_ref[0, pl.ds(pl.multiple_of((1 - place[0]) * HEAD, HEAD), HEAD)]
    heads = jnp.concatenate([first, second])
    for i in range(4):
        a, h = attended[i], hidden[i]
        total = dot(h[...], w_ref[0, 2 * HEAD :]) + dot(a[...], heads)
        out_ref[0, i] = total.astype(out_ref.dtype)


def project_out(attended, hidden, which, weights, xh, dtype):
    rows = hidden[2].shape[0]
    _, depth, block = weights.shape
    step = block // 3

    def rows_of(x):
        at = 0 if x.shape[0] == rows else which
        return pl.BlockSpec((rows, x.shape[1]), lambda side, i, place: (at, 0), pipeline_mode=pl.Buffered(1))

    return pl.pallas_call(
        output_kernel,
        grid_spec=pltpu.PrefetchScalarGridSpec(
            num_scalar_prefetch=1,
            grid=(2, 3),
            in_specs=[rows_of(x) for x in (*attended, *hidden)]
            + [pl.BlockSpec((1, depth, step), lambda side, i, place: (side, 0, i))],
            out_specs=pl.BlockSpec((1, 4, rows, step), lambda side, i, place: (side, 0, 0, i)),
        ),
        out_shape=jax.ShapeDtypeStruct((2, 4, rows, block), dtype),
        compiler_params=pltpu.CompilerParams(vmem_limit_bytes=60 * 2**20),
        name="project_out",
    )(jnp.reshape(xh, (1,)), *attended, *hidden, weights)


def moment_kernel(total_tokens, place, *refs):
    columns, parts, others = refs[0:5], refs[5:10], refs[10:15]
    gram_ref, cross_ref, hold = refs[15:]
    tokens_here = hold.shape[3] // 2
    index = pl.program_id(0)

    @pl.when(index == 0)
    def _():
        for relative, ref in ((0, columns[0]), (1, columns[1]), (3, columns[4])):
            for side in range(2):
                rows = ref[side * 2 * tokens_here : (side + 1) * 2 * tokens_here]
                hold[relative ^ place[0], side ^ place[1]] = rows.T
        for side in range(2):
            hold[2 ^ place[0], side ^ place[1]] = columns[2 + side][...].T

    def part_rows(refs, relative, side):
        if relative == 2:
            return refs[2 + side][...]
        ref = refs[relative if relative < 2 else 4]
        return ref[side * tokens_here : (side + 1) * tokens_here]

    total = None
    for relative in range(4):
        for side in range(2):
            full = jnp.concatenate([part_rows(parts, relative, side), part_rows(others, relative, side)])
            term = dot(hold[relative, side], full)
            total = term if total is None else total + term
    total = total / total_tokens

    @pl.when(index < pl.num_programs(0) - 1)
    def _():
        gram_ref[...] = total

    @pl.when(index == pl.num_programs(0) - 1)
    def _():
        cross_ref[...] = total


def moments(columns, parts, others, place, block, total_tokens):
    narrow = columns[0].shape[1]
    step = parts[0].shape[1] - block
    steps = block // step
    kernel = functools.partial(moment_kernel, total_tokens)

    def whole(x):
        return pl.BlockSpec(x.shape, lambda i, place: (0, 0), pipeline_mode=pl.Buffered(1))

    def column(x):
        return pl.BlockSpec((x.shape[0], step), lambda i, place: (0, i))

    return pl.pallas_call(
        kernel,
        grid_spec=pltpu.PrefetchScalarGridSpec(
            num_scalar_prefetch=1,
            grid=(steps + 1,),
            in_specs=[whole(x) for x in columns] + [column(x) for x in (*parts, *others)],
            out_specs=[
                pl.BlockSpec((narrow, step), lambda i, place: (0, jnp.minimum(i, steps - 1))),
                pl.BlockSpec((narrow, step), lambda i, place: (0, 0)),
            ],
            scratch_shapes=[pltpu.VMEM((4, 2, narrow, columns[2].shape[0]), BF)],
        ),
        out_shape=[
            jax.ShapeDtypeStruct((narrow, block), F32),
            jax.ShapeDtypeStruct((narrow, step), F32),
        ],
        compiler_params=pltpu.CompilerParams(vmem_limit_bytes=60 * 2**20),
        name="moments",
    )(place, *columns, *parts, *others)


def on_device(
    tokens,
    norm_gain,
    qkv_weight,
    qk_gains,
    in_weight,
    in_bias,
    out_weight,
    mlp_out_weight,
    out_bias,
    targets,
):
    xh, z, xl, y, c = (lax.axis_index(a) for a in ("xh", "z", "xl", "y", "c"))
    rows, width = tokens.shape
    block = width // 8
    target_block = targets.shape[1] // 8
    piece = rows // 16
    half = rows // 2
    mine = (c * 4 + y) * 2 + xl

    qkv_w = qkv_weight.transpose(1, 0, 2)
    qkv_w1, qkv_w3 = near(qkv_w, "z")

    share = 2 * piece
    first_rows = dyn(tokens, (c * 4 + y) * share, share, 0)
    give_norm = norm_rows(first_rows, norm_gain, jnp.stack([xl, 1 - xh, z]), 2, piece)
    give_norm = jnp.concatenate(give_norm, axis=1)
    got = swap(give_norm, "xh")
    norm_own = norm_rows(after(tokens, give_norm), norm_gain, jnp.stack([mine, xh, z]), 16, piece)

    out_raw, got, *norm_own = lax.optimization_barrier((out_weight, got, *norm_own))
    depth = mlp_out_weight.shape[0] // 3
    mlp_raws = [mlp_out_weight[i * depth : (i + 1) * depth] for i in range(3)]
    far_ws = [swap(out_raw, "xh")]
    got_one, got_three = near(got, "y")
    got_one, got_three, qkv_w1, qkv_w3, far_ws[0], mlp_raws[0] = lax.optimization_barrier(
        (got_one, got_three, qkv_w1, qkv_w3, far_ws[0], mlp_raws[0])
    )
    far_ws.append(swap(mlp_raws[0], "xh"))
    middle = block // 2
    qkv_low = swap(qkv_w1[:, :middle], "z", 3)
    qkv_high = swap(qkv_w3[:, middle:], "z", 1)
    got_low, got_high = opposite(got_one, got_three, "y")
    got_low, got_high, qkv_low, qkv_high, in_raw, far_ws[1], mlp_raws[1] = lax.optimization_barrier(
        (got_low, got_high, qkv_low, qkv_high, in_weight, far_ws[1], mlp_raws[1])
    )
    far_ws.append(swap(mlp_raws[1], "xh"))
    around = jnp.concatenate([got, got_one, got_low, got_high, got_three])
    beyond = swap(around, "c")
    in_w1, in_w3 = near(in_raw, "z")
    norm_far = [
        jnp.concatenate([p[:, i * block : (i + 1) * block] for p in (around, beyond)]) for i in range(4)
    ]

    give, keep = project_qkv(norm_own, norm_far, (qkv_w, qkv_w1, qkv_low, qkv_high, qkv_w3), xh)
    give, far_ws[2] = lax.optimization_barrier((give, far_ws[2]))
    taken = swap(give, "xh")
    in_w1, in_w3, *norms = lax.optimization_barrier((in_w1, in_w3, *norm_own, *norm_far, give))
    norm_own, norm_far = norms[:4], norms[4:8]
    in_first, in_last = in_w1[:middle], in_w3[middle:]
    in_low, in_high = swap(in_first, "z", 3), swap(in_last, "z", 1)
    taken = after(taken, in_first, in_last)
    qkv = keep + taken.astype(F32)
    queries = layer_norm(qkv[:, :HEAD], qk_gains[0]).astype(BF)
    own_keys = layer_norm(qkv[:, HEAD : 2 * HEAD], qk_gains[1]).astype(BF)
    own_kv = jnp.concatenate([own_keys, qkv[:, 2 * HEAD :].astype(BF)], axis=1)
    kv_one, kv_three = near(own_kv, "z")

    in_ws = (in_weight, in_w1, in_low, in_high, in_w3)
    mlp_give = project_mlp(norm_far, in_ws, BF)
    mlp_far = swap(mlp_give, "xh")
    mlp_give, *norm_own = lax.optimization_barrier((mlp_give, *norm_own))
    mlp_own = project_mlp(norm_own, in_ws, F32)
    mlp_own, kv_one, kv_three = lax.optimization_barrier((mlp_own, kv_one, kv_three))
    kv_low, kv_high = opposite(kv_one, kv_three, "z")
    mlp_far, kv_low, kv_high = lax.optimization_barrier((mlp_far, kv_low, kv_high))
    kv_parts = [own_kv, kv_one, kv_three, kv_low, kv_high]
    mlp_input = mlp_own + mlp_far.astype(F32)
    hidden = jax.nn.gelu(mlp_input + in_bias, approximate=False).astype(BF)
    hidden, queries, mlp_raws[2] = lax.optimization_barrier((hidden, queries, mlp_raws[2]))
    far_ws.append(swap(mlp_raws[2], "xh"))
    hid_one, hid_three = near(hidden, "z")

    attended = attend(queries, kv_parts)
    attended, hid_one, hid_three, far_ws[3] = lax.optimization_barrier((attended, hid_one, hid_three, far_ws[3]))
    out_ws = jnp.stack([jnp.concatenate([out_weight, mlp_out_weight]), jnp.concatenate(far_ws)])
    hid_low, hid_high = opposite(hid_one, hid_three, "z")
    attended = jnp.concatenate([attended[:rows], swap(attended[rows:], "xh")], axis=1)
    att_one, att_three = near(attended, "z")
    att_two = swap(attended, "z", 2)

    att_one, att_two, att_three, hid_low, hid_high, out_ws = lax.optimization_barrier(
        (att_one, att_two, att_three, hid_low, hid_high, out_ws)
    )
    att_parts = (attended, att_one, att_two, att_three)
    hid_keep, hid_give = (hidden, hid_one, hid_low, hid_three), (hidden, hid_one, hid_high, hid_three)

    got_sums = swap(project_out(att_parts, hid_give, 1, out_ws, xh, BF), "c")
    got_sums, raw_tokens, raw_targets = lax.optimization_barrier((got_sums, tokens, targets))

    base_rows = dyn(raw_tokens, mine * piece, piece, 0).reshape(piece, 8, block)
    goal_rows = dyn(raw_targets, mine * piece, piece, 0).reshape(piece, 8, target_block)
    spread_rows = jnp.concatenate([base_rows, goal_rows], axis=2).transpose(1, 0, 2)
    own_spread = lax.all_to_all(spread_rows, ("xh", "z"), split_axis=0, concat_axis=0, tiled=True)
    sums = project_out(att_parts, hid_keep, 0, out_ws, xh, BF)
    own, par = [sums[i].astype(F32) + got_sums[i].astype(F32) for i in range(2)]

    quarter = half // 4

    def chunks(x, start, count):
        return x[:, start * quarter : (start + count) * quarter]

    par_got = swap(chunks(par, 1, 2).astype(BF), "y", 1)
    own_got = swap(chunks(own, 2, 2).astype(BF), "y", 3)
    par_got, own_got, own_spread = lax.optimization_barrier((par_got, own_got, own_spread))
    base = own_spread[:, :, :block].reshape(8 * piece, block)
    own_goals = own_spread[:, :, block:].reshape(8 * piece, target_block)
    par_next = swap((chunks(par, 3, 1) + chunks(par_got, 1, 1).astype(F32)).astype(BF), "y", 3).astype(F32)
    own_next = swap((chunks(own, 1, 1) + chunks(own_got, 0, 1).astype(F32)).astype(BF), "y", 1).astype(F32)
    par_sum = chunks(par, 0, 1) + chunks(par_got, 0, 1).astype(F32) + par_next
    own_sum = chunks(own, 0, 1) + chunks(own_got, 1, 1).astype(F32) + own_next
    sums = jnp.concatenate([own_sum, par_sum], axis=2)
    sums = sums[:, :piece] + swap(sums[:, piece:].astype(BF), "xl").astype(F32)
    theirs = swap(sums[:, :, block:].astype(BF), "xh").astype(F32)
    sum_own = in_order([sums[i, :, :block] for i in range(4)], z)
    sum_theirs = in_order([theirs[i] for i in range(4)], z)
    total = both(xh, sum_own, sum_theirs)
    bias = dyn(out_bias, (xh * 4 + z) * block, block, 0)
    out_piece = (base.astype(F32) + bias + total).astype(BF)

    narrow = block // 2

    stay, leave = dyn(out_piece, c * narrow, narrow, 1), dyn(out_piece, (1 - c) * narrow, narrow, 1)
    pair = jnp.concatenate([stay, swap(leave, "c")])
    beside = jnp.concatenate([out_piece, own_goals], axis=1)
    over_xl = swap(beside, "xl")
    pair = lax.ppermute(
        pair,
        ("xh", "z", "xl", "y"),
        [(a * 8 + b, b * 8 + a) for a in range(8) for b in range(8)],
    )
    pair, over_xl = lax.optimization_barrier((pair, over_xl))
    over_xl_pair = jnp.concatenate([beside, over_xl])
    part_one, part_three = near(over_xl_pair, "y")
    pair = jnp.concatenate([pair, swap(pair, "xh")])
    col_one, col_three = near(pair, "z")
    col_one, col_three, part_one, part_three = lax.optimization_barrier((col_one, col_three, part_one, part_three))
    col_low, col_high = opposite(col_one, col_three, "z")
    part_low, part_high = opposite(part_one, part_three, "y")
    col_low, col_high, part_low, part_high = lax.optimization_barrier((col_low, col_high, part_low, part_high))
    columns = [pair, col_one, col_low, col_high, col_three]
    parts = [over_xl_pair, part_one, part_low, part_high, part_three]
    others = [swap(part, "c") for part in parts]
    return moments(columns, parts, others, jnp.stack([y ^ z, xh ^ xl]), block, rows * 8)


def solution(mesh):
    fine = Mesh(mesh.devices.reshape(2, 4, 2, 4, 2), ("xh", "z", "xl", "y", "c"))
    dp, mp = ("xh", "z"), ("xl", "y", "c")
    placed = (
        P(dp, None),
        P(),
        P(dp, None, mp),
        P(),
        P(dp, mp),
        P(mp),
        P(mp, dp),
        P(mp, dp),
        P(),
        P(dp, None),
    )
    return jax.shard_map(
        on_device,
        mesh=fine,
        in_specs=placed,
        out_specs=(P(mp, dp), P(mp, dp)),
        check_vma=False,
    )
```

profile of v0, /device:TPU:1, one launch (start us, length us, event | category | flops | bytes accessed | tf_op | source)
XLA Modules:
  0.0 333.3 jit_solution(690025067371100530)
XLA Ops:
  0.7 2.5 collective-permute-start.3
  3.2 2.2 collective-permute-start.4
  8.1 2.8 collective-permute-start
  10.9 2.8 copy-done.1
  13.7 6.3 %norm_rows.3 = (bf16[512,768]{1,0:T(8,128)(2,1)S(1)}, bf16[512,768]{1,0:T(8,128)(2,1)S(1)}, bf16[512,768]{1,0:T(8,128)(2,1)S(1)}, bf16[512,768]{1,0:T(8,128)(2,1)S(1)}) custom-call(s32[3]{0:T(128)S(1)} %get-tuple-element.208.place, bf16[512,6144]{1,0:T(8,128)(2,1)S(1)} %copy-done.1, f32[1,6144]{1,0:T(1,128)S(1)} %bitcast.59), custom_call_target="tpu_custom_call" | custom-call | tf_op jit(solution)/shard_map/norm_rows/pallas_call | solution.py:83
  25.2 4.1 %collective-permute-done.1 = bf16[64,3072]{1,0:T(8,128)(2,1)S(1)} collective-permute-done((bf16[64,3072]{1,0:T(8,128)(2,1)S(1)}, bf16[64,3072]{1,0:T(8,128)(2,1)S(1)}, u32[]{:S(2)}, u32[]{:S(2)}) %collective-permute-start.1) | collective-permute-done | bytes 393248 | tf_op jit(solution)/shard_map/ppermute | solution.py:24
  29.3 2.2 collective-permute-done.2
  36.7 2.0 collective-permute-start.10
  38.8 2.8 collective-permute-start.6
  41.7 3.2 collective-permute-done.6
  48.1 4.2 %collective-permute-start.13 = (bf16[256,3072]{1,0:T(8,128)(2,1)S(1)}, bf16[256,3072]{1,0:T(8,128)(2,1)S(1)}, u32[]{:S(2)}, u32[]{:S(2)}) collective-permute-start(bf16[256,3072]{1,0:T(8,128)(2,1)S(1)} %constant_dynamic-update-slice_fusion.4), channel_id=1, source_target_pairs={{0,1},{1,0},{2,3},{3,2},{4,5},{5,4},{6,7},{7,6},{8,9},{9,8},{10,11... | collective-permute-start | bytes 4718600 | tf_op jit(solution)/shard_map/ppermute | solution.py:24
  57.3 7.4 %project_qkv.1 = (bf16[1024,384]{1,0:T(8,128)(2,1)S(1)}, f32[1024,384]{1,0:T(8,128)S(1)}) custom-call(s32[1]{0:T(128)} %bitcast.2.place, bf16[512,768]{1,0:T(8,128)(2,1)S(1)} %get-tuple-element.122.refs_0_, bf16[512,768]{1,0:T(8,128)(2,1)S(1)} %get-tuple-element.123.refs_1_, bf16[512,768]{1,0:T(8,128)(2,1)S(1)} %get-tuple-element.124.refs_2_, ...), custom_call_target="tpu_custom_call" | custom-call | tf_op jit(solution)/shard_map/project_qkv/pallas_call | solution.py:168
  67.2 12.6 %collective-permute-done.11.refs_5_ = bf16[768,768]{1,0:T(8,128)(2,1)S(1)} collective-permute-done((bf16[768,768]{1,0:T(8,128)(2,1)S(1)}, bf16[768,768]{1,0:T(8,128)(2,1)S(1)}, u32[]{:S(2)}, u32[]{:S(2)}) %collective-permute-start.11) | collective-permute-done | bytes 1179680 | tf_op jit(solution)/shard_map/ppermute | solution.py:24
  88.6 8.4 %collective-permute-done.15.refs_6_ = bf16[384,768]{1,0:T(8,128)(2,1)S(1)} collective-permute-done((bf16[384,768]{1,0:T(8,128)(2,1)S(1)}, bf16[384,768]{1,0:T(8,128)(2,1)S(1)}, u32[]{:S(2)}, u32[]{:S(2)}) %collective-permute-start.15) | collective-permute-done | bytes 589856 | tf_op jit(solution)/shard_map/ppermute | solution.py:24
  97.2 4.6 %project_mlp.2 = bf16[512,768]{1,0:T(8,128)(2,1)S(1)} custom-call(bf16[512,768]{1,0:T(8,128)(2,1)S(1)} %pad_maximum_fusion.3.refs_4_.refs_0_, bf16[512,768]{1,0:T(8,128)(2,1)S(1)} %pad_maximum_fusion.4.refs_5_.refs_1_, bf16[512,768]{1,0:T(8,128)(2,1)S(1)} %pad_maximum_fusion.5.refs_6_.refs_2_, bf16[512,768]{1,0:T(8,128)(2,1)S(1)} %pad_maximum_fusion.6.refs_7_.refs_3_, ...), custom_call_target="tpu_custom_call" | custom-call | tf_op jit(solution)/shard_map/project_mlp/pallas_call | solution.py:194
  103.6 5.4 %project_mlp.3 = f32[512,768]{1,0:T(8,128)} custom-call(bf16[512,768]{1,0:T(8,128)(2,1)S(1)} %get-tuple-element.122.refs_0_, bf16[512,768]{1,0:T(8,128)(2,1)S(1)} %get-tuple-element.123.refs_1_, bf16[512,768]{1,0:T(8,128)(2,1)S(1)} %get-tuple-element.124.refs_2_, bf16[512,768]{1,0:T(8,128)(2,1)S(1)} %get-tuple-element.125.refs_3_, ...), custom_call_target="tpu_custom_call" | custom-call | tf_op jit(solution)/shard_map/project_mlp/pallas_call | solution.py:194
  110.6 7.6 %collective-permute-done.20 = bf16[512,768]{1,0:T(8,128)(2,1)S(1)} collective-permute-done((bf16[512,768]{1,0:T(8,128)(2,1)S(1)}, bf16[512,768]{1,0:T(8,128)(2,1)S(1)}, u32[]{:S(2)}, u32[]{:S(2)}) %collective-permute-start.20) | collective-permute-done | bytes 786464 | tf_op jit(solution)/shard_map/ppermute | solution.py:24
  118.2 4.7 %fusion.2.refs_4_ = bf16[512,768]{1,0:T(8,128)(2,1)S(1)} fusion(f32[512,768]{1,0:T(8,128)} %project_mlp.3, bf16[512,768]{1,0:T(8,128)(2,1)S(1)} %collective-permute-done.20, f32[768]{0:T(1024)S(1)} %copy-done.27), kind=kLoop, calls=%fused_computation.6 | loop fusion | flops 26738688 | bytes 3148800 | tf_op jit(solution)/shard_map/convert_element_type | solution.py:390
  126.6 8.0 %attend.1 = bf16[1024,128]{1,0:T(8,128)(2,1)S(1)} custom-call(bf16[1024,128]{1,0:T(8,128)(2,1)S(1)} %get-tuple-element.132.q_ref, bf16[1024,256]{1,0:T(8,128)(2,1)S(1)} %pad_maximum_fusion.8.refs_0_, bf16[1024,256]{1,0:T(8,128)(2,1)S(1)} %collective-permute-done.18.refs_1_, bf16[1024,256]{1,0:T(8,128)(2,1)S(1)} %collective-permute-done.19.refs_2_, ...), custom_call_target="tpu_custom_call" | custom-call | tf_op jit(solution)/shard_map/attend/pallas_call | solution.py:121
  134.6 2.1 collective-permute-done.23.refs_5_
  136.7 2.3 collective-permute-done.24.refs_7_
  142.3 2.2 collective-permute-done.26
  144.6 2.8 collective-permute-start.28
  152.1 6.1 %collective-permute-done.28.refs_2_ = bf16[512,256]{1,0:T(8,128)(2,1)S(1)} collective-permute-done((bf16[512,256]{1,0:T(8,128)(2,1)S(1)}, bf16[512,256]{1,0:T(8,128)(2,1)S(1)}, u32[]{:S(2)}, u32[]{:S(2)}) %collective-permute-start.28) | collective-permute-done | bytes 262176 | tf_op jit(solution)/shard_map/ppermute | solution.py:24
  160.5 8.0 %project_out.3 = bf16[2,4,256,768]{3,2,1,0:T(8,128)(2,1)} custom-call(s32[1]{0:T(128)} %bitcast.2.place, bf16[512,256]{1,0:T(8,128)(2,1)} %copy-done.15, bf16[512,256]{1,0:T(8,128)(2,1)} %copy-done.19, bf16[512,256]{1,0:T(8,128)(2,1)} %copy-done.20, bf16[512,256]{1,0:T(8,128)(2,1)} %copy-done.21, bf16[512,768]{1,0:T(8,128)(2,1)} %copy-done.10, ...), custom_call_target="tpu_custom_call" | custom-call | tf_op jit(solution)/shard_map/project_out/pallas_call | solution.py:226
  168.5 7.2 %collective-permute-start.32 = (bf16[2,4,256,768]{3,2,1,0:T(8,128)(2,1)}, bf16[2,4,256,768]{3,2,1,0:T(8,128)(2,1)}, u32[]{:S(2)}, u32[]{:S(2)}) collective-permute-start(bf16[2,4,256,768]{3,2,1,0:T(8,128)(2,1)} %project_out.3), channel_id=1, source_target_pairs={{0,1},{1,0},{2,3},{3,2},{4,5},{5,4},{6,7},{7,6},{8,9},{9,8},{10,11... | collective-permute-start | bytes 9437192 | tf_op jit(solution)/shard_map/ppermute | solution.py:24
  175.7 8.0 %project_out.2 = bf16[2,4,256,768]{3,2,1,0:T(8,128)(2,1)} custom-call(s32[1]{0:T(128)} %bitcast.2.place, bf16[512,256]{1,0:T(8,128)(2,1)} %copy-done.15, bf16[512,256]{1,0:T(8,128)(2,1)} %copy-done.19, bf16[512,256]{1,0:T(8,128)(2,1)} %copy-done.20, bf16[512,256]{1,0:T(8,128)(2,1)} %copy-done.21, bf16[512,768]{1,0:T(8,128)(2,1)} %copy-done.10, ...), custom_call_target="tpu_custom_call" | custom-call | tf_op jit(solution)/shard_map/project_out/pallas_call | solution.py:226
  183.8 3.5 %add_bitcast_fusion.1 = (f32[4,256,768]{2,1,0:T(8,128)S(1)}, f32[4,256,768]{2,1,0:T(8,128)S(1)}) fusion(bf16[2,4,256,768]{3,2,1,0:T(8,128)(2,1)} %project_out.2, bf16[2,4,256,768]{3,2,1,0:T(8,128)(2,1)} %collective-permute-done.32), kind=kLoop, calls=%fused_computation.2 | loop fusion | flops 4718592 | bytes 12582912 | tf_op jit(solution)/shard_map/add | solution.py:417
  188.2 2.0 collective-permute-start.34
  191.5 14.9 %all_to_all.5 = bf16[8,32,1152]{2,1,0:T(8,128)(2,1)} all-to-all(bf16[8,32,1152]{2,1,0:T(8,128)(2,1)S(1)} %copy.14), channel_id=1, replica_groups=mesh['xh'=2,'z'=4,'xl'=2,'y'=4,'c'=2] {'xh','z'}, dimensions={0} | all-to-all | bytes 1179648 | tf_op jit(solution)/shard_map/all_to_all | solution.py:415
  208.4 2.0 collective-permute-start.36
  210.6 8.6 %collective-permute-done.36 = bf16[4,64,768]{2,1,0:T(8,128)(2,1)S(1)} collective-permute-done((bf16[4,64,768]{2,1,0:T(8,128)(2,1)S(1)}, bf16[4,64,768]{2,1,0:T(8,128)(2,1)S(1)}, u32[]{:S(2)}, u32[]{:S(2)}) %collective-permute-start.36) | collective-permute-done | bytes 393248 | tf_op jit(solution)/shard_map/ppermute | solution.py:24
  220.5 7.8 %collective-permute-done.37 = bf16[4,32,1536]{2,1,0:T(8,128)(2,1)S(1)} collective-permute-done((bf16[4,32,1536]{2,1,0:T(8,128)(2,1)S(1)}, bf16[4,32,1536]{2,1,0:T(8,128)(2,1)S(1)}, u32[]{:S(2)}, u32[]{:S(2)}) %collective-permute-start.37) | collective-permute-done | bytes 393248 | tf_op jit(solution)/shard_map/ppermute | solution.py:24
  232.7 2.9 collective-permute-done.38
  237.1 4.5 %collective-permute-start.39 = (bf16[256,384]{1,0:T(8,128)(2,1)S(1)}, bf16[256,384]{1,0:T(8,128)(2,1)S(1)}, u32[]{:S(2)}, u32[]{:S(2)}) collective-permute-start(bf16[256,384]{1,0:T(8,128)(2,1)S(1)} %get-tuple-element.202), channel_id=1, source_target_pairs={{0,1},{1,0},{2,3},{3,2},{4,5},{5,4},{6,7},{7,6},{8,9},{9,8},{10,11... | collective-permute-start | bytes 589832 | tf_op jit(solution)/shard_map/ppermute | solution.py:24
  243.4 13.3 %collective-permute-done.41 = bf16[256,1152]{1,0:T(8,128)(2,1)S(1)} collective-permute-done((bf16[256,1152]{1,0:T(8,128)(2,1)S(1)}, bf16[256,1152]{1,0:T(8,128)(2,1)S(1)}, u32[]{:S(2)}, u32[]{:S(2)}) %collective-permute-start.41) | collective-permute-done | bytes 589856 | tf_op jit(solution)/shard_map/ppermute | solution.py:24
  259.0 6.3 %collective-permute-start.45 = (bf16[512,1152]{1,0:T(8,128)(2,1)}, bf16[512,1152]{1,0:T(8,128)(2,1)}, u32[]{:S(2)}, u32[]{:S(2)}) collective-permute-start(bf16[512,1152]{1,0:T(8,128)(2,1)} %pad_maximum_fusion.1.refs_5_), channel_id=1, source_target_pairs={{0,2},{2,0},{4,6},{6,4},{1,3},{3,1},{5,7},{7,5},{8,10},{10,8},{12,... | collective-permute-start | bytes 3538952 | tf_op jit(solution)/shard_map/ppermute | solution.py:24
  265.4 5.3 %collective-permute-start.46 = (bf16[512,1152]{1,0:T(8,128)(2,1)}, bf16[512,1152]{1,0:T(8,128)(2,1)}, u32[]{:S(2)}, u32[]{:S(2)}) collective-permute-start(bf16[512,1152]{1,0:T(8,128)(2,1)} %pad_maximum_fusion.1.refs_5_), channel_id=1, source_target_pairs={{0,6},{2,4},{4,2},{6,0},{1,7},{3,5},{5,3},{7,1},{8,14},{10,12},{12... | collective-permute-start | bytes 3538952 | tf_op jit(solution)/shard_map/ppermute | solution.py:24
  270.8 3.3 collective-permute-start.43
  274.1 5.8 %collective-permute-start.44 = (bf16[1024,384]{1,0:T(8,128)(2,1)S(1)}, bf16[1024,384]{1,0:T(8,128)(2,1)S(1)}, u32[]{:S(2)}, u32[]{:S(2)}) collective-permute-start(bf16[1024,384]{1,0:T(8,128)(2,1)S(1)} %constant_dynamic-update-slice_fusion.9.refs_0_), channel_id=1, source_target_pairs={{0,48},{16,32},{32,16},{48,0},{1,49},{17,33},{33,17},{49,1},{2,50}... | collective-permute-start | bytes 2359304 | tf_op jit(solution)/shard_map/ppermute | solution.py:24
  279.8 9.6 %collective-permute-done.45.refs_6_ = bf16[512,1152]{1,0:T(8,128)(2,1)} collective-permute-done((bf16[512,1152]{1,0:T(8,128)(2,1)}, bf16[512,1152]{1,0:T(8,128)(2,1)}, u32[]{:S(2)}, u32[]{:S(2)}) %collective-permute-start.45) | collective-permute-done | bytes 1179680 | tf_op jit(solution)/shard_map/ppermute | solution.py:24
  289.4 6.4 %collective-permute-done.46.refs_9_ = bf16[512,1152]{1,0:T(8,128)(2,1)} collective-permute-done((bf16[512,1152]{1,0:T(8,128)(2,1)}, bf16[512,1152]{1,0:T(8,128)(2,1)}, u32[]{:S(2)}, u32[]{:S(2)}) %collective-permute-start.46) | collective-permute-done | bytes 1179680 | tf_op jit(solution)/shard_map/ppermute | solution.py:24
  296.7 2.2 collective-permute-start.47
  302.7 2.9 collective-permute-start.51
  306.6 3.0 collective-permute-start.52
  310.7 2.9 collective-permute-done.49.refs_7_
  314.8 3.8 %collective-permute-start.53 = (bf16[256,1152]{1,0:T(8,128)(2,1)}, bf16[256,1152]{1,0:T(8,128)(2,1)}, u32[]{:S(2)}, u32[]{:S(2)}) collective-permute-start(bf16[256,1152]{1,0:T(8,128)(2,1)} %collective-permute-done.49.refs_7_), channel_id=1, source_target_pairs={{0,1},{1,0},{2,3},{3,2},{4,5},{5,4},{6,7},{7,6},{8,9},{9,8},{10,11... | collective-permute-start | bytes 1769480 | tf_op jit(solution)/shard_map/ppermute | solution.py:24
  321.4 11.7 %moments.1 = (f32[384,768]{1,0:T(8,128)}, f32[384,384]{1,0:T(8,128)}) custom-call(s32[2]{0:T(128)} %pad_add_fusion.place, bf16[1024,384]{1,0:T(8,128)(2,1)} %copy-done.18, bf16[1024,384]{1,0:T(8,128)(2,1)} %copy-done.16, bf16[512,384]{1,0:T(8,128)(2,1)} %copy-done.22, bf16[512,384]{1,0:T(8,128)(2,1)} %copy-done.23, bf16[1024,384]{1,0:T(8,128)(2,1)} %copy-done.17, ...), custom_call_target="tpu_custom_call" | custom-call | tf_op jit(solution)/shard_map/moments/pallas_call | solution.py:291
  (226 shorter events, 76.3 us)
Async XLA Ops:
  0.7 32.7 %collective-permute-start.3 = (bf16[3,768,256]{2,1,0:T(8,128)(2,1)}, bf16[3,768,256]{2,1,0:T(8,128)(2,1)}, u32[]{:S(2)}, u32[]{:S(2)}) collective-permute-start(bf16[3,768,256]{2,1,0:T(8,128)(2,1)} %bitcast.55), channel_id=1, source_target_pairs={{0,16},{16,0},{32,48},{48,32},{1,17},{17,1},{33,49},{49,33},{2,18}... | collective-permute-start | bytes 3538952 | tf_op jit(solution)/shard_map/ppermute | solution.py:24
  3.2 30.1 %collective-permute-start.4 = (bf16[3,768,256]{2,1,0:T(8,128)(2,1)}, bf16[3,768,256]{2,1,0:T(8,128)(2,1)}, u32[]{:S(2)}, u32[]{:S(2)}) collective-permute-start(bf16[3,768,256]{2,1,0:T(8,128)(2,1)} %bitcast.56), channel_id=1, source_target_pairs={{0,48},{16,32},{32,16},{48,0},{1,49},{17,33},{33,17},{49,1},{2,50}... | collective-permute-start | bytes 3538952 | tf_op jit(solution)/shard_map/ppermute | solution.py:24
  8.1 11.9 %collective-permute-start = (bf16[64,3072]{1,0:T(8,128)(2,1)S(1)}, bf16[64,3072]{1,0:T(8,128)(2,1)S(1)}, u32[]{:S(2)}, u32[]{:S(2)}) collective-permute-start(bf16[64,3072]{1,0:T(8,128)(2,1)S(1)} %constant_dynamic-update-slice_fusion), channel_id=1, source_target_pairs={{0,64},{64,0},{1,65},{65,1},{2,66},{66,2},{3,67},{67,3},{4,68},{68... | collective-permute-start | bytes 1179656 | tf_op jit(solution)/shard_map/ppermute | solution.py:24
  20.0 9.3 %collective-permute-start.1 = (bf16[64,3072]{1,0:T(8,128)(2,1)S(1)}, bf16[64,3072]{1,0:T(8,128)(2,1)S(1)}, u32[]{:S(2)}, u32[]{:S(2)}) collective-permute-start(bf16[64,3072]{1,0:T(8,128)(2,1)S(1)} %collective-permute-done), channel_id=1, source_target_pairs={{0,2},{2,0},{4,6},{6,4},{1,3},{3,1},{5,7},{7,5},{8,10},{10,8},{12,... | collective-permute-start | bytes 1179656 | tf_op jit(solution)/shard_map/ppermute | solution.py:24
  21.4 10.1 %collective-permute-start.2 = (bf16[64,3072]{1,0:T(8,128)(2,1)S(1)}, bf16[64,3072]{1,0:T(8,128)(2,1)S(1)}, u32[]{:S(2)}, u32[]{:S(2)}) collective-permute-start(bf16[64,3072]{1,0:T(8,128)(2,1)S(1)} %collective-permute-done), channel_id=1, source_target_pairs={{0,6},{2,4},{4,2},{6,0},{1,7},{3,5},{5,3},{7,1},{8,14},{10,12},{12... | collective-permute-start | bytes 1179656 | tf_op jit(solution)/shard_map/ppermute | solution.py:24
  23.3 10.0 %collective-permute-start.5 = (bf16[256,768]{1,0:T(8,128)(2,1)S(1)}, bf16[256,768]{1,0:T(8,128)(2,1)S(1)}, u32[]{:S(2)}, u32[]{:S(2)}) collective-permute-start(bf16[256,768]{1,0:T(8,128)(2,1)S(1)} %copy-done.24), channel_id=1, source_target_pairs={{0,64},{64,0},{1,65},{65,1},{2,66},{66,2},{3,67},{67,3},{4,68},{68... | collective-permute-start | bytes 1179656 | tf_op jit(solution)/shard_map/ppermute | solution.py:24
  34.5 13.1 %collective-permute-start.8 = (bf16[3,384,256]{2,1,0:T(8,128)(2,1)S(1)}, bf16[3,384,256]{2,1,0:T(8,128)(2,1)S(1)}, u32[]{:S(2)}, u32[]{:S(2)}) collective-permute-start(bf16[3,384,256]{2,1,0:T(8,128)(2,1)S(1)} %slice.185), channel_id=1, source_target_pairs={{0,48},{16,32},{32,16},{48,0},{1,49},{17,33},{33,17},{49,1},{2,50}... | collective-permute-start | bytes 1769480 | tf_op jit(solution)/shard_map/ppermute | solution.py:24
  36.3 11.7 %collective-permute-start.9 = (bf16[3,384,256]{2,1,0:T(8,128)(2,1)S(1)}, bf16[3,384,256]{2,1,0:T(8,128)(2,1)S(1)}, u32[]{:S(2)}, u32[]{:S(2)}) collective-permute-start(bf16[3,384,256]{2,1,0:T(8,128)(2,1)S(1)} %slice.186), channel_id=1, source_target_pairs={{0,16},{16,0},{32,48},{48,32},{1,17},{17,1},{33,49},{49,33},{2,18}... | collective-permute-start | bytes 1769480 | tf_op jit(solution)/shard_map/ppermute | solution.py:24
  36.7 9.7 %collective-permute-start.10 = (bf16[256,768]{1,0:T(8,128)(2,1)S(1)}, bf16[256,768]{1,0:T(8,128)(2,1)S(1)}, u32[]{:S(2)}, u32[]{:S(2)}) collective-permute-start(bf16[256,768]{1,0:T(8,128)(2,1)S(1)} %get-tuple-element.99), channel_id=1, source_target_pairs={{0,64},{64,0},{1,65},{65,1},{2,66},{66,2},{3,67},{67,3},{4,68},{68... | collective-permute-start | bytes 1179656 | tf_op jit(solution)/shard_map/ppermute | solution.py:24
  48.1 7.7 %collective-permute-start.13 = (bf16[256,3072]{1,0:T(8,128)(2,1)S(1)}, bf16[256,3072]{1,0:T(8,128)(2,1)S(1)}, u32[]{:S(2)}, u32[]{:S(2)}) collective-permute-start(bf16[256,3072]{1,0:T(8,128)(2,1)S(1)} %constant_dynamic-update-slice_fusion.4), channel_id=1, source_target_pairs={{0,1},{1,0},{2,3},{3,2},{4,5},{5,4},{6,7},{7,6},{8,9},{9,8},{10,11... | collective-permute-start | bytes 4718600 | tf_op jit(solution)/shard_map/ppermute | solution.py:24
  52.2 27.5 %collective-permute-start.11 = (bf16[768,768]{1,0:T(8,128)(2,1)S(1)}, bf16[768,768]{1,0:T(8,128)(2,1)S(1)}, u32[]{:S(2)}, u32[]{:S(2)}) collective-permute-start(bf16[768,768]{1,0:T(8,128)(2,1)S(1)} %copy-done.2), channel_id=1, source_target_pairs={{0,16},{16,0},{32,48},{48,32},{1,17},{17,1},{33,49},{49,33},{2,18}... | collective-permute-start | bytes 3538952 | tf_op jit(solution)/shard_map/ppermute | solution.py:24
  52.7 28.4 %collective-permute-start.12 = (bf16[768,768]{1,0:T(8,128)(2,1)S(1)}, bf16[768,768]{1,0:T(8,128)(2,1)S(1)}, u32[]{:S(2)}, u32[]{:S(2)}) collective-permute-start(bf16[768,768]{1,0:T(8,128)(2,1)S(1)} %copy-done.2), channel_id=1, source_target_pairs={{0,48},{16,32},{32,16},{48,0},{1,49},{17,33},{33,17},{49,1},{2,50}... | collective-permute-start | bytes 3538952 | tf_op jit(solution)/shard_map/ppermute | solution.py:24
  54.5 11.5 %collective-permute-start.14 = (bf16[256,768]{1,0:T(8,128)(2,1)S(1)}, bf16[256,768]{1,0:T(8,128)(2,1)S(1)}, u32[]{:S(2)}, u32[]{:S(2)}) collective-permute-start(bf16[256,768]{1,0:T(8,128)(2,1)S(1)} %get-tuple-element.110), channel_id=1, source_target_pairs={{0,64},{64,0},{1,65},{65,1},{2,66},{66,2},{3,67},{67,3},{4,68},{68... | collective-permute-start | bytes 1179656 | tf_op jit(solution)/shard_map/ppermute | solution.py:24
  66.0 19.0 %collective-permute-start.17 = (bf16[1024,384]{1,0:T(8,128)(2,1)S(1)}, bf16[1024,384]{1,0:T(8,128)(2,1)S(1)}, u32[]{:S(2)}, u32[]{:S(2)}) collective-permute-start(bf16[1024,384]{1,0:T(8,128)(2,1)S(1)} %get-tuple-element.111), channel_id=1, source_target_pairs={{0,64},{64,0},{1,65},{65,1},{2,66},{66,2},{3,67},{67,3},{4,68},{68... | collective-permute-start | bytes 2359304 | tf_op jit(solution)/shard_map/ppermute | solution.py:24
  82.1 14.8 %collective-permute-start.15 = (bf16[384,768]{1,0:T(8,128)(2,1)S(1)}, bf16[384,768]{1,0:T(8,128)(2,1)S(1)}, u32[]{:S(2)}, u32[]{:S(2)}) collective-permute-start(bf16[384,768]{1,0:T(8,128)(2,1)S(1)} %slice.196), channel_id=1, source_target_pairs={{0,48},{16,32},{32,16},{48,0},{1,49},{17,33},{33,17},{49,1},{2,50}... | collective-permute-start | bytes 1769480 | tf_op jit(solution)/shard_map/ppermute | solution.py:24
  83.9 13.4 %collective-permute-start.16 = (bf16[384,768]{1,0:T(8,128)(2,1)S(1)}, bf16[384,768]{1,0:T(8,128)(2,1)S(1)}, u32[]{:S(2)}, u32[]{:S(2)}) collective-permute-start(bf16[384,768]{1,0:T(8,128)(2,1)S(1)} %slice.197), channel_id=1, source_target_pairs={{0,16},{16,0},{32,48},{48,32},{1,17},{17,1},{33,49},{49,33},{2,18}... | collective-permute-start | bytes 1769480 | tf_op jit(solution)/shard_map/ppermute | solution.py:24
  87.2 21.8 %collective-permute-start.18 = (bf16[1024,256]{1,0:T(8,128)(2,1)S(1)}, bf16[1024,256]{1,0:T(8,128)(2,1)S(1)}, u32[]{:S(2)}, u32[]{:S(2)}) collective-permute-start(bf16[1024,256]{1,0:T(8,128)(2,1)S(1)} %pad_maximum_fusion.8.refs_0_), channel_id=1, source_target_pairs={{0,16},{16,0},{32,48},{48,32},{1,17},{17,1},{33,49},{49,33},{2,18}... | collective-permute-start | bytes 1572872 | tf_op jit(solution)/shard_map/ppermute | solution.py:24
  88.0 21.0 %collective-permute-start.19 = (bf16[1024,256]{1,0:T(8,128)(2,1)S(1)}, bf16[1024,256]{1,0:T(8,128)(2,1)S(1)}, u32[]{:S(2)}, u32[]{:S(2)}) collective-permute-start(bf16[1024,256]{1,0:T(8,128)(2,1)S(1)} %pad_maximum_fusion.8.refs_0_), channel_id=1, source_target_pairs={{0,48},{16,32},{32,16},{48,0},{1,49},{17,33},{33,17},{49,1},{2,50}... | collective-permute-start | bytes 1572872 | tf_op jit(solution)/shard_map/ppermute | solution.py:24
  101.9 16.2 %collective-permute-start.20 = (bf16[512,768]{1,0:T(8,128)(2,1)S(1)}, bf16[512,768]{1,0:T(8,128)(2,1)S(1)}, u32[]{:S(2)}, u32[]{:S(2)}) collective-permute-start(bf16[512,768]{1,0:T(8,128)(2,1)S(1)} %project_mlp.2), channel_id=1, source_target_pairs={{0,64},{64,0},{1,65},{65,1},{2,66},{66,2},{3,67},{67,3},{4,68},{68... | collective-permute-start | bytes 2359304 | tf_op jit(solution)/shard_map/ppermute | solution.py:24
  109.0 9.1 %collective-permute-start.21 = (bf16[512,256]{1,0:T(8,128)(2,1)S(1)}, bf16[512,256]{1,0:T(8,128)(2,1)S(1)}, u32[]{:S(2)}, u32[]{:S(2)}) collective-permute-start(bf16[512,256]{1,0:T(8,128)(2,1)S(1)} %slice.201), channel_id=1, source_target_pairs={{0,48},{16,32},{32,16},{48,0},{1,49},{17,33},{33,17},{49,1},{2,50}... | collective-permute-start | bytes 786440 | tf_op jit(solution)/shard_map/ppermute | solution.py:24
  110.5 7.7 %collective-permute-start.22 = (bf16[512,256]{1,0:T(8,128)(2,1)S(1)}, bf16[512,256]{1,0:T(8,128)(2,1)S(1)}, u32[]{:S(2)}, u32[]{:S(2)}) collective-permute-start(bf16[512,256]{1,0:T(8,128)(2,1)S(1)} %slice.202), channel_id=1, source_target_pairs={{0,16},{16,0},{32,48},{48,32},{1,17},{17,1},{33,49},{49,33},{2,18}... | collective-permute-start | bytes 786440 | tf_op jit(solution)/shard_map/ppermute | solution.py:24
  122.9 13.8 %collective-permute-start.23 = (bf16[512,768]{1,0:T(8,128)(2,1)S(1)}, bf16[512,768]{1,0:T(8,128)(2,1)S(1)}, u32[]{:S(2)}, u32[]{:S(2)}) collective-permute-start(bf16[512,768]{1,0:T(8,128)(2,1)S(1)} %fusion.2.refs_4_), channel_id=1, source_target_pairs={{0,16},{16,0},{32,48},{48,32},{1,17},{17,1},{33,49},{49,33},{2,18}... | collective-permute-start | bytes 2359304 | tf_op jit(solution)/shard_map/ppermute | solution.py:24
  123.8 15.2 %collective-permute-start.24 = (bf16[512,768]{1,0:T(8,128)(2,1)S(1)}, bf16[512,768]{1,0:T(8,128)(2,1)S(1)}, u32[]{:S(2)}, u32[]{:S(2)}) collective-permute-start(bf16[512,768]{1,0:T(8,128)(2,1)S(1)} %fusion.2.refs_4_), channel_id=1, source_target_pairs={{0,48},{16,32},{32,16},{48,0},{1,49},{17,33},{33,17},{49,1},{2,50}... | collective-permute-start | bytes 2359304 | tf_op jit(solution)/shard_map/ppermute | solution.py:24
  125.1 9.4 %collective-permute-start.25 = (bf16[256,768]{1,0:T(8,128)(2,1)S(1)}, bf16[256,768]{1,0:T(8,128)(2,1)S(1)}, u32[]{:S(2)}, u32[]{:S(2)}) collective-permute-start(bf16[256,768]{1,0:T(8,128)(2,1)S(1)} %get-tuple-element.136), channel_id=1, source_target_pairs={{0,64},{64,0},{1,65},{65,1},{2,66},{66,2},{3,67},{67,3},{4,68},{68... | collective-permute-start | bytes 1179656 | tf_op jit(solution)/shard_map/ppermute | solution.py:24
  140.5 19.3 %collective-permute-start.30 = (bf16[256,768]{1,0:T(8,128)(2,1)S(1)}, bf16[256,768]{1,0:T(8,128)(2,1)}, u32[]{:S(2)}, u32[]{:S(2)}) collective-permute-start(bf16[256,768]{1,0:T(8,128)(2,1)S(1)} %slice.208), channel_id=1, source_target_pairs={{0,48},{16,32},{32,16},{48,0},{1,49},{17,33},{33,17},{49,1},{2,50}... | collective-permute-start | bytes 1179656 | tf_op jit(solution)/shard_map/ppermute | solution.py:24
  142.2 17.6 %collective-permute-start.31 = (bf16[256,768]{1,0:T(8,128)(2,1)S(1)}, bf16[256,768]{1,0:T(8,128)(2,1)}, u32[]{:S(2)}, u32[]{:S(2)}) collective-permute-start(bf16[256,768]{1,0:T(8,128)(2,1)S(1)} %slice.209), channel_id=1, source_target_pairs={{0,16},{16,0},{32,48},{48,32},{1,17},{17,1},{33,49},{49,33},{2,18}... | collective-permute-start | bytes 1179656 | tf_op jit(solution)/shard_map/ppermute | solution.py:24
  144.6 13.6 %collective-permute-start.28 = (bf16[512,256]{1,0:T(8,128)(2,1)S(1)}, bf16[512,256]{1,0:T(8,128)(2,1)S(1)}, u32[]{:S(2)}, u32[]{:S(2)}) collective-permute-start(bf16[512,256]{1,0:T(8,128)(2,1)S(1)} %pad_maximum_fusion.10.refs_0_), channel_id=1, source_target_pairs={{0,32},{16,48},{32,0},{48,16},{1,33},{17,49},{33,1},{49,17},{2,34}... | collective-permute-start | bytes 786440 | tf_op jit(solution)/shard_map/ppermute | solution.py:24
  147.4 12.4 %collective-permute-start.29 = (bf16[512,256]{1,0:T(8,128)(2,1)S(1)}, bf16[512,256]{1,0:T(8,128)(2,1)S(1)}, u32[]{:S(2)}, u32[]{:S(2)}) collective-permute-start(bf16[512,256]{1,0:T(8,128)(2,1)S(1)} %pad_maximum_fusion.10.refs_0_), channel_id=1, source_target_pairs={{0,48},{16,32},{32,16},{48,0},{1,49},{17,33},{33,17},{49,1},{2,50}... | collective-permute-start | bytes 786440 | tf_op jit(solution)/shard_map/ppermute | solution.py:24
  168.5 15.3 %collective-permute-start.32 = (bf16[2,4,256,768]{3,2,1,0:T(8,128)(2,1)}, bf16[2,4,256,768]{3,2,1,0:T(8,128)(2,1)}, u32[]{:S(2)}, u32[]{:S(2)}) collective-permute-start(bf16[2,4,256,768]{3,2,1,0:T(8,128)(2,1)} %project_out.3), channel_id=1, source_target_pairs={{0,1},{1,0},{2,3},{3,2},{4,5},{5,4},{6,7},{7,6},{8,9},{9,8},{10,11... | collective-permute-start | bytes 9437192 | tf_op jit(solution)/shard_map/ppermute | solution.py:24
  187.4 19.3 %collective-permute-start.33 = (bf16[4,128,768]{2,1,0:T(8,128)(2,1)S(1)}, bf16[4,128,768]{2,1,0:T(8,128)(2,1)S(1)}, u32[]{:S(2)}, u32[]{:S(2)}) collective-permute-start(bf16[4,128,768]{2,1,0:T(8,128)(2,1)S(1)} %slice.350), channel_id=1, source_target_pairs={{0,2},{2,0},{4,6},{6,4},{1,3},{3,1},{5,7},{7,5},{8,10},{10,8},{12,... | collective-permute-start | bytes 2359304 | tf_op jit(solution)/shard_map/ppermute | solution.py:24
  188.2 20.1 %collective-permute-start.34 = (bf16[4,128,768]{2,1,0:T(8,128)(2,1)S(1)}, bf16[4,128,768]{2,1,0:T(8,128)(2,1)S(1)}, u32[]{:S(2)}, u32[]{:S(2)}) collective-permute-start(bf16[4,128,768]{2,1,0:T(8,128)(2,1)S(1)} %slice.349), channel_id=1, source_target_pairs={{0,6},{2,4},{4,2},{6,0},{1,7},{3,5},{5,3},{7,1},{8,14},{10,12},{12... | collective-permute-start | bytes 2359304 | tf_op jit(solution)/shard_map/ppermute | solution.py:24
  208.4 10.8 %collective-permute-start.36 = (bf16[4,64,768]{2,1,0:T(8,128)(2,1)S(1)}, bf16[4,64,768]{2,1,0:T(8,128)(2,1)S(1)}, u32[]{:S(2)}, u32[]{:S(2)}) collective-permute-start(bf16[4,64,768]{2,1,0:T(8,128)(2,1)S(1)} %fusion.13), channel_id=1, source_target_pairs={{0,6},{2,4},{4,2},{6,0},{1,7},{3,5},{5,3},{7,1},{8,14},{10,12},{12... | collective-permute-start | bytes 1179656 | tf_op jit(solution)/shard_map/ppermute | solution.py:24
  210.5 9.3 %collective-permute-start.35 = (bf16[4,64,768]{2,1,0:T(8,128)(2,1)S(1)}, bf16[4,64,768]{2,1,0:T(8,128)(2,1)S(1)}, u32[]{:S(2)}, u32[]{:S(2)}) collective-permute-start(bf16[4,64,768]{2,1,0:T(8,128)(2,1)S(1)} %fusion.15), channel_id=1, source_target_pairs={{0,2},{2,0},{4,6},{6,4},{1,3},{3,1},{5,7},{7,5},{8,10},{10,8},{12,... | collective-permute-start | bytes 1179656 | tf_op jit(solution)/shard_map/ppermute | solution.py:24
  220.0 8.4 %collective-permute-start.37 = (bf16[4,32,1536]{2,1,0:T(8,128)(2,1)S(1)}, bf16[4,32,1536]{2,1,0:T(8,128)(2,1)S(1)}, u32[]{:S(2)}, u32[]{:S(2)}) collective-permute-start(bf16[4,32,1536]{2,1,0:T(8,128)(2,1)S(1)} %fusion.12), channel_id=1, source_target_pairs={{0,8},{8,0},{1,9},{9,1},{2,10},{10,2},{3,11},{11,3},{4,12},{12,4},... | collective-permute-start | bytes 1179656 | tf_op jit(solution)/shard_map/ppermute | solution.py:24
  241.6 15.0 %collective-permute-start.41 = (bf16[256,1152]{1,0:T(8,128)(2,1)S(1)}, bf16[256,1152]{1,0:T(8,128)(2,1)S(1)}, u32[]{:S(2)}, u32[]{:S(2)}) collective-permute-start(bf16[256,1152]{1,0:T(8,128)(2,1)S(1)} %pad_maximum_fusion.7), channel_id=1, source_target_pairs={{0,8},{8,0},{1,9},{9,1},{2,10},{10,2},{3,11},{11,3},{4,12},{12,4},... | collective-permute-start | bytes 1769480 | tf_op jit(solution)/shard_map/ppermute | solution.py:24
  242.7 14.0 %collective-permute-start.40 = (bf16[512,384]{1,0:T(8,128)(2,1)S(1)}, bf16[512,384]{1,0:T(8,128)(2,1)S(1)}, u32[]{:S(2)}, u32[]{:S(2)}) collective-permute-start(bf16[512,384]{1,0:T(8,128)(2,1)S(1)} %pad_maximum_fusion.9), channel_id=1, source_target_pairs={{0,0},{2,16},{4,32},{6,48},{8,64},{10,80},{12,96},{14,112},{16,2},... | collective-permute-start | bytes 1179656 | tf_op jit(solution)/shard_map/ppermute | solution.py:448
  256.6 14.1 %collective-permute-start.42 = (bf16[512,384]{1,0:T(8,128)(2,1)S(1)}, bf16[512,384]{1,0:T(8,128)(2,1)S(1)}, u32[]{:S(2)}, u32[]{:S(2)}) collective-permute-start(bf16[512,384]{1,0:T(8,128)(2,1)S(1)} %collective-permute-done.40), channel_id=1, source_target_pairs={{0,64},{64,0},{1,65},{65,1},{2,66},{66,2},{3,67},{67,3},{4,68},{68... | collective-permute-start | bytes 1179656 | tf_op jit(solution)/shard_map/ppermute | solution.py:24
  259.0 30.4 %collective-permute-start.45 = (bf16[512,1152]{1,0:T(8,128)(2,1)}, bf16[512,1152]{1,0:T(8,128)(2,1)}, u32[]{:S(2)}, u32[]{:S(2)}) collective-permute-start(bf16[512,1152]{1,0:T(8,128)(2,1)} %pad_maximum_fusion.1.refs_5_), channel_id=1, source_target_pairs={{0,2},{2,0},{4,6},{6,4},{1,3},{3,1},{5,7},{7,5},{8,10},{10,8},{12,... | collective-permute-start | bytes 3538952 | tf_op jit(solution)/shard_map/ppermute | solution.py:24
  265.4 30.5 %collective-permute-start.46 = (bf16[512,1152]{1,0:T(8,128)(2,1)}, bf16[512,1152]{1,0:T(8,128)(2,1)}, u32[]{:S(2)}, u32[]{:S(2)}) collective-permute-start(bf16[512,1152]{1,0:T(8,128)(2,1)} %pad_maximum_fusion.1.refs_5_), channel_id=1, source_target_pairs={{0,6},{2,4},{4,2},{6,0},{1,7},{3,5},{5,3},{7,1},{8,14},{10,12},{12... | collective-permute-start | bytes 3538952 | tf_op jit(solution)/shard_map/ppermute | solution.py:24
  270.8 25.0 %collective-permute-start.43 = (bf16[1024,384]{1,0:T(8,128)(2,1)S(1)}, bf16[1024,384]{1,0:T(8,128)(2,1)S(1)}, u32[]{:S(2)}, u32[]{:S(2)}) collective-permute-start(bf16[1024,384]{1,0:T(8,128)(2,1)S(1)} %constant_dynamic-update-slice_fusion.9.refs_0_), channel_id=1, source_target_pairs={{0,16},{16,0},{32,48},{48,32},{1,17},{17,1},{33,49},{49,33},{2,18}... | collective-permute-start | bytes 2359304 | tf_op jit(solution)/shard_map/ppermute | solution.py:24
  274.1 22.4 %collective-permute-start.44 = (bf16[1024,384]{1,0:T(8,128)(2,1)S(1)}, bf16[1024,384]{1,0:T(8,128)(2,1)S(1)}, u32[]{:S(2)}, u32[]{:S(2)}) collective-permute-start(bf16[1024,384]{1,0:T(8,128)(2,1)S(1)} %constant_dynamic-update-slice_fusion.9.refs_0_), channel_id=1, source_target_pairs={{0,48},{16,32},{32,16},{48,0},{1,49},{17,33},{33,17},{49,1},{2,50}... | collective-permute-start | bytes 2359304 | tf_op jit(solution)/shard_map/ppermute | solution.py:24
  296.7 9.8 %collective-permute-start.47 = (bf16[512,384]{1,0:T(8,128)(2,1)S(1)}, bf16[512,384]{1,0:T(8,128)(2,1)S(1)}, u32[]{:S(2)}, u32[]{:S(2)}) collective-permute-start(bf16[512,384]{1,0:T(8,128)(2,1)S(1)} %slice.237), channel_id=1, source_target_pairs={{0,48},{16,32},{32,16},{48,0},{1,49},{17,33},{33,17},{49,1},{2,50}... | collective-permute-start | bytes 1179656 | tf_op jit(solution)/shard_map/ppermute | solution.py:24
  299.0 10.5 %collective-permute-start.48 = (bf16[512,384]{1,0:T(8,128)(2,1)S(1)}, bf16[512,384]{1,0:T(8,128)(2,1)S(1)}, u32[]{:S(2)}, u32[]{:S(2)}) collective-permute-start(bf16[512,384]{1,0:T(8,128)(2,1)S(1)} %slice.238), channel_id=1, source_target_pairs={{0,16},{16,0},{32,48},{48,32},{1,17},{17,1},{33,49},{49,33},{2,18}... | collective-permute-start | bytes 1179656 | tf_op jit(solution)/shard_map/ppermute | solution.py:24
  300.3 13.3 %collective-permute-start.49 = (bf16[256,1152]{1,0:T(8,128)(2,1)S(1)}, bf16[256,1152]{1,0:T(8,128)(2,1)}, u32[]{:S(2)}, u32[]{:S(2)}) collective-permute-start(bf16[256,1152]{1,0:T(8,128)(2,1)S(1)} %slice.239), channel_id=1, source_target_pairs={{0,6},{2,4},{4,2},{6,0},{1,7},{3,5},{5,3},{7,1},{8,14},{10,12},{12... | collective-permute-start | bytes 1769480 | tf_op jit(solution)/shard_map/ppermute | solution.py:24
  302.6 12.2 %collective-permute-start.50 = (bf16[256,1152]{1,0:T(8,128)(2,1)S(1)}, bf16[256,1152]{1,0:T(8,128)(2,1)}, u32[]{:S(2)}, u32[]{:S(2)}) collective-permute-start(bf16[256,1152]{1,0:T(8,128)(2,1)S(1)} %slice.240), channel_id=1, source_target_pairs={{0,2},{2,0},{4,6},{6,4},{1,3},{3,1},{5,7},{7,5},{8,10},{10,8},{12,... | collective-permute-start | bytes 1769480 | tf_op jit(solution)/shard_map/ppermute | solution.py:24
  302.7 16.4 %collective-permute-start.51 = (bf16[512,1152]{1,0:T(8,128)(2,1)}, bf16[512,1152]{1,0:T(8,128)(2,1)}, u32[]{:S(2)}, u32[]{:S(2)}) collective-permute-start(bf16[512,1152]{1,0:T(8,128)(2,1)} %pad_maximum_fusion.1.refs_5_), channel_id=1, source_target_pairs={{0,1},{1,0},{2,3},{3,2},{4,5},{5,4},{6,7},{7,6},{8,9},{9,8},{10,11... | collective-permute-start | bytes 3538952 | tf_op jit(solution)/shard_map/ppermute | solution.py:24
  306.6 14.8 %collective-permute-start.52 = (bf16[512,1152]{1,0:T(8,128)(2,1)}, bf16[512,1152]{1,0:T(8,128)(2,1)}, u32[]{:S(2)}, u32[]{:S(2)}) collective-permute-start(bf16[512,1152]{1,0:T(8,128)(2,1)} %collective-permute-done.45.refs_6_), channel_id=1, source_target_pairs={{0,1},{1,0},{2,3},{3,2},{4,5},{5,4},{6,7},{7,6},{8,9},{9,8},{10,11... | collective-permute-start | bytes 3538952 | tf_op jit(solution)/shard_map/ppermute | solution.py:24
  309.6 11.8 %collective-permute-start.55 = (bf16[512,1152]{1,0:T(8,128)(2,1)}, bf16[512,1152]{1,0:T(8,128)(2,1)}, u32[]{:S(2)}, u32[]{:S(2)}) collective-permute-start(bf16[512,1152]{1,0:T(8,128)(2,1)} %collective-permute-done.46.refs_9_), channel_id=1, source_target_pairs={{0,1},{1,0},{2,3},{3,2},{4,5},{5,4},{6,7},{7,6},{8,9},{9,8},{10,11... | collective-permute-start | bytes 3538952 | tf_op jit(solution)/shard_map/ppermute | solution.py:24
  (38 other events, 463.0 us)
where the time goes:
time: 334 us; the launch traced here: 333 us
  waiting for transfers between devices  122 us (37%)
  starting transfers between devices  101 us (30%)
  Pallas kernels  60.7 us (18%)
  local copies, waits for them, and re-layouts  17.2 us (5%)
  other arithmetic  15.5 us (5%)
  blocking collectives  14.9 us (4%)
    ppermute x55, waiting for transfers between devices, swap(): return lax.ppermute(x, axis, [(i, i ^ mask) for i in range(size)])  122 us
    ppermute x55, starting transfers between devices, swap(): return lax.ppermute(x, axis, [(i, i ^ mask) for i in range(size)])  100 us
    pallas_call x2, Pallas kernels, project_out(): pl.pallas_call(output_kernel, grid_spec=pltpu.PrefetchScalarGridSpec(num_...  16 us
    all_to_all x1, blocking collectives, on_device(): lax.all_to_all(spread_rows, ('xh', 'z'), split_axis=0, concat_axis=0, til...  14.9 us
    pallas_call x1, Pallas kernels, moments(): pl.pallas_call(kernel, grid_spec=pltpu.PrefetchScalarGridSpec(num_scalar_...  11.7 us
    pallas_call x2, Pallas kernels, project_mlp(): pl.pallas_call(mlp_kernel, grid=(3,), in_specs=[pl.BlockSpec(x.shape, lam...  10.1 us
    pallas_call x1, Pallas kernels, attend(): pl.pallas_call(attend_kernel, grid=(rows // step,), in_specs=[pl.BlockSpe...  7.98 us
    pallas_call x2, Pallas kernels, norm_rows(): pl.pallas_call(norm_kernel, grid_spec=pltpu.PrefetchScalarGridSpec(num_sc...  7.6 us
  transfers between devices with their start and end apart: 56, of which 36 were waited for; matrix products, arithmetic and copies ran while one was open for 4% of the time, Pallas kernels for 12%

commit v1 on v0

--- a/solution.py
+++ b/solution.py
@@ -426,14 +426,19 @@
     par_got, own_got, own_spread = lax.optimization_barrier((par_got, own_got, own_spread))
     base = own_spread[:, :, :block].reshape(8 * piece, block)
     own_goals = own_spread[:, :, block:].reshape(8 * piece, target_block)
-    par_next = swap((chunks(par, 3, 1) + chunks(par_got, 1, 1).astype(F32)).astype(BF), "y", 3).astype(F32)
-    own_next = swap((chunks(own, 1, 1) + chunks(own_got, 0, 1).astype(F32)).astype(BF), "y", 1).astype(F32)
-    par_sum = chunks(par, 0, 1) + chunks(par_got, 0, 1).astype(F32) + par_next
-    own_sum = chunks(own, 0, 1) + chunks(own_got, 1, 1).astype(F32) + own_next
-    sums = jnp.concatenate([own_sum, par_sum], axis=2)
-    sums = sums[:, :piece] + swap(sums[:, piece:].astype(BF), "xl").astype(F32)
-    theirs = swap(sums[:, :, block:].astype(BF), "xh").astype(F32)
-    sum_own = in_order([sums[i, :, :block] for i in range(4)], z)
+    far_goals = swap(own_goals, "xl")
+    par_next = swap((chunks(par, 3, 1) + chunks(par_got, 1, 1).astype(F32)).astype(BF), "y", 3)
+    own_next = swap((chunks(own, 1, 1) + chunks(own_got, 0, 1).astype(F32)).astype(BF), "y", 1)
+    par_next, own_next, far_goals = lax.optimization_barrier((par_next, own_next, far_goals))
+    par_sum = chunks(par, 0, 1) + chunks(par_got, 0, 1).astype(F32) + par_next.astype(F32)
+    own_sum = chunks(own, 0, 1) + chunks(own_got, 1, 1).astype(F32) + own_next.astype(F32)
+    par_sum = par_sum.astype(BF)
+    got_own = swap(own_sum[:, piece:].astype(BF), "xl")
+    got_near = swap(par_sum[:, :piece], "xh")
+    got_far = lax.ppermute(par_sum[:, piece:], ("xh", "xl"), [(i, i ^ 3) for i in range(4)])
+    ours = own_sum[:, :piece] + got_own.astype(F32)
+    theirs = got_near.astype(F32) + got_far.astype(F32)
+    sum_own = in_order([ours[i] for i in range(4)], z)
     sum_theirs = in_order([theirs[i] for i in range(4)], z)
     total = both(xh, sum_own, sum_theirs)
     bias = dyn(out_bias, (xh * 4 + z) * block, block, 0)
@@ -443,21 +448,22 @@
 
     stay, leave = dyn(out_piece, c * narrow, narrow, 1), dyn(out_piece, (1 - c) * narrow, narrow, 1)
     pair = jnp.concatenate([stay, swap(leave, "c")])
-    beside = jnp.concatenate([out_piece, own_goals], axis=1)
-    over_xl = swap(beside, "xl")
+    over_xl = swap(out_piece, "xl")
     pair = lax.ppermute(
         pair,
         ("xh", "z", "xl", "y"),
         [(a * 8 + b, b * 8 + a) for a in range(8) for b in range(8)],
     )
     pair, over_xl = lax.optimization_barrier((pair, over_xl))
-    over_xl_pair = jnp.concatenate([beside, over_xl])
+    beside = jnp.concatenate([out_piece, own_goals], axis=1)
+    over_xl_pair = jnp.concatenate([beside, jnp.concatenate([over_xl, far_goals], axis=1)])
     part_one, part_three = near(over_xl_pair, "y")
     pair = jnp.concatenate([pair, swap(pair, "xh")])
     col_one, col_three = near(pair, "z")
-    col_one, col_three, part_one, part_three = lax.optimization_barrier((col_one, col_three, part_one, part_three))
+    low_rows, high_rows = part_one[: 8 * piece], part_three[8 * piece :]
+    part_low, part_high = swap(low_rows, "y", 3), swap(high_rows, "y", 1)
+    col_one, col_three, *_ = lax.optimization_barrier((col_one, col_three, low_rows, high_rows))
     col_low, col_high = opposite(col_one, col_three, "z")
-    part_low, part_high = opposite(part_one, part_three, "y")
     col_low, col_high, part_low, part_high = lax.optimization_barrier((col_low, col_high, part_low, part_high))
     columns = [pair, col_one, col_low, col_high, col_three]
     parts = [over_xl_pair, part_one, part_low, part_high, part_three]

time: 334 us -> 329 us (0.985)
  waiting for transfers between devices: 122 us -> 112 us
  other arithmetic: 15.5 us -> 19.7 us
    ppermute x55 -> x56, waiting for transfers between devices: 122 us -> 106 us  [swap(): return lax.ppermute(x, axis, [(i, i ^ mask) for i in range(size)])]
    ppermute x0 -> x1, waiting for transfers between devices: none -> 5.95 us  [on_device(): lax.ppermute(par_sum[:, piece:], ('xh', 'xl'), [(i, i ^ 3) for i in range...]
    ppermute x55 -> x56, starting transfers between devices: 100 us -> 101 us  [swap(): return lax.ppermute(x, axis, [(i, i ^ mask) for i in range(size)])]
    unnamed x75 -> x83, local copies, waits for them, and re-layouts: 7.06 us -> 6.9 us
  transfers between devices with their start and end apart: 56 -> 58, of which waited for: 36 -> 36; matrix products, arithmetic and copies ran while one was open for 4% -> 5% of each run, Pallas kernels for 12% -> 13%
where the time goes in v1:
time: 329 us; the launch traced here: 328 us
  waiting for transfers between devices  112 us (34%)
  starting transfers between devices  103 us (31%)
  Pallas kernels  60.7 us (18%)
  other arithmetic  19.7 us (6%)
  local copies, waits for them, and re-layouts  16.2 us (5%)
  blocking collectives  14.8 us (4%)
    ppermute x56, waiting for transfers between devices, swap(): return lax.ppermute(x, axis, [(i, i ^ mask) for i in range(size)])  106 us
    ppermute x56, starting transfers between devices, swap(): return lax.ppermute(x, axis, [(i, i ^ mask) for i in range(size)])  101 us
    pallas_call x2, Pallas kernels, project_out(): pl.pallas_call(output_kernel, grid_spec=pltpu.PrefetchScalarGridSpec(num_...  16 us
    all_to_all x1, blocking collectives, on_device(): lax.all_to_all(spread_rows, ('xh', 'z'), split_axis=0, concat_axis=0, til...  14.8 us
    pallas_call x1, Pallas kernels, moments(): pl.pallas_call(kernel, grid_spec=pltpu.PrefetchScalarGridSpec(num_scalar_...  11.7 us
    pallas_call x2, Pallas kernels, project_mlp(): pl.pallas_call(mlp_kernel, grid=(3,), in_specs=[pl.BlockSpec(x.shape, lam...  10 us
    pallas_call x1, Pallas kernels, attend(): pl.pallas_call(attend_kernel, grid=(rows // step,), in_specs=[pl.BlockSpe...  7.98 us
    pallas_call x2, Pallas kernels, norm_rows(): pl.pallas_call(norm_kernel, grid_spec=pltpu.PrefetchScalarGridSpec(num_sc...  7.6 us
  transfers between devices with their start and end apart: 58, of which 36 were waited for; matrix products, arithmetic and copies ran while one was open for 5% of the time, Pallas kernels for 13%

profile of v1, /device:TPU:1, one launch (start us, length us, event | category | flops | bytes accessed | tf_op | source)
XLA Modules:
  0.0 328.2 jit_solution(10827494475321788737)
XLA Ops:
  0.7 2.5 collective-permute-start.3
  3.2 2.2 collective-permute-start.4
  8.1 2.8 collective-permute-start
  10.9 2.8 copy-done.1
  13.7 6.3 %norm_rows.3 = (bf16[512,768]{1,0:T(8,128)(2,1)S(1)}, bf16[512,768]{1,0:T(8,128)(2,1)S(1)}, bf16[512,768]{1,0:T(8,128)(2,1)S(1)}, bf16[512,768]{1,0:T(8,128)(2,1)S(1)}) custom-call(s32[3]{0:T(128)S(1)} %get-tuple-element.212.place, bf16[512,6144]{1,0:T(8,128)(2,1)S(1)} %copy-done.1, f32[1,6144]{1,0:T(1,128)S(1)} %bitcast.59), custom_call_target="tpu_custom_call" | custom-call | tf_op jit(solution)/shard_map/norm_rows/pallas_call | solution.py:83
  25.2 4.1 %collective-permute-done.1 = bf16[64,3072]{1,0:T(8,128)(2,1)S(1)} collective-permute-done((bf16[64,3072]{1,0:T(8,128)(2,1)S(1)}, bf16[64,3072]{1,0:T(8,128)(2,1)S(1)}, u32[]{:S(2)}, u32[]{:S(2)}) %collective-permute-start.1) | collective-permute-done | bytes 393248 | tf_op jit(solution)/shard_map/ppermute | solution.py:24
  29.3 2.2 collective-permute-done.2
  36.7 2.0 collective-permute-start.10
  38.8 2.8 collective-permute-start.6
  41.7 3.2 collective-permute-done.6
  48.1 4.2 %collective-permute-start.13 = (bf16[256,3072]{1,0:T(8,128)(2,1)S(1)}, bf16[256,3072]{1,0:T(8,128)(2,1)S(1)}, u32[]{:S(2)}, u32[]{:S(2)}) collective-permute-start(bf16[256,3072]{1,0:T(8,128)(2,1)S(1)} %constant_dynamic-update-slice_fusion.4), channel_id=1, source_target_pairs={{0,1},{1,0},{2,3},{3,2},{4,5},{5,4},{6,7},{7,6},{8,9},{9,8},{10,11... | collective-permute-start | bytes 4718600 | tf_op jit(solution)/shard_map/ppermute | solution.py:24
  57.3 7.4 %project_qkv.1 = (bf16[1024,384]{1,0:T(8,128)(2,1)S(1)}, f32[1024,384]{1,0:T(8,128)S(1)}) custom-call(s32[1]{0:T(128)} %bitcast.2.place, bf16[512,768]{1,0:T(8,128)(2,1)S(1)} %get-tuple-element.123.refs_0_, bf16[512,768]{1,0:T(8,128)(2,1)S(1)} %get-tuple-element.124.refs_1_, bf16[512,768]{1,0:T(8,128)(2,1)S(1)} %get-tuple-element.125.refs_2_, ...), custom_call_target="tpu_custom_call" | custom-call | tf_op jit(solution)/shard_map/project_qkv/pallas_call | solution.py:168
  67.2 12.6 %collective-permute-done.11.refs_5_ = bf16[768,768]{1,0:T(8,128)(2,1)S(1)} collective-permute-done((bf16[768,768]{1,0:T(8,128)(2,1)S(1)}, bf16[768,768]{1,0:T(8,128)(2,1)S(1)}, u32[]{:S(2)}, u32[]{:S(2)}) %collective-permute-start.11) | collective-permute-done | bytes 1179680 | tf_op jit(solution)/shard_map/ppermute | solution.py:24
  88.6 8.5 %collective-permute-done.15.refs_6_ = bf16[384,768]{1,0:T(8,128)(2,1)S(1)} collective-permute-done((bf16[384,768]{1,0:T(8,128)(2,1)S(1)}, bf16[384,768]{1,0:T(8,128)(2,1)S(1)}, u32[]{:S(2)}, u32[]{:S(2)}) %collective-permute-start.15) | collective-permute-done | bytes 589856 | tf_op jit(solution)/shard_map/ppermute | solution.py:24
  97.4 4.6 %project_mlp.2 = bf16[512,768]{1,0:T(8,128)(2,1)S(1)} custom-call(bf16[512,768]{1,0:T(8,128)(2,1)S(1)} %pad_maximum_fusion.1.refs_4_.refs_0_, bf16[512,768]{1,0:T(8,128)(2,1)S(1)} %pad_maximum_fusion.2.refs_5_.refs_1_, bf16[512,768]{1,0:T(8,128)(2,1)S(1)} %pad_maximum_fusion.3.refs_6_.refs_2_, bf16[512,768]{1,0:T(8,128)(2,1)S(1)} %pad_maximum_fusion.4.refs_7_.refs_3_, ...), custom_call_target="tpu_custom_call" | custom-call | tf_op jit(solution)/shard_map/project_mlp/pallas_call | solution.py:194
  103.7 5.4 %project_mlp.3 = f32[512,768]{1,0:T(8,128)} custom-call(bf16[512,768]{1,0:T(8,128)(2,1)S(1)} %get-tuple-element.123.refs_0_, bf16[512,768]{1,0:T(8,128)(2,1)S(1)} %get-tuple-element.124.refs_1_, bf16[512,768]{1,0:T(8,128)(2,1)S(1)} %get-tuple-element.125.refs_2_, bf16[512,768]{1,0:T(8,128)(2,1)S(1)} %get-tuple-element.126.refs_3_, ...), custom_call_target="tpu_custom_call" | custom-call | tf_op jit(solution)/shard_map/project_mlp/pallas_call | solution.py:194
  110.7 7.6 %collective-permute-done.20 = bf16[512,768]{1,0:T(8,128)(2,1)S(1)} collective-permute-done((bf16[512,768]{1,0:T(8,128)(2,1)S(1)}, bf16[512,768]{1,0:T(8,128)(2,1)S(1)}, u32[]{:S(2)}, u32[]{:S(2)}) %collective-permute-start.20) | collective-permute-done | bytes 786464 | tf_op jit(solution)/shard_map/ppermute | solution.py:24
  118.3 4.7 %fusion.2.refs_4_ = bf16[512,768]{1,0:T(8,128)(2,1)S(1)} fusion(f32[512,768]{1,0:T(8,128)} %project_mlp.3, bf16[512,768]{1,0:T(8,128)(2,1)S(1)} %collective-permute-done.20, f32[768]{0:T(1024)S(1)} %copy-done.31), kind=kLoop, calls=%fused_computation.6 | loop fusion | flops 26738688 | bytes 3148800 | tf_op jit(solution)/shard_map/convert_element_type | solution.py:390
  126.7 8.0 %attend.1 = bf16[1024,128]{1,0:T(8,128)(2,1)S(1)} custom-call(bf16[1024,128]{1,0:T(8,128)(2,1)S(1)} %get-tuple-element.133.q_ref, bf16[1024,256]{1,0:T(8,128)(2,1)S(1)} %pad_maximum_fusion.5.refs_0_, bf16[1024,256]{1,0:T(8,128)(2,1)S(1)} %collective-permute-done.18.refs_1_, bf16[1024,256]{1,0:T(8,128)(2,1)S(1)} %collective-permute-done.19.refs_2_, ...), custom_call_target="tpu_custom_call" | custom-call | tf_op jit(solution)/shard_map/attend/pallas_call | solution.py:121
  134.7 2.1 collective-permute-done.23.refs_5_
  136.9 2.3 collective-permute-done.24.refs_7_
  142.4 2.2 collective-permute-done.26
  144.8 2.8 collective-permute-start.28
  148.7 1.9 pad_maximum_fusion.refs_8_
  152.3 6.1 %collective-permute-done.28.refs_2_ = bf16[512,256]{1,0:T(8,128)(2,1)S(1)} collective-permute-done((bf16[512,256]{1,0:T(8,128)(2,1)S(1)}, bf16[512,256]{1,0:T(8,128)(2,1)S(1)}, u32[]{:S(2)}, u32[]{:S(2)}) %collective-permute-start.28) | collective-permute-done | bytes 262176 | tf_op jit(solution)/shard_map/ppermute | solution.py:24
  160.7 8.0 %project_out.3 = bf16[2,4,256,768]{3,2,1,0:T(8,128)(2,1)} custom-call(s32[1]{0:T(128)} %bitcast.2.place, bf16[512,256]{1,0:T(8,128)(2,1)} %copy-done.15, bf16[512,256]{1,0:T(8,128)(2,1)} %copy-done.20, bf16[512,256]{1,0:T(8,128)(2,1)} %copy-done.21, bf16[512,256]{1,0:T(8,128)(2,1)} %copy-done.22, bf16[512,768]{1,0:T(8,128)(2,1)} %copy-done.10, ...), custom_call_target="tpu_custom_call" | custom-call | tf_op jit(solution)/shard_map/project_out/pallas_call | solution.py:226
  168.6 7.2 %collective-permute-start.32 = (bf16[2,4,256,768]{3,2,1,0:T(8,128)(2,1)}, bf16[2,4,256,768]{3,2,1,0:T(8,128)(2,1)}, u32[]{:S(2)}, u32[]{:S(2)}) collective-permute-start(bf16[2,4,256,768]{3,2,1,0:T(8,128)(2,1)} %project_out.3), channel_id=1, source_target_pairs={{0,1},{1,0},{2,3},{3,2},{4,5},{5,4},{6,7},{7,6},{8,9},{9,8},{10,11... | collective-permute-start | bytes 9437192 | tf_op jit(solution)/shard_map/ppermute | solution.py:24
  175.9 8.0 %project_out.2 = bf16[2,4,256,768]{3,2,1,0:T(8,128)(2,1)} custom-call(s32[1]{0:T(128)} %bitcast.2.place, bf16[512,256]{1,0:T(8,128)(2,1)} %copy-done.15, bf16[512,256]{1,0:T(8,128)(2,1)} %copy-done.20, bf16[512,256]{1,0:T(8,128)(2,1)} %copy-done.21, bf16[512,256]{1,0:T(8,128)(2,1)} %copy-done.22, bf16[512,768]{1,0:T(8,128)(2,1)} %copy-done.10, ...), custom_call_target="tpu_custom_call" | custom-call | tf_op jit(solution)/shard_map/project_out/pallas_call | solution.py:226
  183.9 3.5 %add_bitcast_fusion = (f32[4,256,768]{2,1,0:T(8,128)S(1)}, f32[4,256,768]{2,1,0:T(8,128)S(1)}) fusion(bf16[2,4,256,768]{3,2,1,0:T(8,128)(2,1)} %project_out.2, bf16[2,4,256,768]{3,2,1,0:T(8,128)(2,1)} %collective-permute-done.32), kind=kLoop, calls=%fused_computation.1 | loop fusion | flops 4718592 | bytes 12582912 | tf_op jit(solution)/shard_map/add | solution.py:417
  188.4 2.0 collective-permute-start.34
  191.7 14.8 %all_to_all.5 = bf16[8,32,1152]{2,1,0:T(8,128)(2,1)S(1)} all-to-all(bf16[8,32,1152]{2,1,0:T(8,128)(2,1)S(1)} %copy.14), channel_id=1, replica_groups=mesh['xh'=2,'z'=4,'xl'=2,'y'=4,'c'=2] {'xh','z'}, dimensions={0} | all-to-all | bytes 1179648 | tf_op jit(solution)/shard_map/all_to_all | solution.py:415
  213.6 3.8 %collective-permute-done.37 = bf16[256,384]{1,0:T(8,128)(2,1)S(1)} collective-permute-done((bf16[256,384]{1,0:T(8,128)(2,1)S(1)}, bf16[256,384]{1,0:T(8,128)(2,1)S(1)}, u32[]{:S(2)}, u32[]{:S(2)}) %collective-permute-start.37) | collective-permute-done | bytes 196640 | tf_op jit(solution)/shard_map/ppermute | solution.py:24
  217.4 1.9 collective-permute-done.36
  219.3 2.0 collective-permute-done.35
  229.3 6.0 %collective-permute-done.40 = bf16[4,32,768]{2,1,0:T(8,128)(2,1)S(1)} collective-permute-done((bf16[4,32,768]{2,1,0:T(8,128)(2,1)S(1)}, bf16[4,32,768]{2,1,0:T(8,128)(2,1)S(1)}, u32[]{:S(2)}, u32[]{:S(2)}) %collective-permute-start.40) | collective-permute-done | bytes 196640 | tf_op jit(solution)/shard_map/ppermute | solution.py:438
  239.6 8.9 %collective-permute-done.43 = bf16[256,768]{1,0:T(8,128)(2,1)S(1)} collective-permute-done((bf16[256,768]{1,0:T(8,128)(2,1)S(1)}, bf16[256,768]{1,0:T(8,128)(2,1)S(1)}, u32[]{:S(2)}, u32[]{:S(2)}) %collective-permute-start.43) | collective-permute-done | bytes 393248 | tf_op jit(solution)/shard_map/ppermute | solution.py:24
  248.4 4.4 %collective-permute-start.44 = (bf16[512,384]{1,0:T(8,128)(2,1)S(1)}, bf16[512,384]{1,0:T(8,128)(2,1)S(1)}, u32[]{:S(2)}, u32[]{:S(2)}) collective-permute-start(bf16[512,384]{1,0:T(8,128)(2,1)S(1)} %collective-permute-done.42), channel_id=1, source_target_pairs={{0,64},{64,0},{1,65},{65,1},{2,66},{66,2},{3,67},{67,3},{4,68},{68... | collective-permute-start | bytes 1179656 | tf_op jit(solution)/shard_map/ppermute | solution.py:24
  254.0 7.1 %collective-permute-start.47 = (bf16[512,1152]{1,0:T(8,128)(2,1)}, bf16[512,1152]{1,0:T(8,128)(2,1)}, u32[]{:S(2)}, u32[]{:S(2)}) collective-permute-start(bf16[512,1152]{1,0:T(8,128)(2,1)} %maximum_maximum_fusion.refs_5_), channel_id=1, source_target_pairs={{0,2},{2,0},{4,6},{6,4},{1,3},{3,1},{5,7},{7,5},{8,10},{10,8},{12,... | collective-permute-start | bytes 3538952 | tf_op jit(solution)/shard_map/ppermute | solution.py:24
  261.0 6.1 %collective-permute-start.48 = (bf16[512,1152]{1,0:T(8,128)(2,1)}, bf16[512,1152]{1,0:T(8,128)(2,1)}, u32[]{:S(2)}, u32[]{:S(2)}) collective-permute-start(bf16[512,1152]{1,0:T(8,128)(2,1)} %maximum_maximum_fusion.refs_5_), channel_id=1, source_target_pairs={{0,6},{2,4},{4,2},{6,0},{1,7},{3,5},{5,3},{7,1},{8,14},{10,12},{12... | collective-permute-start | bytes 3538952 | tf_op jit(solution)/shard_map/ppermute | solution.py:24
  268.6 7.1 %collective-permute-start.46 = (bf16[1024,384]{1,0:T(8,128)(2,1)S(1)}, bf16[1024,384]{1,0:T(8,128)(2,1)S(1)}, u32[]{:S(2)}, u32[]{:S(2)}) collective-permute-start(bf16[1024,384]{1,0:T(8,128)(2,1)S(1)} %constant_dynamic-update-slice_fusion.9.refs_0_), channel_id=1, source_target_pairs={{0,48},{16,32},{32,16},{48,0},{1,49},{17,33},{33,17},{49,1},{2,50}... | collective-permute-start | bytes 2359304 | tf_op jit(solution)/shard_map/ppermute | solution.py:24
  275.7 9.2 %collective-permute-done.47.refs_6_ = bf16[512,1152]{1,0:T(8,128)(2,1)} collective-permute-done((bf16[512,1152]{1,0:T(8,128)(2,1)}, bf16[512,1152]{1,0:T(8,128)(2,1)}, u32[]{:S(2)}, u32[]{:S(2)}) %collective-permute-start.47) | collective-permute-done | bytes 1179680 | tf_op jit(solution)/shard_map/ppermute | solution.py:24
  286.0 5.9 %collective-permute-done.48.refs_9_ = bf16[512,1152]{1,0:T(8,128)(2,1)} collective-permute-done((bf16[512,1152]{1,0:T(8,128)(2,1)}, bf16[512,1152]{1,0:T(8,128)(2,1)}, u32[]{:S(2)}, u32[]{:S(2)}) %collective-permute-start.48) | collective-permute-done | bytes 1179680 | tf_op jit(solution)/shard_map/ppermute | solution.py:24
  294.0 2.0 collective-permute-start.49
  297.7 2.8 collective-permute-start.53
  300.5 3.0 collective-permute-done.49.refs_2_
  303.5 3.4 %collective-permute-start.54 = (bf16[512,1152]{1,0:T(8,128)(2,1)}, bf16[512,1152]{1,0:T(8,128)(2,1)}, u32[]{:S(2)}, u32[]{:S(2)}) collective-permute-start(bf16[512,1152]{1,0:T(8,128)(2,1)} %collective-permute-done.47.refs_6_), channel_id=1, source_target_pairs={{0,1},{1,0},{2,3},{3,2},{4,5},{5,4},{6,7},{7,6},{8,9},{9,8},{10,11... | collective-permute-start | bytes 3538952 | tf_op jit(solution)/shard_map/ppermute | solution.py:24
  309.8 3.7 %collective-permute-start.55 = (bf16[256,1152]{1,0:T(8,128)(2,1)}, bf16[256,1152]{1,0:T(8,128)(2,1)}, u32[]{:S(2)}, u32[]{:S(2)}) collective-permute-start(bf16[256,1152]{1,0:T(8,128)(2,1)} %collective-permute-done.51.refs_7_), channel_id=1, source_target_pairs={{0,1},{1,0},{2,3},{3,2},{4,5},{5,4},{6,7},{7,6},{8,9},{9,8},{10,11... | collective-permute-start | bytes 1769480 | tf_op jit(solution)/shard_map/ppermute | solution.py:24
  316.3 11.7 %moments.1 = (f32[384,768]{1,0:T(8,128)}, f32[384,384]{1,0:T(8,128)}) custom-call(s32[2]{0:T(128)} %pad_add_fusion.place, bf16[1024,384]{1,0:T(8,128)(2,1)} %copy-done.19, bf16[1024,384]{1,0:T(8,128)(2,1)} %copy-done.17, bf16[512,384]{1,0:T(8,128)(2,1)} %copy-done.26, bf16[512,384]{1,0:T(8,128)(2,1)} %copy-done.27, bf16[1024,384]{1,0:T(8,128)(2,1)} %copy-done.18, ...), custom_call_target="tpu_custom_call" | custom-call | tf_op jit(solution)/shard_map/moments/pallas_call | solution.py:291
  (237 shorter events, 82.5 us)
Async XLA Ops:
  0.7 32.7 %collective-permute-start.3 = (bf16[3,768,256]{2,1,0:T(8,128)(2,1)}, bf16[3,768,256]{2,1,0:T(8,128)(2,1)}, u32[]{:S(2)}, u32[]{:S(2)}) collective-permute-start(bf16[3,768,256]{2,1,0:T(8,128)(2,1)} %bitcast.55), channel_id=1, source_target_pairs={{0,16},{16,0},{32,48},{48,32},{1,17},{17,1},{33,49},{49,33},{2,18}... | collective-permute-start | bytes 3538952 | tf_op jit(solution)/shard_map/ppermute | solution.py:24
  3.2 30.1 %collective-permute-start.4 = (bf16[3,768,256]{2,1,0:T(8,128)(2,1)}, bf16[3,768,256]{2,1,0:T(8,128)(2,1)}, u32[]{:S(2)}, u32[]{:S(2)}) collective-permute-start(bf16[3,768,256]{2,1,0:T(8,128)(2,1)} %bitcast.56), channel_id=1, source_target_pairs={{0,48},{16,32},{32,16},{48,0},{1,49},{17,33},{33,17},{49,1},{2,50}... | collective-permute-start | bytes 3538952 | tf_op jit(solution)/shard_map/ppermute | solution.py:24
  8.1 11.9 %collective-permute-start = (bf16[64,3072]{1,0:T(8,128)(2,1)S(1)}, bf16[64,3072]{1,0:T(8,128)(2,1)S(1)}, u32[]{:S(2)}, u32[]{:S(2)}) collective-permute-start(bf16[64,3072]{1,0:T(8,128)(2,1)S(1)} %constant_dynamic-update-slice_fusion), channel_id=1, source_target_pairs={{0,64},{64,0},{1,65},{65,1},{2,66},{66,2},{3,67},{67,3},{4,68},{68... | collective-permute-start | bytes 1179656 | tf_op jit(solution)/shard_map/ppermute | solution.py:24
  20.0 9.3 %collective-permute-start.1 = (bf16[64,3072]{1,0:T(8,128)(2,1)S(1)}, bf16[64,3072]{1,0:T(8,128)(2,1)S(1)}, u32[]{:S(2)}, u32[]{:S(2)}) collective-permute-start(bf16[64,3072]{1,0:T(8,128)(2,1)S(1)} %collective-permute-done), channel_id=1, source_target_pairs={{0,2},{2,0},{4,6},{6,4},{1,3},{3,1},{5,7},{7,5},{8,10},{10,8},{12,... | collective-permute-start | bytes 1179656 | tf_op jit(solution)/shard_map/ppermute | solution.py:24
  21.4 10.1 %collective-permute-start.2 = (bf16[64,3072]{1,0:T(8,128)(2,1)S(1)}, bf16[64,3072]{1,0:T(8,128)(2,1)S(1)}, u32[]{:S(2)}, u32[]{:S(2)}) collective-permute-start(bf16[64,3072]{1,0:T(8,128)(2,1)S(1)} %collective-permute-done), channel_id=1, source_target_pairs={{0,6},{2,4},{4,2},{6,0},{1,7},{3,5},{5,3},{7,1},{8,14},{10,12},{12... | collective-permute-start | bytes 1179656 | tf_op jit(solution)/shard_map/ppermute | solution.py:24
  23.3 10.0 %collective-permute-start.5 = (bf16[256,768]{1,0:T(8,128)(2,1)S(1)}, bf16[256,768]{1,0:T(8,128)(2,1)S(1)}, u32[]{:S(2)}, u32[]{:S(2)}) collective-permute-start(bf16[256,768]{1,0:T(8,128)(2,1)S(1)} %copy-done.28), channel_id=1, source_target_pairs={{0,64},{64,0},{1,65},{65,1},{2,66},{66,2},{3,67},{67,3},{4,68},{68... | collective-permute-start | bytes 1179656 | tf_op jit(solution)/shard_map/ppermute | solution.py:24
  34.5 13.1 %collective-permute-start.8 = (bf16[3,384,256]{2,1,0:T(8,128)(2,1)S(1)}, bf16[3,384,256]{2,1,0:T(8,128)(2,1)S(1)}, u32[]{:S(2)}, u32[]{:S(2)}) collective-permute-start(bf16[3,384,256]{2,1,0:T(8,128)(2,1)S(1)} %slice.187), channel_id=1, source_target_pairs={{0,48},{16,32},{32,16},{48,0},{1,49},{17,33},{33,17},{49,1},{2,50}... | collective-permute-start | bytes 1769480 | tf_op jit(solution)/shard_map/ppermute | solution.py:24
  36.3 11.7 %collective-permute-start.9 = (bf16[3,384,256]{2,1,0:T(8,128)(2,1)S(1)}, bf16[3,384,256]{2,1,0:T(8,128)(2,1)S(1)}, u32[]{:S(2)}, u32[]{:S(2)}) collective-permute-start(bf16[3,384,256]{2,1,0:T(8,128)(2,1)S(1)} %slice.188), channel_id=1, source_target_pairs={{0,16},{16,0},{32,48},{48,32},{1,17},{17,1},{33,49},{49,33},{2,18}... | collective-permute-start | bytes 1769480 | tf_op jit(solution)/shard_map/ppermute | solution.py:24
  36.7 9.7 %collective-permute-start.10 = (bf16[256,768]{1,0:T(8,128)(2,1)S(1)}, bf16[256,768]{1,0:T(8,128)(2,1)S(1)}, u32[]{:S(2)}, u32[]{:S(2)}) collective-permute-start(bf16[256,768]{1,0:T(8,128)(2,1)S(1)} %get-tuple-element.100), channel_id=1, source_target_pairs={{0,64},{64,0},{1,65},{65,1},{2,66},{66,2},{3,67},{67,3},{4,68},{68... | collective-permute-start | bytes 1179656 | tf_op jit(solution)/shard_map/ppermute | solution.py:24
  48.1 7.7 %collective-permute-start.13 = (bf16[256,3072]{1,0:T(8,128)(2,1)S(1)}, bf16[256,3072]{1,0:T(8,128)(2,1)S(1)}, u32[]{:S(2)}, u32[]{:S(2)}) collective-permute-start(bf16[256,3072]{1,0:T(8,128)(2,1)S(1)} %constant_dynamic-update-slice_fusion.4), channel_id=1, source_target_pairs={{0,1},{1,0},{2,3},{3,2},{4,5},{5,4},{6,7},{7,6},{8,9},{9,8},{10,11... | collective-permute-start | bytes 4718600 | tf_op jit(solution)/shard_map/ppermute | solution.py:24
  52.2 27.5 %collective-permute-start.11 = (bf16[768,768]{1,0:T(8,128)(2,1)S(1)}, bf16[768,768]{1,0:T(8,128)(2,1)S(1)}, u32[]{:S(2)}, u32[]{:S(2)}) collective-permute-start(bf16[768,768]{1,0:T(8,128)(2,1)S(1)} %copy-done.2), channel_id=1, source_target_pairs={{0,16},{16,0},{32,48},{48,32},{1,17},{17,1},{33,49},{49,33},{2,18}... | collective-permute-start | bytes 3538952 | tf_op jit(solution)/shard_map/ppermute | solution.py:24
  52.7 28.4 %collective-permute-start.12 = (bf16[768,768]{1,0:T(8,128)(2,1)S(1)}, bf16[768,768]{1,0:T(8,128)(2,1)S(1)}, u32[]{:S(2)}, u32[]{:S(2)}) collective-permute-start(bf16[768,768]{1,0:T(8,128)(2,1)S(1)} %copy-done.2), channel_id=1, source_target_pairs={{0,48},{16,32},{32,16},{48,0},{1,49},{17,33},{33,17},{49,1},{2,50}... | collective-permute-start | bytes 3538952 | tf_op jit(solution)/shard_map/ppermute | solution.py:24
  54.5 11.5 %collective-permute-start.14 = (bf16[256,768]{1,0:T(8,128)(2,1)S(1)}, bf16[256,768]{1,0:T(8,128)(2,1)S(1)}, u32[]{:S(2)}, u32[]{:S(2)}) collective-permute-start(bf16[256,768]{1,0:T(8,128)(2,1)S(1)} %get-tuple-element.111), channel_id=1, source_target_pairs={{0,64},{64,0},{1,65},{65,1},{2,66},{66,2},{3,67},{67,3},{4,68},{68... | collective-permute-start | bytes 1179656 | tf_op jit(solution)/shard_map/ppermute | solution.py:24
  66.0 19.0 %collective-permute-start.17 = (bf16[1024,384]{1,0:T(8,128)(2,1)S(1)}, bf16[1024,384]{1,0:T(8,128)(2,1)S(1)}, u32[]{:S(2)}, u32[]{:S(2)}) collective-permute-start(bf16[1024,384]{1,0:T(8,128)(2,1)S(1)} %get-tuple-element.112), channel_id=1, source_target_pairs={{0,64},{64,0},{1,65},{65,1},{2,66},{66,2},{3,67},{67,3},{4,68},{68... | collective-permute-start | bytes 2359304 | tf_op jit(solution)/shard_map/ppermute | solution.py:24
  82.2 14.9 %collective-permute-start.15 = (bf16[384,768]{1,0:T(8,128)(2,1)S(1)}, bf16[384,768]{1,0:T(8,128)(2,1)S(1)}, u32[]{:S(2)}, u32[]{:S(2)}) collective-permute-start(bf16[384,768]{1,0:T(8,128)(2,1)S(1)} %slice.198), channel_id=1, source_target_pairs={{0,48},{16,32},{32,16},{48,0},{1,49},{17,33},{33,17},{49,1},{2,50}... | collective-permute-start | bytes 1769480 | tf_op jit(solution)/shard_map/ppermute | solution.py:24
  84.0 13.4 %collective-permute-start.16 = (bf16[384,768]{1,0:T(8,128)(2,1)S(1)}, bf16[384,768]{1,0:T(8,128)(2,1)S(1)}, u32[]{:S(2)}, u32[]{:S(2)}) collective-permute-start(bf16[384,768]{1,0:T(8,128)(2,1)S(1)} %slice.199), channel_id=1, source_target_pairs={{0,16},{16,0},{32,48},{48,32},{1,17},{17,1},{33,49},{49,33},{2,18}... | collective-permute-start | bytes 1769480 | tf_op jit(solution)/shard_map/ppermute | solution.py:24
  87.2 21.9 %collective-permute-start.18 = (bf16[1024,256]{1,0:T(8,128)(2,1)S(1)}, bf16[1024,256]{1,0:T(8,128)(2,1)S(1)}, u32[]{:S(2)}, u32[]{:S(2)}) collective-permute-start(bf16[1024,256]{1,0:T(8,128)(2,1)S(1)} %pad_maximum_fusion.5.refs_0_), channel_id=1, source_target_pairs={{0,16},{16,0},{32,48},{48,32},{1,17},{17,1},{33,49},{49,33},{2,18}... | collective-permute-start | bytes 1572872 | tf_op jit(solution)/shard_map/ppermute | solution.py:24
  88.0 21.1 %collective-permute-start.19 = (bf16[1024,256]{1,0:T(8,128)(2,1)S(1)}, bf16[1024,256]{1,0:T(8,128)(2,1)S(1)}, u32[]{:S(2)}, u32[]{:S(2)}) collective-permute-start(bf16[1024,256]{1,0:T(8,128)(2,1)S(1)} %pad_maximum_fusion.5.refs_0_), channel_id=1, source_target_pairs={{0,48},{16,32},{32,16},{48,0},{1,49},{17,33},{33,17},{49,1},{2,50}... | collective-permute-start | bytes 1572872 | tf_op jit(solution)/shard_map/ppermute | solution.py:24
  102.0 16.2 %collective-permute-start.20 = (bf16[512,768]{1,0:T(8,128)(2,1)S(1)}, bf16[512,768]{1,0:T(8,128)(2,1)S(1)}, u32[]{:S(2)}, u32[]{:S(2)}) collective-permute-start(bf16[512,768]{1,0:T(8,128)(2,1)S(1)} %project_mlp.2), channel_id=1, source_target_pairs={{0,64},{64,0},{1,65},{65,1},{2,66},{66,2},{3,67},{67,3},{4,68},{68... | collective-permute-start | bytes 2359304 | tf_op jit(solution)/shard_map/ppermute | solution.py:24
  109.1 9.1 %collective-permute-start.21 = (bf16[512,256]{1,0:T(8,128)(2,1)S(1)}, bf16[512,256]{1,0:T(8,128)(2,1)S(1)}, u32[]{:S(2)}, u32[]{:S(2)}) collective-permute-start(bf16[512,256]{1,0:T(8,128)(2,1)S(1)} %slice.203), channel_id=1, source_target_pairs={{0,48},{16,32},{32,16},{48,0},{1,49},{17,33},{33,17},{49,1},{2,50}... | collective-permute-start | bytes 786440 | tf_op jit(solution)/shard_map/ppermute | solution.py:24
  123.1 13.8 %collective-permute-start.23 = (bf16[512,768]{1,0:T(8,128)(2,1)S(1)}, bf16[512,768]{1,0:T(8,128)(2,1)S(1)}, u32[]{:S(2)}, u32[]{:S(2)}) collective-permute-start(bf16[512,768]{1,0:T(8,128)(2,1)S(1)} %fusion.2.refs_4_), channel_id=1, source_target_pairs={{0,16},{16,0},{32,48},{48,32},{1,17},{17,1},{33,49},{49,33},{2,18}... | collective-permute-start | bytes 2359304 | tf_op jit(solution)/shard_map/ppermute | solution.py:24
  124.0 15.2 %collective-permute-start.24 = (bf16[512,768]{1,0:T(8,128)(2,1)S(1)}, bf16[512,768]{1,0:T(8,128)(2,1)S(1)}, u32[]{:S(2)}, u32[]{:S(2)}) collective-permute-start(bf16[512,768]{1,0:T(8,128)(2,1)S(1)} %fusion.2.refs_4_), channel_id=1, source_target_pairs={{0,48},{16,32},{32,16},{48,0},{1,49},{17,33},{33,17},{49,1},{2,50}... | collective-permute-start | bytes 2359304 | tf_op jit(solution)/shard_map/ppermute | solution.py:24
  125.3 9.4 %collective-permute-start.25 = (bf16[256,768]{1,0:T(8,128)(2,1)S(1)}, bf16[256,768]{1,0:T(8,128)(2,1)S(1)}, u32[]{:S(2)}, u32[]{:S(2)}) collective-permute-start(bf16[256,768]{1,0:T(8,128)(2,1)S(1)} %get-tuple-element.137), channel_id=1, source_target_pairs={{0,64},{64,0},{1,65},{65,1},{2,66},{66,2},{3,67},{67,3},{4,68},{68... | collective-permute-start | bytes 1179656 | tf_op jit(solution)/shard_map/ppermute | solution.py:24
  140.7 19.3 %collective-permute-start.30 = (bf16[256,768]{1,0:T(8,128)(2,1)S(1)}, bf16[256,768]{1,0:T(8,128)(2,1)}, u32[]{:S(2)}, u32[]{:S(2)}) collective-permute-start(bf16[256,768]{1,0:T(8,128)(2,1)S(1)} %slice.210), channel_id=1, source_target_pairs={{0,48},{16,32},{32,16},{48,0},{1,49},{17,33},{33,17},{49,1},{2,50}... | collective-permute-start | bytes 1179656 | tf_op jit(solution)/shard_map/ppermute | solution.py:24
  142.3 17.6 %collective-permute-start.31 = (bf16[256,768]{1,0:T(8,128)(2,1)S(1)}, bf16[256,768]{1,0:T(8,128)(2,1)}, u32[]{:S(2)}, u32[]{:S(2)}) collective-permute-start(bf16[256,768]{1,0:T(8,128)(2,1)S(1)} %slice.211), channel_id=1, source_target_pairs={{0,16},{16,0},{32,48},{48,32},{1,17},{17,1},{33,49},{49,33},{2,18}... | collective-permute-start | bytes 1179656 | tf_op jit(solution)/shard_map/ppermute | solution.py:24
  144.8 13.5 %collective-permute-start.28 = (bf16[512,256]{1,0:T(8,128)(2,1)S(1)}, bf16[512,256]{1,0:T(8,128)(2,1)S(1)}, u32[]{:S(2)}, u32[]{:S(2)}) collective-permute-start(bf16[512,256]{1,0:T(8,128)(2,1)S(1)} %pad_maximum_fusion.7.refs_0_), channel_id=1, source_target_pairs={{0,32},{16,48},{32,0},{48,16},{1,33},{17,49},{33,1},{49,17},{2,34}... | collective-permute-start | bytes 786440 | tf_op jit(solution)/shard_map/ppermute | solution.py:24
  147.5 12.4 %collective-permute-start.29 = (bf16[512,256]{1,0:T(8,128)(2,1)S(1)}, bf16[512,256]{1,0:T(8,128)(2,1)S(1)}, u32[]{:S(2)}, u32[]{:S(2)}) collective-permute-start(bf16[512,256]{1,0:T(8,128)(2,1)S(1)} %pad_maximum_fusion.7.refs_0_), channel_id=1, source_target_pairs={{0,48},{16,32},{32,16},{48,0},{1,49},{17,33},{33,17},{49,1},{2,50}... | collective-permute-start | bytes 786440 | tf_op jit(solution)/shard_map/ppermute | solution.py:24
  168.6 15.3 %collective-permute-start.32 = (bf16[2,4,256,768]{3,2,1,0:T(8,128)(2,1)}, bf16[2,4,256,768]{3,2,1,0:T(8,128)(2,1)}, u32[]{:S(2)}, u32[]{:S(2)}) collective-permute-start(bf16[2,4,256,768]{3,2,1,0:T(8,128)(2,1)} %project_out.3), channel_id=1, source_target_pairs={{0,1},{1,0},{2,3},{3,2},{4,5},{5,4},{6,7},{7,6},{8,9},{9,8},{10,11... | collective-permute-start | bytes 9437192 | tf_op jit(solution)/shard_map/ppermute | solution.py:24
  187.6 19.2 %collective-permute-start.33 = (bf16[4,128,768]{2,1,0:T(8,128)(2,1)S(1)}, bf16[4,128,768]{2,1,0:T(8,128)(2,1)S(1)}, u32[]{:S(2)}, u32[]{:S(2)}) collective-permute-start(bf16[4,128,768]{2,1,0:T(8,128)(2,1)S(1)} %slice.351), channel_id=1, source_target_pairs={{0,2},{2,0},{4,6},{6,4},{1,3},{3,1},{5,7},{7,5},{8,10},{10,8},{12,... | collective-permute-start | bytes 2359304 | tf_op jit(solution)/shard_map/ppermute | solution.py:24
  188.4 20.1 %collective-permute-start.34 = (bf16[4,128,768]{2,1,0:T(8,128)(2,1)S(1)}, bf16[4,128,768]{2,1,0:T(8,128)(2,1)S(1)}, u32[]{:S(2)}, u32[]{:S(2)}) collective-permute-start(bf16[4,128,768]{2,1,0:T(8,128)(2,1)S(1)} %slice.350), channel_id=1, source_target_pairs={{0,6},{2,4},{4,2},{6,0},{1,7},{3,5},{5,3},{7,1},{8,14},{10,12},{12... | collective-permute-start | bytes 2359304 | tf_op jit(solution)/shard_map/ppermute | solution.py:24
  209.5 9.8 %collective-permute-start.36 = (bf16[4,64,768]{2,1,0:T(8,128)(2,1)}, bf16[4,64,768]{2,1,0:T(8,128)(2,1)}, u32[]{:S(2)}, u32[]{:S(2)}) collective-permute-start(bf16[4,64,768]{2,1,0:T(8,128)(2,1)} %fusion.12), channel_id=1, source_target_pairs={{0,2},{2,0},{4,6},{6,4},{1,3},{3,1},{5,7},{7,5},{8,10},{10,8},{12,... | collective-permute-start | bytes 1179656 | tf_op jit(solution)/shard_map/ppermute | solution.py:24
  210.4 11.0 %collective-permute-start.35 = (bf16[4,64,768]{2,1,0:T(8,128)(2,1)}, bf16[4,64,768]{2,1,0:T(8,128)(2,1)}, u32[]{:S(2)}, u32[]{:S(2)}) collective-permute-start(bf16[4,64,768]{2,1,0:T(8,128)(2,1)} %fusion.13), channel_id=1, source_target_pairs={{0,6},{2,4},{4,2},{6,0},{1,7},{3,5},{5,3},{7,1},{8,14},{10,12},{12... | collective-permute-start | bytes 1179656 | tf_op jit(solution)/shard_map/ppermute | solution.py:24
  224.6 10.6 %collective-permute-start.40 = (bf16[4,32,768]{2,1,0:T(8,128)(2,1)S(1)}, bf16[4,32,768]{2,1,0:T(8,128)(2,1)S(1)}, u32[]{:S(2)}, u32[]{:S(2)}) collective-permute-start(bf16[4,32,768]{2,1,0:T(8,128)(2,1)S(1)} %get-tuple-element.206), channel_id=1, source_target_pairs={{0,72},{8,64},{64,8},{72,0},{1,73},{9,65},{65,9},{73,1},{2,74},{10... | collective-permute-start | bytes 589832 | tf_op jit(solution)/shard_map/ppermute | solution.py:438
  227.4 8.1 %collective-permute-start.38 = (bf16[4,32,768]{2,1,0:T(8,128)(2,1)S(1)}, bf16[4,32,768]{2,1,0:T(8,128)(2,1)S(1)}, u32[]{:S(2)}, u32[]{:S(2)}) collective-permute-start(bf16[4,32,768]{2,1,0:T(8,128)(2,1)S(1)} %slice.353), channel_id=1, source_target_pairs={{0,8},{8,0},{1,9},{9,1},{2,10},{10,2},{3,11},{11,3},{4,12},{12,4},... | collective-permute-start | bytes 589832 | tf_op jit(solution)/shard_map/ppermute | solution.py:24
  237.7 10.7 %collective-permute-start.43 = (bf16[256,768]{1,0:T(8,128)(2,1)S(1)}, bf16[256,768]{1,0:T(8,128)(2,1)S(1)}, u32[]{:S(2)}, u32[]{:S(2)}) collective-permute-start(bf16[256,768]{1,0:T(8,128)(2,1)S(1)} %fusion.16), channel_id=1, source_target_pairs={{0,8},{8,0},{1,9},{9,1},{2,10},{10,2},{3,11},{11,3},{4,12},{12,4},... | collective-permute-start | bytes 1179656 | tf_op jit(solution)/shard_map/ppermute | solution.py:24
  238.9 9.6 %collective-permute-start.42 = (bf16[512,384]{1,0:T(8,128)(2,1)S(1)}, bf16[512,384]{1,0:T(8,128)(2,1)S(1)}, u32[]{:S(2)}, u32[]{:S(2)}) collective-permute-start(bf16[512,384]{1,0:T(8,128)(2,1)S(1)} %pad_maximum_fusion.6), channel_id=1, source_target_pairs={{0,0},{2,16},{4,32},{6,48},{8,64},{10,80},{12,96},{14,112},{16,2},... | collective-permute-start | bytes 1179656 | tf_op jit(solution)/shard_map/ppermute | solution.py:452
  248.4 18.8 %collective-permute-start.44 = (bf16[512,384]{1,0:T(8,128)(2,1)S(1)}, bf16[512,384]{1,0:T(8,128)(2,1)S(1)}, u32[]{:S(2)}, u32[]{:S(2)}) collective-permute-start(bf16[512,384]{1,0:T(8,128)(2,1)S(1)} %collective-permute-done.42), channel_id=1, source_target_pairs={{0,64},{64,0},{1,65},{65,1},{2,66},{66,2},{3,67},{67,3},{4,68},{68... | collective-permute-start | bytes 1179656 | tf_op jit(solution)/shard_map/ppermute | solution.py:24
  254.0 31.0 %collective-permute-start.47 = (bf16[512,1152]{1,0:T(8,128)(2,1)}, bf16[512,1152]{1,0:T(8,128)(2,1)}, u32[]{:S(2)}, u32[]{:S(2)}) collective-permute-start(bf16[512,1152]{1,0:T(8,128)(2,1)} %maximum_maximum_fusion.refs_5_), channel_id=1, source_target_pairs={{0,2},{2,0},{4,6},{6,4},{1,3},{3,1},{5,7},{7,5},{8,10},{10,8},{12,... | collective-permute-start | bytes 3538952 | tf_op jit(solution)/shard_map/ppermute | solution.py:24
  261.0 31.0 %collective-permute-start.48 = (bf16[512,1152]{1,0:T(8,128)(2,1)}, bf16[512,1152]{1,0:T(8,128)(2,1)}, u32[]{:S(2)}, u32[]{:S(2)}) collective-permute-start(bf16[512,1152]{1,0:T(8,128)(2,1)} %maximum_maximum_fusion.refs_5_), channel_id=1, source_target_pairs={{0,6},{2,4},{4,2},{6,0},{1,7},{3,5},{5,3},{7,1},{8,14},{10,12},{12... | collective-permute-start | bytes 3538952 | tf_op jit(solution)/shard_map/ppermute | solution.py:24
  267.3 25.8 %collective-permute-start.45 = (bf16[1024,384]{1,0:T(8,128)(2,1)S(1)}, bf16[1024,384]{1,0:T(8,128)(2,1)S(1)}, u32[]{:S(2)}, u32[]{:S(2)}) collective-permute-start(bf16[1024,384]{1,0:T(8,128)(2,1)S(1)} %constant_dynamic-update-slice_fusion.9.refs_0_), channel_id=1, source_target_pairs={{0,16},{16,0},{32,48},{48,32},{1,17},{17,1},{33,49},{49,33},{2,18}... | collective-permute-start | bytes 2359304 | tf_op jit(solution)/shard_map/ppermute | solution.py:24
  268.6 24.5 %collective-permute-start.46 = (bf16[1024,384]{1,0:T(8,128)(2,1)S(1)}, bf16[1024,384]{1,0:T(8,128)(2,1)S(1)}, u32[]{:S(2)}, u32[]{:S(2)}) collective-permute-start(bf16[1024,384]{1,0:T(8,128)(2,1)S(1)} %constant_dynamic-update-slice_fusion.9.refs_0_), channel_id=1, source_target_pairs={{0,48},{16,32},{32,16},{48,0},{1,49},{17,33},{33,17},{49,1},{2,50}... | collective-permute-start | bytes 2359304 | tf_op jit(solution)/shard_map/ppermute | solution.py:24
  294.0 9.4 %collective-permute-start.49 = (bf16[512,384]{1,0:T(8,128)(2,1)S(1)}, bf16[512,384]{1,0:T(8,128)(2,1)S(1)}, u32[]{:S(2)}, u32[]{:S(2)}) collective-permute-start(bf16[512,384]{1,0:T(8,128)(2,1)S(1)} %slice.242), channel_id=1, source_target_pairs={{0,48},{16,32},{32,16},{48,0},{1,49},{17,33},{33,17},{49,1},{2,50}... | collective-permute-start | bytes 1179656 | tf_op jit(solution)/shard_map/ppermute | solution.py:24
  296.1 10.8 %collective-permute-start.50 = (bf16[512,384]{1,0:T(8,128)(2,1)S(1)}, bf16[512,384]{1,0:T(8,128)(2,1)S(1)}, u32[]{:S(2)}, u32[]{:S(2)}) collective-permute-start(bf16[512,384]{1,0:T(8,128)(2,1)S(1)} %slice.243), channel_id=1, source_target_pairs={{0,16},{16,0},{32,48},{48,32},{1,17},{17,1},{33,49},{49,33},{2,18}... | collective-permute-start | bytes 1179656 | tf_op jit(solution)/shard_map/ppermute | solution.py:24
  296.2 13.4 %collective-permute-start.51 = (bf16[256,1152]{1,0:T(8,128)(2,1)S(1)}, bf16[256,1152]{1,0:T(8,128)(2,1)}, u32[]{:S(2)}, u32[]{:S(2)}) collective-permute-start(bf16[256,1152]{1,0:T(8,128)(2,1)S(1)} %slice.275), channel_id=1, source_target_pairs={{0,6},{2,4},{4,2},{6,0},{1,7},{3,5},{5,3},{7,1},{8,14},{10,12},{12... | collective-permute-start | bytes 1769480 | tf_op jit(solution)/shard_map/ppermute | solution.py:24
  297.7 12.1 %collective-permute-start.52 = (bf16[256,1152]{1,0:T(8,128)(2,1)S(1)}, bf16[256,1152]{1,0:T(8,128)(2,1)}, u32[]{:S(2)}, u32[]{:S(2)}) collective-permute-start(bf16[256,1152]{1,0:T(8,128)(2,1)S(1)} %slice.276), channel_id=1, source_target_pairs={{0,2},{2,0},{4,6},{6,4},{1,3},{3,1},{5,7},{7,5},{8,10},{10,8},{12,... | collective-permute-start | bytes 1769480 | tf_op jit(solution)/shard_map/ppermute | solution.py:24
  297.7 16.5 %collective-permute-start.53 = (bf16[512,1152]{1,0:T(8,128)(2,1)}, bf16[512,1152]{1,0:T(8,128)(2,1)}, u32[]{:S(2)}, u32[]{:S(2)}) collective-permute-start(bf16[512,1152]{1,0:T(8,128)(2,1)} %maximum_maximum_fusion.refs_5_), channel_id=1, source_target_pairs={{0,1},{1,0},{2,3},{3,2},{4,5},{5,4},{6,7},{7,6},{8,9},{9,8},{10,11... | collective-permute-start | bytes 3538952 | tf_op jit(solution)/shard_map/ppermute | solution.py:24
  303.5 12.9 %collective-permute-start.54 = (bf16[512,1152]{1,0:T(8,128)(2,1)}, bf16[512,1152]{1,0:T(8,128)(2,1)}, u32[]{:S(2)}, u32[]{:S(2)}) collective-permute-start(bf16[512,1152]{1,0:T(8,128)(2,1)} %collective-permute-done.47.refs_6_), channel_id=1, source_target_pairs={{0,1},{1,0},{2,3},{3,2},{4,5},{5,4},{6,7},{7,6},{8,9},{9,8},{10,11... | collective-permute-start | bytes 3538952 | tf_op jit(solution)/shard_map/ppermute | solution.py:24
  306.8 9.5 %collective-permute-start.57 = (bf16[512,1152]{1,0:T(8,128)(2,1)}, bf16[512,1152]{1,0:T(8,128)(2,1)}, u32[]{:S(2)}, u32[]{:S(2)}) collective-permute-start(bf16[512,1152]{1,0:T(8,128)(2,1)} %collective-permute-done.48.refs_9_), channel_id=1, source_target_pairs={{0,1},{1,0},{2,3},{3,2},{4,5},{5,4},{6,7},{7,6},{8,9},{9,8},{10,11... | collective-permute-start | bytes 3538952 | tf_op jit(solution)/shard_map/ppermute | solution.py:24
  (44 other events, 531.6 us)

commit v2 on v1

--- a/solution.py
+++ b/solution.py
@@ -217,20 +217,19 @@
 def project_out(attended, hidden, which, weights, xh, dtype):
     rows = hidden[2].shape[0]
     _, depth, block = weights.shape
-    step = block // 3
 
     def rows_of(x):
         at = 0 if x.shape[0] == rows else which
-        return pl.BlockSpec((rows, x.shape[1]), lambda side, i, place: (at, 0), pipeline_mode=pl.Buffered(1))
+        return pl.BlockSpec((rows, x.shape[1]), lambda side, place: (at, 0), pipeline_mode=pl.Buffered(1))
 
     return pl.pallas_call(
         output_kernel,
         grid_spec=pltpu.PrefetchScalarGridSpec(
             num_scalar_prefetch=1,
-            grid=(2, 3),
+            grid=(2,),
             in_specs=[rows_of(x) for x in (*attended, *hidden)]
-            + [pl.BlockSpec((1, depth, step), lambda side, i, place: (side, 0, i))],
-            out_specs=pl.BlockSpec((1, 4, rows, step), lambda side, i, place: (side, 0, 0, i)),
+            + [pl.BlockSpec((1, depth, block), lambda side, place: (side, 0, 0))],
+            out_specs=pl.BlockSpec((1, 4, rows, block), lambda side, place: (side, 0, 0, 0)),
         ),
         out_shape=jax.ShapeDtypeStruct((2, 4, rows, block), dtype),
         compiler_params=pltpu.CompilerParams(vmem_limit_bytes=60 * 2**20),

time: 329 us -> 326 us (level)
  transfers between devices with their start and end apart: 58 -> 58, of which waited for: 36 -> 36; matrix products, arithmetic and copies ran while one was open for 5% -> 5% of each run, Pallas kernels for 13% -> 12%
where the time goes in v2:
time: 326 us
  waiting for transfers between devices  112 us (34%)
  starting transfers between devices  103 us (32%)
  Pallas kernels  58.3 us (18%)
  other arithmetic  19.7 us (6%)
  local copies, waits for them, and re-layouts  16.2 us (5%)
  blocking collectives  14.8 us (5%)
    ppermute x56, waiting for transfers between devices, swap(): return lax.ppermute(x, axis, [(i, i ^ mask) for i in range(size)])  106 us
    ppermute x56, starting transfers between devices, swap(): return lax.ppermute(x, axis, [(i, i ^ mask) for i in range(size)])  100 us
    all_to_all x1, blocking collectives, on_device(): lax.all_to_all(spread_rows, ('xh', 'z'), split_axis=0, concat_axis=0, til...  14.8 us
    pallas_call x2, Pallas kernels, project_out(): pl.pallas_call(output_kernel, grid_spec=pltpu.PrefetchScalarGridSpec(num_...  13.5 us
    pallas_call x1, Pallas kernels, moments(): pl.pallas_call(kernel, grid_spec=pltpu.PrefetchScalarGridSpec(num_scalar_...  11.7 us
    pallas_call x2, Pallas kernels, project_mlp(): pl.pallas_call(mlp_kernel, grid=(3,), in_specs=[pl.BlockSpec(x.shape, lam...  10 us
    pallas_call x1, Pallas kernels, attend(): pl.pallas_call(attend_kernel, grid=(rows // step,), in_specs=[pl.BlockSpe...  7.98 us
    pallas_call x2, Pallas kernels, norm_rows(): pl.pallas_call(norm_kernel, grid_spec=pltpu.PrefetchScalarGridSpec(num_sc...  7.6 us
  transfers between devices with their start and end apart: 58, of which 36 were waited for; matrix products, arithmetic and copies ran while one was open for 5% of the time, Pallas kernels for 12%

profile of v2, /device:TPU:1, one launch (start us, length us, event | category | flops | bytes accessed | tf_op | source)
XLA Modules:
  0.0 325.6 jit_solution(4317845169746868160)
XLA Ops:
  0.7 2.5 collective-permute-start.3
  3.2 2.2 collective-permute-start.4
  8.1 2.8 collective-permute-start
  10.9 2.8 copy-done.1
  13.7 6.3 %norm_rows.3 = (bf16[512,768]{1,0:T(8,128)(2,1)S(1)}, bf16[512,768]{1,0:T(8,128)(2,1)S(1)}, bf16[512,768]{1,0:T(8,128)(2,1)S(1)}, bf16[512,768]{1,0:T(8,128)(2,1)S(1)}) custom-call(s32[3]{0:T(128)S(1)} %get-tuple-element.212.place, bf16[512,6144]{1,0:T(8,128)(2,1)S(1)} %copy-done.1, f32[1,6144]{1,0:T(1,128)S(1)} %bitcast.59), custom_call_target="tpu_custom_call" | custom-call | tf_op jit(solution)/shard_map/norm_rows/pallas_call | solution.py:83
  25.2 4.1 %collective-permute-done.1 = bf16[64,3072]{1,0:T(8,128)(2,1)S(1)} collective-permute-done((bf16[64,3072]{1,0:T(8,128)(2,1)S(1)}, bf16[64,3072]{1,0:T(8,128)(2,1)S(1)}, u32[]{:S(2)}, u32[]{:S(2)}) %collective-permute-start.1) | collective-permute-done | bytes 393248 | tf_op jit(solution)/shard_map/ppermute | solution.py:24
  29.3 2.2 collective-permute-done.2
  36.7 2.0 collective-permute-start.10
  38.8 2.8 collective-permute-start.6
  41.7 3.2 collective-permute-done.6
  48.1 4.2 %collective-permute-start.13 = (bf16[256,3072]{1,0:T(8,128)(2,1)S(1)}, bf16[256,3072]{1,0:T(8,128)(2,1)S(1)}, u32[]{:S(2)}, u32[]{:S(2)}) collective-permute-start(bf16[256,3072]{1,0:T(8,128)(2,1)S(1)} %constant_dynamic-update-slice_fusion.4), channel_id=1, source_target_pairs={{0,1},{1,0},{2,3},{3,2},{4,5},{5,4},{6,7},{7,6},{8,9},{9,8},{10,11... | collective-permute-start | bytes 4718600 | tf_op jit(solution)/shard_map/ppermute | solution.py:24
  57.3 7.4 %project_qkv.1 = (bf16[1024,384]{1,0:T(8,128)(2,1)S(1)}, f32[1024,384]{1,0:T(8,128)S(1)}) custom-call(s32[1]{0:T(128)} %bitcast.2.place, bf16[512,768]{1,0:T(8,128)(2,1)S(1)} %get-tuple-element.123.refs_0_, bf16[512,768]{1,0:T(8,128)(2,1)S(1)} %get-tuple-element.124.refs_1_, bf16[512,768]{1,0:T(8,128)(2,1)S(1)} %get-tuple-element.125.refs_2_, ...), custom_call_target="tpu_custom_call" | custom-call | tf_op jit(solution)/shard_map/project_qkv/pallas_call | solution.py:168
  67.2 12.6 %collective-permute-done.11.refs_5_ = bf16[768,768]{1,0:T(8,128)(2,1)S(1)} collective-permute-done((bf16[768,768]{1,0:T(8,128)(2,1)S(1)}, bf16[768,768]{1,0:T(8,128)(2,1)S(1)}, u32[]{:S(2)}, u32[]{:S(2)}) %collective-permute-start.11) | collective-permute-done | bytes 1179680 | tf_op jit(solution)/shard_map/ppermute | solution.py:24
  88.6 8.5 %collective-permute-done.15.refs_6_ = bf16[384,768]{1,0:T(8,128)(2,1)S(1)} collective-permute-done((bf16[384,768]{1,0:T(8,128)(2,1)S(1)}, bf16[384,768]{1,0:T(8,128)(2,1)S(1)}, u32[]{:S(2)}, u32[]{:S(2)}) %collective-permute-start.15) | collective-permute-done | bytes 589856 | tf_op jit(solution)/shard_map/ppermute | solution.py:24
  97.4 4.6 %project_mlp.2 = bf16[512,768]{1,0:T(8,128)(2,1)S(1)} custom-call(bf16[512,768]{1,0:T(8,128)(2,1)S(1)} %pad_maximum_fusion.1.refs_4_.refs_0_, bf16[512,768]{1,0:T(8,128)(2,1)S(1)} %pad_maximum_fusion.2.refs_5_.refs_1_, bf16[512,768]{1,0:T(8,128)(2,1)S(1)} %pad_maximum_fusion.3.refs_6_.refs_2_, bf16[512,768]{1,0:T(8,128)(2,1)S(1)} %pad_maximum_fusion.4.refs_7_.refs_3_, ...), custom_call_target="tpu_custom_call" | custom-call | tf_op jit(solution)/shard_map/project_mlp/pallas_call | solution.py:194
  103.7 5.4 %project_mlp.3 = f32[512,768]{1,0:T(8,128)} custom-call(bf16[512,768]{1,0:T(8,128)(2,1)S(1)} %get-tuple-element.123.refs_0_, bf16[512,768]{1,0:T(8,128)(2,1)S(1)} %get-tuple-element.124.refs_1_, bf16[512,768]{1,0:T(8,128)(2,1)S(1)} %get-tuple-element.125.refs_2_, bf16[512,768]{1,0:T(8,128)(2,1)S(1)} %get-tuple-element.126.refs_3_, ...), custom_call_target="tpu_custom_call" | custom-call | tf_op jit(solution)/shard_map/project_mlp/pallas_call | solution.py:194
  110.7 7.6 %collective-permute-done.20 = bf16[512,768]{1,0:T(8,128)(2,1)S(1)} collective-permute-done((bf16[512,768]{1,0:T(8,128)(2,1)S(1)}, bf16[512,768]{1,0:T(8,128)(2,1)S(1)}, u32[]{:S(2)}, u32[]{:S(2)}) %collective-permute-start.20) | collective-permute-done | bytes 786464 | tf_op jit(solution)/shard_map/ppermute | solution.py:24
  118.3 4.7 %fusion.2.refs_4_ = bf16[512,768]{1,0:T(8,128)(2,1)S(1)} fusion(f32[512,768]{1,0:T(8,128)} %project_mlp.3, bf16[512,768]{1,0:T(8,128)(2,1)S(1)} %collective-permute-done.20, f32[768]{0:T(1024)S(1)} %copy-done.31), kind=kLoop, calls=%fused_computation.6 | loop fusion | flops 26738688 | bytes 3148800 | tf_op jit(solution)/shard_map/convert_element_type | solution.py:389
  126.7 8.0 %attend.1 = bf16[1024,128]{1,0:T(8,128)(2,1)S(1)} custom-call(bf16[1024,128]{1,0:T(8,128)(2,1)S(1)} %get-tuple-element.133.q_ref, bf16[1024,256]{1,0:T(8,128)(2,1)S(1)} %pad_maximum_fusion.5.refs_0_, bf16[1024,256]{1,0:T(8,128)(2,1)S(1)} %collective-permute-done.18.refs_1_, bf16[1024,256]{1,0:T(8,128)(2,1)S(1)} %collective-permute-done.19.refs_2_, ...), custom_call_target="tpu_custom_call" | custom-call | tf_op jit(solution)/shard_map/attend/pallas_call | solution.py:121
  134.7 2.1 collective-permute-done.23.refs_5_
  136.9 2.3 collective-permute-done.24.refs_7_
  142.4 2.2 collective-permute-done.26
  144.8 2.8 collective-permute-start.28
  148.7 1.9 pad_maximum_fusion.refs_8_
  152.3 6.1 %collective-permute-done.28.refs_2_ = bf16[512,256]{1,0:T(8,128)(2,1)S(1)} collective-permute-done((bf16[512,256]{1,0:T(8,128)(2,1)S(1)}, bf16[512,256]{1,0:T(8,128)(2,1)S(1)}, u32[]{:S(2)}, u32[]{:S(2)}) %collective-permute-start.28) | collective-permute-done | bytes 262176 | tf_op jit(solution)/shard_map/ppermute | solution.py:24
  160.7 6.7 %project_out.3 = bf16[2,4,256,768]{3,2,1,0:T(8,128)(2,1)} custom-call(s32[1]{0:T(128)} %bitcast.2.place, bf16[512,256]{1,0:T(8,128)(2,1)} %copy-done.15, bf16[512,256]{1,0:T(8,128)(2,1)} %copy-done.20, bf16[512,256]{1,0:T(8,128)(2,1)} %copy-done.21, bf16[512,256]{1,0:T(8,128)(2,1)} %copy-done.22, bf16[512,768]{1,0:T(8,128)(2,1)} %copy-done.10, ...), custom_call_target="tpu_custom_call" | custom-call | tf_op jit(solution)/shard_map/project_out/pallas_call | solution.py:225
  167.4 7.2 %collective-permute-start.32 = (bf16[2,4,256,768]{3,2,1,0:T(8,128)(2,1)}, bf16[2,4,256,768]{3,2,1,0:T(8,128)(2,1)}, u32[]{:S(2)}, u32[]{:S(2)}) collective-permute-start(bf16[2,4,256,768]{3,2,1,0:T(8,128)(2,1)} %project_out.3), channel_id=1, source_target_pairs={{0,1},{1,0},{2,3},{3,2},{4,5},{5,4},{6,7},{7,6},{8,9},{9,8},{10,11... | collective-permute-start | bytes 9437192 | tf_op jit(solution)/shard_map/ppermute | solution.py:24
  174.7 6.8 %project_out.2 = bf16[2,4,256,768]{3,2,1,0:T(8,128)(2,1)} custom-call(s32[1]{0:T(128)} %bitcast.2.place, bf16[512,256]{1,0:T(8,128)(2,1)} %copy-done.15, bf16[512,256]{1,0:T(8,128)(2,1)} %copy-done.20, bf16[512,256]{1,0:T(8,128)(2,1)} %copy-done.21, bf16[512,256]{1,0:T(8,128)(2,1)} %copy-done.22, bf16[512,768]{1,0:T(8,128)(2,1)} %copy-done.10, ...), custom_call_target="tpu_custom_call" | custom-call | tf_op jit(solution)/shard_map/project_out/pallas_call | solution.py:225
  181.5 3.5 %add_bitcast_fusion = (f32[4,256,768]{2,1,0:T(8,128)S(1)}, f32[4,256,768]{2,1,0:T(8,128)S(1)}) fusion(bf16[2,4,256,768]{3,2,1,0:T(8,128)(2,1)} %project_out.2, bf16[2,4,256,768]{3,2,1,0:T(8,128)(2,1)} %collective-permute-done.32), kind=kLoop, calls=%fused_computation.1 | loop fusion | flops 4718592 | bytes 12582912 | tf_op jit(solution)/shard_map/add | solution.py:416
  186.0 2.0 collective-permute-start.34
  189.3 14.8 %all_to_all.5 = bf16[8,32,1152]{2,1,0:T(8,128)(2,1)S(1)} all-to-all(bf16[8,32,1152]{2,1,0:T(8,128)(2,1)S(1)} %copy.14), channel_id=1, replica_groups=mesh['xh'=2,'z'=4,'xl'=2,'y'=4,'c'=2] {'xh','z'}, dimensions={0} | all-to-all | bytes 1179648 | tf_op jit(solution)/shard_map/all_to_all | solution.py:414
  211.2 3.8 %collective-permute-done.37 = bf16[256,384]{1,0:T(8,128)(2,1)S(1)} collective-permute-done((bf16[256,384]{1,0:T(8,128)(2,1)S(1)}, bf16[256,384]{1,0:T(8,128)(2,1)S(1)}, u32[]{:S(2)}, u32[]{:S(2)}) %collective-permute-start.37) | collective-permute-done | bytes 196640 | tf_op jit(solution)/shard_map/ppermute | solution.py:24
  215.0 1.9 collective-permute-done.36
  216.9 2.0 collective-permute-done.35
  226.7 6.0 %collective-permute-done.40 = bf16[4,32,768]{2,1,0:T(8,128)(2,1)S(1)} collective-permute-done((bf16[4,32,768]{2,1,0:T(8,128)(2,1)S(1)}, bf16[4,32,768]{2,1,0:T(8,128)(2,1)S(1)}, u32[]{:S(2)}, u32[]{:S(2)}) %collective-permute-start.40) | collective-permute-done | bytes 196640 | tf_op jit(solution)/shard_map/ppermute | solution.py:437
  236.9 8.9 %collective-permute-done.43 = bf16[256,768]{1,0:T(8,128)(2,1)S(1)} collective-permute-done((bf16[256,768]{1,0:T(8,128)(2,1)S(1)}, bf16[256,768]{1,0:T(8,128)(2,1)S(1)}, u32[]{:S(2)}, u32[]{:S(2)}) %collective-permute-start.43) | collective-permute-done | bytes 393248 | tf_op jit(solution)/shard_map/ppermute | solution.py:24
  245.8 4.4 %collective-permute-start.44 = (bf16[512,384]{1,0:T(8,128)(2,1)S(1)}, bf16[512,384]{1,0:T(8,128)(2,1)S(1)}, u32[]{:S(2)}, u32[]{:S(2)}) collective-permute-start(bf16[512,384]{1,0:T(8,128)(2,1)S(1)} %collective-permute-done.42), channel_id=1, source_target_pairs={{0,64},{64,0},{1,65},{65,1},{2,66},{66,2},{3,67},{67,3},{4,68},{68... | collective-permute-start | bytes 1179656 | tf_op jit(solution)/shard_map/ppermute | solution.py:24
  251.3 7.1 %collective-permute-start.47 = (bf16[512,1152]{1,0:T(8,128)(2,1)}, bf16[512,1152]{1,0:T(8,128)(2,1)}, u32[]{:S(2)}, u32[]{:S(2)}) collective-permute-start(bf16[512,1152]{1,0:T(8,128)(2,1)} %maximum_maximum_fusion.refs_5_), channel_id=1, source_target_pairs={{0,2},{2,0},{4,6},{6,4},{1,3},{3,1},{5,7},{7,5},{8,10},{10,8},{12,... | collective-permute-start | bytes 3538952 | tf_op jit(solution)/shard_map/ppermute | solution.py:24
  258.4 6.1 %collective-permute-start.48 = (bf16[512,1152]{1,0:T(8,128)(2,1)}, bf16[512,1152]{1,0:T(8,128)(2,1)}, u32[]{:S(2)}, u32[]{:S(2)}) collective-permute-start(bf16[512,1152]{1,0:T(8,128)(2,1)} %maximum_maximum_fusion.refs_5_), channel_id=1, source_target_pairs={{0,6},{2,4},{4,2},{6,0},{1,7},{3,5},{5,3},{7,1},{8,14},{10,12},{12... | collective-permute-start | bytes 3538952 | tf_op jit(solution)/shard_map/ppermute | solution.py:24
  266.0 7.1 %collective-permute-start.46 = (bf16[1024,384]{1,0:T(8,128)(2,1)S(1)}, bf16[1024,384]{1,0:T(8,128)(2,1)S(1)}, u32[]{:S(2)}, u32[]{:S(2)}) collective-permute-start(bf16[1024,384]{1,0:T(8,128)(2,1)S(1)} %constant_dynamic-update-slice_fusion.9.refs_0_), channel_id=1, source_target_pairs={{0,48},{16,32},{32,16},{48,0},{1,49},{17,33},{33,17},{49,1},{2,50}... | collective-permute-start | bytes 2359304 | tf_op jit(solution)/shard_map/ppermute | solution.py:24
  273.1 9.2 %collective-permute-done.47.refs_6_ = bf16[512,1152]{1,0:T(8,128)(2,1)} collective-permute-done((bf16[512,1152]{1,0:T(8,128)(2,1)}, bf16[512,1152]{1,0:T(8,128)(2,1)}, u32[]{:S(2)}, u32[]{:S(2)}) %collective-permute-start.47) | collective-permute-done | bytes 1179680 | tf_op jit(solution)/shard_map/ppermute | solution.py:24
  283.4 6.0 %collective-permute-done.48.refs_9_ = bf16[512,1152]{1,0:T(8,128)(2,1)} collective-permute-done((bf16[512,1152]{1,0:T(8,128)(2,1)}, bf16[512,1152]{1,0:T(8,128)(2,1)}, u32[]{:S(2)}, u32[]{:S(2)}) %collective-permute-start.48) | collective-permute-done | bytes 1179680 | tf_op jit(solution)/shard_map/ppermute | solution.py:24
  291.4 2.0 collective-permute-start.49
  295.0 2.8 collective-permute-start.53
  297.9 3.0 collective-permute-done.49.refs_2_
  300.8 3.4 %collective-permute-start.54 = (bf16[512,1152]{1,0:T(8,128)(2,1)}, bf16[512,1152]{1,0:T(8,128)(2,1)}, u32[]{:S(2)}, u32[]{:S(2)}) collective-permute-start(bf16[512,1152]{1,0:T(8,128)(2,1)} %collective-permute-done.47.refs_6_), channel_id=1, source_target_pairs={{0,1},{1,0},{2,3},{3,2},{4,5},{5,4},{6,7},{7,6},{8,9},{9,8},{10,11... | collective-permute-start | bytes 3538952 | tf_op jit(solution)/shard_map/ppermute | solution.py:24
  307.1 3.7 %collective-permute-start.55 = (bf16[256,1152]{1,0:T(8,128)(2,1)}, bf16[256,1152]{1,0:T(8,128)(2,1)}, u32[]{:S(2)}, u32[]{:S(2)}) collective-permute-start(bf16[256,1152]{1,0:T(8,128)(2,1)} %collective-permute-done.51.refs_7_), channel_id=1, source_target_pairs={{0,1},{1,0},{2,3},{3,2},{4,5},{5,4},{6,7},{7,6},{8,9},{9,8},{10,11... | collective-permute-start | bytes 1769480 | tf_op jit(solution)/shard_map/ppermute | solution.py:24
  313.7 11.7 %moments.1 = (f32[384,768]{1,0:T(8,128)}, f32[384,384]{1,0:T(8,128)}) custom-call(s32[2]{0:T(128)} %pad_add_fusion.place, bf16[1024,384]{1,0:T(8,128)(2,1)} %copy-done.19, bf16[1024,384]{1,0:T(8,128)(2,1)} %copy-done.17, bf16[512,384]{1,0:T(8,128)(2,1)} %copy-done.26, bf16[512,384]{1,0:T(8,128)(2,1)} %copy-done.27, bf16[1024,384]{1,0:T(8,128)(2,1)} %copy-done.18, ...), custom_call_target="tpu_custom_call" | custom-call | tf_op jit(solution)/shard_map/moments/pallas_call | solution.py:290
  (237 shorter events, 82.3 us)
Async XLA Ops:
  0.7 32.7 %collective-permute-start.3 = (bf16[3,768,256]{2,1,0:T(8,128)(2,1)}, bf16[3,768,256]{2,1,0:T(8,128)(2,1)}, u32[]{:S(2)}, u32[]{:S(2)}) collective-permute-start(bf16[3,768,256]{2,1,0:T(8,128)(2,1)} %bitcast.55), channel_id=1, source_target_pairs={{0,16},{16,0},{32,48},{48,32},{1,17},{17,1},{33,49},{49,33},{2,18}... | collective-permute-start | bytes 3538952 | tf_op jit(solution)/shard_map/ppermute | solution.py:24
  3.2 30.1 %collective-permute-start.4 = (bf16[3,768,256]{2,1,0:T(8,128)(2,1)}, bf16[3,768,256]{2,1,0:T(8,128)(2,1)}, u32[]{:S(2)}, u32[]{:S(2)}) collective-permute-start(bf16[3,768,256]{2,1,0:T(8,128)(2,1)} %bitcast.56), channel_id=1, source_target_pairs={{0,48},{16,32},{32,16},{48,0},{1,49},{17,33},{33,17},{49,1},{2,50}... | collective-permute-start | bytes 3538952 | tf_op jit(solution)/shard_map/ppermute | solution.py:24
  8.1 11.9 %collective-permute-start = (bf16[64,3072]{1,0:T(8,128)(2,1)S(1)}, bf16[64,3072]{1,0:T(8,128)(2,1)S(1)}, u32[]{:S(2)}, u32[]{:S(2)}) collective-permute-start(bf16[64,3072]{1,0:T(8,128)(2,1)S(1)} %constant_dynamic-update-slice_fusion), channel_id=1, source_target_pairs={{0,64},{64,0},{1,65},{65,1},{2,66},{66,2},{3,67},{67,3},{4,68},{68... | collective-permute-start | bytes 1179656 | tf_op jit(solution)/shard_map/ppermute | solution.py:24
  20.0 9.3 %collective-permute-start.1 = (bf16[64,3072]{1,0:T(8,128)(2,1)S(1)}, bf16[64,3072]{1,0:T(8,128)(2,1)S(1)}, u32[]{:S(2)}, u32[]{:S(2)}) collective-permute-start(bf16[64,3072]{1,0:T(8,128)(2,1)S(1)} %collective-permute-done), channel_id=1, source_target_pairs={{0,2},{2,0},{4,6},{6,4},{1,3},{3,1},{5,7},{7,5},{8,10},{10,8},{12,... | collective-permute-start | bytes 1179656 | tf_op jit(solution)/shard_map/ppermute | solution.py:24
  21.4 10.1 %collective-permute-start.2 = (bf16[64,3072]{1,0:T(8,128)(2,1)S(1)}, bf16[64,3072]{1,0:T(8,128)(2,1)S(1)}, u32[]{:S(2)}, u32[]{:S(2)}) collective-permute-start(bf16[64,3072]{1,0:T(8,128)(2,1)S(1)} %collective-permute-done), channel_id=1, source_target_pairs={{0,6},{2,4},{4,2},{6,0},{1,7},{3,5},{5,3},{7,1},{8,14},{10,12},{12... | collective-permute-start | bytes 1179656 | tf_op jit(solution)/shard_map/ppermute | solution.py:24
  23.3 10.0 %collective-permute-start.5 = (bf16[256,768]{1,0:T(8,128)(2,1)S(1)}, bf16[256,768]{1,0:T(8,128)(2,1)S(1)}, u32[]{:S(2)}, u32[]{:S(2)}) collective-permute-start(bf16[256,768]{1,0:T(8,128)(2,1)S(1)} %copy-done.28), channel_id=1, source_target_pairs={{0,64},{64,0},{1,65},{65,1},{2,66},{66,2},{3,67},{67,3},{4,68},{68... | collective-permute-start | bytes 1179656 | tf_op jit(solution)/shard_map/ppermute | solution.py:24
  34.5 13.1 %collective-permute-start.8 = (bf16[3,384,256]{2,1,0:T(8,128)(2,1)S(1)}, bf16[3,384,256]{2,1,0:T(8,128)(2,1)S(1)}, u32[]{:S(2)}, u32[]{:S(2)}) collective-permute-start(bf16[3,384,256]{2,1,0:T(8,128)(2,1)S(1)} %slice.187), channel_id=1, source_target_pairs={{0,48},{16,32},{32,16},{48,0},{1,49},{17,33},{33,17},{49,1},{2,50}... | collective-permute-start | bytes 1769480 | tf_op jit(solution)/shard_map/ppermute | solution.py:24
  36.3 11.7 %collective-permute-start.9 = (bf16[3,384,256]{2,1,0:T(8,128)(2,1)S(1)}, bf16[3,384,256]{2,1,0:T(8,128)(2,1)S(1)}, u32[]{:S(2)}, u32[]{:S(2)}) collective-permute-start(bf16[3,384,256]{2,1,0:T(8,128)(2,1)S(1)} %slice.188), channel_id=1, source_target_pairs={{0,16},{16,0},{32,48},{48,32},{1,17},{17,1},{33,49},{49,33},{2,18}... | collective-permute-start | bytes 1769480 | tf_op jit(solution)/shard_map/ppermute | solution.py:24
  36.7 9.7 %collective-permute-start.10 = (bf16[256,768]{1,0:T(8,128)(2,1)S(1)}, bf16[256,768]{1,0:T(8,128)(2,1)S(1)}, u32[]{:S(2)}, u32[]{:S(2)}) collective-permute-start(bf16[256,768]{1,0:T(8,128)(2,1)S(1)} %get-tuple-element.100), channel_id=1, source_target_pairs={{0,64},{64,0},{1,65},{65,1},{2,66},{66,2},{3,67},{67,3},{4,68},{68... | collective-permute-start | bytes 1179656 | tf_op jit(solution)/shard_map/ppermute | solution.py:24
  48.1 7.7 %collective-permute-start.13 = (bf16[256,3072]{1,0:T(8,128)(2,1)S(1)}, bf16[256,3072]{1,0:T(8,128)(2,1)S(1)}, u32[]{:S(2)}, u32[]{:S(2)}) collective-permute-start(bf16[256,3072]{1,0:T(8,128)(2,1)S(1)} %constant_dynamic-update-slice_fusion.4), channel_id=1, source_target_pairs={{0,1},{1,0},{2,3},{3,2},{4,5},{5,4},{6,7},{7,6},{8,9},{9,8},{10,11... | collective-permute-start | bytes 4718600 | tf_op jit(solution)/shard_map/ppermute | solution.py:24
  52.2 27.5 %collective-permute-start.11 = (bf16[768,768]{1,0:T(8,128)(2,1)S(1)}, bf16[768,768]{1,0:T(8,128)(2,1)S(1)}, u32[]{:S(2)}, u32[]{:S(2)}) collective-permute-start(bf16[768,768]{1,0:T(8,128)(2,1)S(1)} %copy-done.2), channel_id=1, source_target_pairs={{0,16},{16,0},{32,48},{48,32},{1,17},{17,1},{33,49},{49,33},{2,18}... | collective-permute-start | bytes 3538952 | tf_op jit(solution)/shard_map/ppermute | solution.py:24
  52.7 28.4 %collective-permute-start.12 = (bf16[768,768]{1,0:T(8,128)(2,1)S(1)}, bf16[768,768]{1,0:T(8,128)(2,1)S(1)}, u32[]{:S(2)}, u32[]{:S(2)}) collective-permute-start(bf16[768,768]{1,0:T(8,128)(2,1)S(1)} %copy-done.2), channel_id=1, source_target_pairs={{0,48},{16,32},{32,16},{48,0},{1,49},{17,33},{33,17},{49,1},{2,50}... | collective-permute-start | bytes 3538952 | tf_op jit(solution)/shard_map/ppermute | solution.py:24
  54.5 11.5 %collective-permute-start.14 = (bf16[256,768]{1,0:T(8,128)(2,1)S(1)}, bf16[256,768]{1,0:T(8,128)(2,1)S(1)}, u32[]{:S(2)}, u32[]{:S(2)}) collective-permute-start(bf16[256,768]{1,0:T(8,128)(2,1)S(1)} %get-tuple-element.111), channel_id=1, source_target_pairs={{0,64},{64,0},{1,65},{65,1},{2,66},{66,2},{3,67},{67,3},{4,68},{68... | collective-permute-start | bytes 1179656 | tf_op jit(solution)/shard_map/ppermute | solution.py:24
  66.0 19.0 %collective-permute-start.17 = (bf16[1024,384]{1,0:T(8,128)(2,1)S(1)}, bf16[1024,384]{1,0:T(8,128)(2,1)S(1)}, u32[]{:S(2)}, u32[]{:S(2)}) collective-permute-start(bf16[1024,384]{1,0:T(8,128)(2,1)S(1)} %get-tuple-element.112), channel_id=1, source_target_pairs={{0,64},{64,0},{1,65},{65,1},{2,66},{66,2},{3,67},{67,3},{4,68},{68... | collective-permute-start | bytes 2359304 | tf_op jit(solution)/shard_map/ppermute | solution.py:24
  82.2 14.9 %collective-permute-start.15 = (bf16[384,768]{1,0:T(8,128)(2,1)S(1)}, bf16[384,768]{1,0:T(8,128)(2,1)S(1)}, u32[]{:S(2)}, u32[]{:S(2)}) collective-permute-start(bf16[384,768]{1,0:T(8,128)(2,1)S(1)} %slice.198), channel_id=1, source_target_pairs={{0,48},{16,32},{32,16},{48,0},{1,49},{17,33},{33,17},{49,1},{2,50}... | collective-permute-start | bytes 1769480 | tf_op jit(solution)/shard_map/ppermute | solution.py:24
  84.0 13.4 %collective-permute-start.16 = (bf16[384,768]{1,0:T(8,128)(2,1)S(1)}, bf16[384,768]{1,0:T(8,128)(2,1)S(1)}, u32[]{:S(2)}, u32[]{:S(2)}) collective-permute-start(bf16[384,768]{1,0:T(8,128)(2,1)S(1)} %slice.199), channel_id=1, source_target_pairs={{0,16},{16,0},{32,48},{48,32},{1,17},{17,1},{33,49},{49,33},{2,18}... | collective-permute-start | bytes 1769480 | tf_op jit(solution)/shard_map/ppermute | solution.py:24
  87.2 21.9 %collective-permute-start.18 = (bf16[1024,256]{1,0:T(8,128)(2,1)S(1)}, bf16[1024,256]{1,0:T(8,128)(2,1)S(1)}, u32[]{:S(2)}, u32[]{:S(2)}) collective-permute-start(bf16[1024,256]{1,0:T(8,128)(2,1)S(1)} %pad_maximum_fusion.5.refs_0_), channel_id=1, source_target_pairs={{0,16},{16,0},{32,48},{48,32},{1,17},{17,1},{33,49},{49,33},{2,18}... | collective-permute-start | bytes 1572872 | tf_op jit(solution)/shard_map/ppermute | solution.py:24
  88.0 21.1 %collective-permute-start.19 = (bf16[1024,256]{1,0:T(8,128)(2,1)S(1)}, bf16[1024,256]{1,0:T(8,128)(2,1)S(1)}, u32[]{:S(2)}, u32[]{:S(2)}) collective-permute-start(bf16[1024,256]{1,0:T(8,128)(2,1)S(1)} %pad_maximum_fusion.5.refs_0_), channel_id=1, source_target_pairs={{0,48},{16,32},{32,16},{48,0},{1,49},{17,33},{33,17},{49,1},{2,50}... | collective-permute-start | bytes 1572872 | tf_op jit(solution)/shard_map/ppermute | solution.py:24
  102.0 16.2 %collective-permute-start.20 = (bf16[512,768]{1,0:T(8,128)(2,1)S(1)}, bf16[512,768]{1,0:T(8,128)(2,1)S(1)}, u32[]{:S(2)}, u32[]{:S(2)}) collective-permute-start(bf16[512,768]{1,0:T(8,128)(2,1)S(1)} %project_mlp.2), channel_id=1, source_target_pairs={{0,64},{64,0},{1,65},{65,1},{2,66},{66,2},{3,67},{67,3},{4,68},{68... | collective-permute-start | bytes 2359304 | tf_op jit(solution)/shard_map/ppermute | solution.py:24
  109.1 9.1 %collective-permute-start.21 = (bf16[512,256]{1,0:T(8,128)(2,1)S(1)}, bf16[512,256]{1,0:T(8,128)(2,1)S(1)}, u32[]{:S(2)}, u32[]{:S(2)}) collective-permute-start(bf16[512,256]{1,0:T(8,128)(2,1)S(1)} %slice.203), channel_id=1, source_target_pairs={{0,48},{16,32},{32,16},{48,0},{1,49},{17,33},{33,17},{49,1},{2,50}... | collective-permute-start | bytes 786440 | tf_op jit(solution)/shard_map/ppermute | solution.py:24
  123.1 13.8 %collective-permute-start.23 = (bf16[512,768]{1,0:T(8,128)(2,1)S(1)}, bf16[512,768]{1,0:T(8,128)(2,1)S(1)}, u32[]{:S(2)}, u32[]{:S(2)}) collective-permute-start(bf16[512,768]{1,0:T(8,128)(2,1)S(1)} %fusion.2.refs_4_), channel_id=1, source_target_pairs={{0,16},{16,0},{32,48},{48,32},{1,17},{17,1},{33,49},{49,33},{2,18}... | collective-permute-start | bytes 2359304 | tf_op jit(solution)/shard_map/ppermute | solution.py:24
  124.0 15.2 %collective-permute-start.24 = (bf16[512,768]{1,0:T(8,128)(2,1)S(1)}, bf16[512,768]{1,0:T(8,128)(2,1)S(1)}, u32[]{:S(2)}, u32[]{:S(2)}) collective-permute-start(bf16[512,768]{1,0:T(8,128)(2,1)S(1)} %fusion.2.refs_4_), channel_id=1, source_target_pairs={{0,48},{16,32},{32,16},{48,0},{1,49},{17,33},{33,17},{49,1},{2,50}... | collective-permute-start | bytes 2359304 | tf_op jit(solution)/shard_map/ppermute | solution.py:24
  125.3 9.4 %collective-permute-start.25 = (bf16[256,768]{1,0:T(8,128)(2,1)S(1)}, bf16[256,768]{1,0:T(8,128)(2,1)S(1)}, u32[]{:S(2)}, u32[]{:S(2)}) collective-permute-start(bf16[256,768]{1,0:T(8,128)(2,1)S(1)} %get-tuple-element.137), channel_id=1, source_target_pairs={{0,64},{64,0},{1,65},{65,1},{2,66},{66,2},{3,67},{67,3},{4,68},{68... | collective-permute-start | bytes 1179656 | tf_op jit(solution)/shard_map/ppermute | solution.py:24
  140.7 19.3 %collective-permute-start.30 = (bf16[256,768]{1,0:T(8,128)(2,1)S(1)}, bf16[256,768]{1,0:T(8,128)(2,1)}, u32[]{:S(2)}, u32[]{:S(2)}) collective-permute-start(bf16[256,768]{1,0:T(8,128)(2,1)S(1)} %slice.210), channel_id=1, source_target_pairs={{0,48},{16,32},{32,16},{48,0},{1,49},{17,33},{33,17},{49,1},{2,50}... | collective-permute-start | bytes 1179656 | tf_op jit(solution)/shard_map/ppermute | solution.py:24
  142.3 17.6 %collective-permute-start.31 = (bf16[256,768]{1,0:T(8,128)(2,1)S(1)}, bf16[256,768]{1,0:T(8,128)(2,1)}, u32[]{:S(2)}, u32[]{:S(2)}) collective-permute-start(bf16[256,768]{1,0:T(8,128)(2,1)S(1)} %slice.211), channel_id=1, source_target_pairs={{0,16},{16,0},{32,48},{48,32},{1,17},{17,1},{33,49},{49,33},{2,18}... | collective-permute-start | bytes 1179656 | tf_op jit(solution)/shard_map/ppermute | solution.py:24
  144.8 13.5 %collective-permute-start.28 = (bf16[512,256]{1,0:T(8,128)(2,1)S(1)}, bf16[512,256]{1,0:T(8,128)(2,1)S(1)}, u32[]{:S(2)}, u32[]{:S(2)}) collective-permute-start(bf16[512,256]{1,0:T(8,128)(2,1)S(1)} %pad_maximum_fusion.7.refs_0_), channel_id=1, source_target_pairs={{0,32},{16,48},{32,0},{48,16},{1,33},{17,49},{33,1},{49,17},{2,34}... | collective-permute-start | bytes 786440 | tf_op jit(solution)/shard_map/ppermute | solution.py:24
  147.5 12.4 %collective-permute-start.29 = (bf16[512,256]{1,0:T(8,128)(2,1)S(1)}, bf16[512,256]{1,0:T(8,128)(2,1)S(1)}, u32[]{:S(2)}, u32[]{:S(2)}) collective-permute-start(bf16[512,256]{1,0:T(8,128)(2,1)S(1)} %pad_maximum_fusion.7.refs_0_), channel_id=1, source_target_pairs={{0,48},{16,32},{32,16},{48,0},{1,49},{17,33},{33,17},{49,1},{2,50}... | collective-permute-start | bytes 786440 | tf_op jit(solution)/shard_map/ppermute | solution.py:24
  167.4 14.0 %collective-permute-start.32 = (bf16[2,4,256,768]{3,2,1,0:T(8,128)(2,1)}, bf16[2,4,256,768]{3,2,1,0:T(8,128)(2,1)}, u32[]{:S(2)}, u32[]{:S(2)}) collective-permute-start(bf16[2,4,256,768]{3,2,1,0:T(8,128)(2,1)} %project_out.3), channel_id=1, source_target_pairs={{0,1},{1,0},{2,3},{3,2},{4,5},{5,4},{6,7},{7,6},{8,9},{9,8},{10,11... | collective-permute-start | bytes 9437192 | tf_op jit(solution)/shard_map/ppermute | solution.py:24
  185.1 19.2 %collective-permute-start.33 = (bf16[4,128,768]{2,1,0:T(8,128)(2,1)S(1)}, bf16[4,128,768]{2,1,0:T(8,128)(2,1)S(1)}, u32[]{:S(2)}, u32[]{:S(2)}) collective-permute-start(bf16[4,128,768]{2,1,0:T(8,128)(2,1)S(1)} %slice.351), channel_id=1, source_target_pairs={{0,2},{2,0},{4,6},{6,4},{1,3},{3,1},{5,7},{7,5},{8,10},{10,8},{12,... | collective-permute-start | bytes 2359304 | tf_op jit(solution)/shard_map/ppermute | solution.py:24
  186.0 20.1 %collective-permute-start.34 = (bf16[4,128,768]{2,1,0:T(8,128)(2,1)S(1)}, bf16[4,128,768]{2,1,0:T(8,128)(2,1)S(1)}, u32[]{:S(2)}, u32[]{:S(2)}) collective-permute-start(bf16[4,128,768]{2,1,0:T(8,128)(2,1)S(1)} %slice.350), channel_id=1, source_target_pairs={{0,6},{2,4},{4,2},{6,0},{1,7},{3,5},{5,3},{7,1},{8,14},{10,12},{12... | collective-permute-start | bytes 2359304 | tf_op jit(solution)/shard_map/ppermute | solution.py:24
  207.1 9.8 %collective-permute-start.36 = (bf16[4,64,768]{2,1,0:T(8,128)(2,1)}, bf16[4,64,768]{2,1,0:T(8,128)(2,1)}, u32[]{:S(2)}, u32[]{:S(2)}) collective-permute-start(bf16[4,64,768]{2,1,0:T(8,128)(2,1)} %fusion.12), channel_id=1, source_target_pairs={{0,2},{2,0},{4,6},{6,4},{1,3},{3,1},{5,7},{7,5},{8,10},{10,8},{12,... | collective-permute-start | bytes 1179656 | tf_op jit(solution)/shard_map/ppermute | solution.py:24
  207.9 11.0 %collective-permute-start.35 = (bf16[4,64,768]{2,1,0:T(8,128)(2,1)}, bf16[4,64,768]{2,1,0:T(8,128)(2,1)}, u32[]{:S(2)}, u32[]{:S(2)}) collective-permute-start(bf16[4,64,768]{2,1,0:T(8,128)(2,1)} %fusion.13), channel_id=1, source_target_pairs={{0,6},{2,4},{4,2},{6,0},{1,7},{3,5},{5,3},{7,1},{8,14},{10,12},{12... | collective-permute-start | bytes 1179656 | tf_op jit(solution)/shard_map/ppermute | solution.py:24
  222.0 10.6 %collective-permute-start.40 = (bf16[4,32,768]{2,1,0:T(8,128)(2,1)S(1)}, bf16[4,32,768]{2,1,0:T(8,128)(2,1)S(1)}, u32[]{:S(2)}, u32[]{:S(2)}) collective-permute-start(bf16[4,32,768]{2,1,0:T(8,128)(2,1)S(1)} %get-tuple-element.206), channel_id=1, source_target_pairs={{0,72},{8,64},{64,8},{72,0},{1,73},{9,65},{65,9},{73,1},{2,74},{10... | collective-permute-start | bytes 589832 | tf_op jit(solution)/shard_map/ppermute | solution.py:437
  224.7 8.1 %collective-permute-start.38 = (bf16[4,32,768]{2,1,0:T(8,128)(2,1)S(1)}, bf16[4,32,768]{2,1,0:T(8,128)(2,1)S(1)}, u32[]{:S(2)}, u32[]{:S(2)}) collective-permute-start(bf16[4,32,768]{2,1,0:T(8,128)(2,1)S(1)} %slice.353), channel_id=1, source_target_pairs={{0,8},{8,0},{1,9},{9,1},{2,10},{10,2},{3,11},{11,3},{4,12},{12,4},... | collective-permute-start | bytes 589832 | tf_op jit(solution)/shard_map/ppermute | solution.py:24
  235.1 10.7 %collective-permute-start.43 = (bf16[256,768]{1,0:T(8,128)(2,1)S(1)}, bf16[256,768]{1,0:T(8,128)(2,1)S(1)}, u32[]{:S(2)}, u32[]{:S(2)}) collective-permute-start(bf16[256,768]{1,0:T(8,128)(2,1)S(1)} %fusion.16), channel_id=1, source_target_pairs={{0,8},{8,0},{1,9},{9,1},{2,10},{10,2},{3,11},{11,3},{4,12},{12,4},... | collective-permute-start | bytes 1179656 | tf_op jit(solution)/shard_map/ppermute | solution.py:24
  236.2 9.6 %collective-permute-start.42 = (bf16[512,384]{1,0:T(8,128)(2,1)S(1)}, bf16[512,384]{1,0:T(8,128)(2,1)S(1)}, u32[]{:S(2)}, u32[]{:S(2)}) collective-permute-start(bf16[512,384]{1,0:T(8,128)(2,1)S(1)} %pad_maximum_fusion.6), channel_id=1, source_target_pairs={{0,0},{2,16},{4,32},{6,48},{8,64},{10,80},{12,96},{14,112},{16,2},... | collective-permute-start | bytes 1179656 | tf_op jit(solution)/shard_map/ppermute | solution.py:451
  245.8 18.8 %collective-permute-start.44 = (bf16[512,384]{1,0:T(8,128)(2,1)S(1)}, bf16[512,384]{1,0:T(8,128)(2,1)S(1)}, u32[]{:S(2)}, u32[]{:S(2)}) collective-permute-start(bf16[512,384]{1,0:T(8,128)(2,1)S(1)} %collective-permute-done.42), channel_id=1, source_target_pairs={{0,64},{64,0},{1,65},{65,1},{2,66},{66,2},{3,67},{67,3},{4,68},{68... | collective-permute-start | bytes 1179656 | tf_op jit(solution)/shard_map/ppermute | solution.py:24
  251.3 30.9 %collective-permute-start.47 = (bf16[512,1152]{1,0:T(8,128)(2,1)}, bf16[512,1152]{1,0:T(8,128)(2,1)}, u32[]{:S(2)}, u32[]{:S(2)}) collective-permute-start(bf16[512,1152]{1,0:T(8,128)(2,1)} %maximum_maximum_fusion.refs_5_), channel_id=1, source_target_pairs={{0,2},{2,0},{4,6},{6,4},{1,3},{3,1},{5,7},{7,5},{8,10},{10,8},{12,... | collective-permute-start | bytes 3538952 | tf_op jit(solution)/shard_map/ppermute | solution.py:24
  258.4 31.0 %collective-permute-start.48 = (bf16[512,1152]{1,0:T(8,128)(2,1)}, bf16[512,1152]{1,0:T(8,128)(2,1)}, u32[]{:S(2)}, u32[]{:S(2)}) collective-permute-start(bf16[512,1152]{1,0:T(8,128)(2,1)} %maximum_maximum_fusion.refs_5_), channel_id=1, source_target_pairs={{0,6},{2,4},{4,2},{6,0},{1,7},{3,5},{5,3},{7,1},{8,14},{10,12},{12... | collective-permute-start | bytes 3538952 | tf_op jit(solution)/shard_map/ppermute | solution.py:24
  264.7 25.8 %collective-permute-start.45 = (bf16[1024,384]{1,0:T(8,128)(2,1)S(1)}, bf16[1024,384]{1,0:T(8,128)(2,1)S(1)}, u32[]{:S(2)}, u32[]{:S(2)}) collective-permute-start(bf16[1024,384]{1,0:T(8,128)(2,1)S(1)} %constant_dynamic-update-slice_fusion.9.refs_0_), channel_id=1, source_target_pairs={{0,16},{16,0},{32,48},{48,32},{1,17},{17,1},{33,49},{49,33},{2,18}... | collective-permute-start | bytes 2359304 | tf_op jit(solution)/shard_map/ppermute | solution.py:24
  266.0 24.5 %collective-permute-start.46 = (bf16[1024,384]{1,0:T(8,128)(2,1)S(1)}, bf16[1024,384]{1,0:T(8,128)(2,1)S(1)}, u32[]{:S(2)}, u32[]{:S(2)}) collective-permute-start(bf16[1024,384]{1,0:T(8,128)(2,1)S(1)} %constant_dynamic-update-slice_fusion.9.refs_0_), channel_id=1, source_target_pairs={{0,48},{16,32},{32,16},{48,0},{1,49},{17,33},{33,17},{49,1},{2,50}... | collective-permute-start | bytes 2359304 | tf_op jit(solution)/shard_map/ppermute | solution.py:24
  291.4 9.5 %collective-permute-start.49 = (bf16[512,384]{1,0:T(8,128)(2,1)S(1)}, bf16[512,384]{1,0:T(8,128)(2,1)S(1)}, u32[]{:S(2)}, u32[]{:S(2)}) collective-permute-start(bf16[512,384]{1,0:T(8,128)(2,1)S(1)} %slice.242), channel_id=1, source_target_pairs={{0,48},{16,32},{32,16},{48,0},{1,49},{17,33},{33,17},{49,1},{2,50}... | collective-permute-start | bytes 1179656 | tf_op jit(solution)/shard_map/ppermute | solution.py:24
  293.4 10.8 %collective-permute-start.50 = (bf16[512,384]{1,0:T(8,128)(2,1)S(1)}, bf16[512,384]{1,0:T(8,128)(2,1)S(1)}, u32[]{:S(2)}, u32[]{:S(2)}) collective-permute-start(bf16[512,384]{1,0:T(8,128)(2,1)S(1)} %slice.243), channel_id=1, source_target_pairs={{0,16},{16,0},{32,48},{48,32},{1,17},{17,1},{33,49},{49,33},{2,18}... | collective-permute-start | bytes 1179656 | tf_op jit(solution)/shard_map/ppermute | solution.py:24
  293.5 13.4 %collective-permute-start.51 = (bf16[256,1152]{1,0:T(8,128)(2,1)S(1)}, bf16[256,1152]{1,0:T(8,128)(2,1)}, u32[]{:S(2)}, u32[]{:S(2)}) collective-permute-start(bf16[256,1152]{1,0:T(8,128)(2,1)S(1)} %slice.275), channel_id=1, source_target_pairs={{0,6},{2,4},{4,2},{6,0},{1,7},{3,5},{5,3},{7,1},{8,14},{10,12},{12... | collective-permute-start | bytes 1769480 | tf_op jit(solution)/shard_map/ppermute | solution.py:24
  295.0 12.1 %collective-permute-start.52 = (bf16[256,1152]{1,0:T(8,128)(2,1)S(1)}, bf16[256,1152]{1,0:T(8,128)(2,1)}, u32[]{:S(2)}, u32[]{:S(2)}) collective-permute-start(bf16[256,1152]{1,0:T(8,128)(2,1)S(1)} %slice.276), channel_id=1, source_target_pairs={{0,2},{2,0},{4,6},{6,4},{1,3},{3,1},{5,7},{7,5},{8,10},{10,8},{12,... | collective-permute-start | bytes 1769480 | tf_op jit(solution)/shard_map/ppermute | solution.py:24
  295.0 16.5 %collective-permute-start.53 = (bf16[512,1152]{1,0:T(8,128)(2,1)}, bf16[512,1152]{1,0:T(8,128)(2,1)}, u32[]{:S(2)}, u32[]{:S(2)}) collective-permute-start(bf16[512,1152]{1,0:T(8,128)(2,1)} %maximum_maximum_fusion.refs_5_), channel_id=1, source_target_pairs={{0,1},{1,0},{2,3},{3,2},{4,5},{5,4},{6,7},{7,6},{8,9},{9,8},{10,11... | collective-permute-start | bytes 3538952 | tf_op jit(solution)/shard_map/ppermute | solution.py:24
  300.8 12.9 %collective-permute-start.54 = (bf16[512,1152]{1,0:T(8,128)(2,1)}, bf16[512,1152]{1,0:T(8,128)(2,1)}, u32[]{:S(2)}, u32[]{:S(2)}) collective-permute-start(bf16[512,1152]{1,0:T(8,128)(2,1)} %collective-permute-done.47.refs_6_), channel_id=1, source_target_pairs={{0,1},{1,0},{2,3},{3,2},{4,5},{5,4},{6,7},{7,6},{8,9},{9,8},{10,11... | collective-permute-start | bytes 3538952 | tf_op jit(solution)/shard_map/ppermute | solution.py:24
  304.2 9.5 %collective-permute-start.57 = (bf16[512,1152]{1,0:T(8,128)(2,1)}, bf16[512,1152]{1,0:T(8,128)(2,1)}, u32[]{:S(2)}, u32[]{:S(2)}) collective-permute-start(bf16[512,1152]{1,0:T(8,128)(2,1)} %collective-permute-done.48.refs_9_), channel_id=1, source_target_pairs={{0,1},{1,0},{2,3},{3,2},{4,5},{5,4},{6,7},{7,6},{8,9},{9,8},{10,11... | collective-permute-start | bytes 3538952 | tf_op jit(solution)/shard_map/ppermute | solution.py:24
  (44 other events, 528.8 us)

commit v3 on v2

--- a/solution.py
+++ b/solution.py
@@ -377,7 +377,11 @@
     kv_one, kv_three = near(own_kv, "z")
 
     in_ws = (in_weight, in_w1, in_low, in_high, in_w3)
-    mlp_give = project_mlp(norm_far, in_ws, BF)
+    early = dot(norm_far[0], in_weight) + dot(norm_far[1], in_w1) + dot(norm_far[3], in_w3)
+    early, in_low, in_high = lax.optimization_barrier((early, in_low, in_high))
+    in_ws = (in_weight, in_w1, in_low, in_high, in_w3)
+    mlp_give = early + dot(norm_far[2][:, :middle], in_low) + dot(norm_far[2][:, middle:], in_high)
+    mlp_give = mlp_give.astype(BF)
     mlp_far = swap(mlp_give, "xh")
     mlp_give, *norm_own = lax.optimization_barrier((mlp_give, *norm_own))
     mlp_own = project_mlp(norm_own, in_ws, F32)

time: 326 us -> 329 us (level)
  Pallas kernels: 58.3 us -> 53.7 us
  waiting for transfers between devices: 112 us -> 116 us
  matrix products: 0 us -> 3.46 us
    pallas_call x2 -> x1, Pallas kernels: 10 us -> 5.44 us  [project_mlp(): pl.pallas_call(mlp_kernel, grid=(3,), in_specs=[pl.BlockSpec(x.shape, lam...]
    ppermute x56, waiting for transfers between devices: 106 us -> 110 us  [swap(): return lax.ppermute(x, axis, [(i, i ^ mask) for i in range(size)])]
    dot_general x0 -> x5, matrix products: none -> 3.46 us  [dot(): return jnp.dot(a, b, preferred_element_type=F32)]
    unnamed x83 -> x75, local copies, waits for them, and re-layouts: 6.9 us -> 5.29 us
  transfers between devices with their start and end apart: 58 -> 58, of which waited for: 36 -> 37; matrix products, arithmetic and copies ran while one was open for 5% -> 5% of each run, Pallas kernels for 12% -> 11%
where the time goes in v3:
time: 329 us; the launch traced here: 328 us
  waiting for transfers between devices  116 us (35%)
  starting transfers between devices  105 us (32%)
  Pallas kernels  53.7 us (16%)
  other arithmetic  19.6 us (6%)
  local copies, waits for them, and re-layouts  14.5 us (4%)
  blocking collectives  14.1 us (4%)
  matrix products  3.46 us (1%)
    ppermute x56, waiting for transfers between devices, swap(): return lax.ppermute(x, axis, [(i, i ^ mask) for i in range(size)])  110 us
    ppermute x56, starting transfers between devices, swap(): return lax.ppermute(x, axis, [(i, i ^ mask) for i in range(size)])  102 us
    all_to_all x1, blocking collectives, on_device(): lax.all_to_all(spread_rows, ('xh', 'z'), split_axis=0, concat_axis=0, til...  14.1 us
    pallas_call x2, Pallas kernels, project_out(): pl.pallas_call(output_kernel, grid_spec=pltpu.PrefetchScalarGridSpec(num_...  13.6 us
    pallas_call x1, Pallas kernels, moments(): pl.pallas_call(kernel, grid_spec=pltpu.PrefetchScalarGridSpec(num_scalar_...  11.7 us
    pallas_call x1, Pallas kernels, attend(): pl.pallas_call(attend_kernel, grid=(rows // step,), in_specs=[pl.BlockSpe...  7.98 us
    pallas_call x2, Pallas kernels, norm_rows(): pl.pallas_call(norm_kernel, grid_spec=pltpu.PrefetchScalarGridSpec(num_sc...  7.6 us
    pallas_call x1, Pallas kernels, project_qkv(): pl.pallas_call(qkv_kernel, grid_spec=pltpu.PrefetchScalarGridSpec(num_sca...  7.4 us
  transfers between devices with their start and end apart: 58, of which 37 were waited for; matrix products, arithmetic and copies ran while one was open for 5% of the time, Pallas kernels for 11%

profile of v3, /device:TPU:1, one launch (start us, length us, event | category | flops | bytes accessed | tf_op | source)
XLA Modules:
  0.0 328.1 jit_solution(4012809411030807808)
XLA Ops:
  0.7 2.5 collective-permute-start.3
  3.2 2.2 collective-permute-start.4
  8.1 2.8 collective-permute-start
  10.9 2.8 copy-done.1
  13.7 6.3 %norm_rows.3 = (bf16[512,768]{1,0:T(8,128)(2,1)S(1)}, bf16[512,768]{1,0:T(8,128)(2,1)S(1)}, bf16[512,768]{1,0:T(8,128)(2,1)S(1)}, bf16[512,768]{1,0:T(8,128)(2,1)S(1)}) custom-call(s32[3]{0:T(128)S(1)} %get-tuple-element.218.place, bf16[512,6144]{1,0:T(8,128)(2,1)S(1)} %copy-done.1, f32[1,6144]{1,0:T(1,128)S(1)} %bitcast.67), custom_call_target="tpu_custom_call" | custom-call | tf_op jit(solution)/shard_map/norm_rows/pallas_call | solution.py:83
  25.2 4.1 %collective-permute-done.1 = bf16[64,3072]{1,0:T(8,128)(2,1)S(1)} collective-permute-done((bf16[64,3072]{1,0:T(8,128)(2,1)S(1)}, bf16[64,3072]{1,0:T(8,128)(2,1)S(1)}, u32[]{:S(2)}, u32[]{:S(2)}) %collective-permute-start.1) | collective-permute-done | bytes 393248 | tf_op jit(solution)/shard_map/ppermute | solution.py:24
  29.3 2.2 collective-permute-done.2
  38.8 2.8 collective-permute-start.6
  41.7 3.2 collective-permute-done.6
  48.1 4.2 %collective-permute-start.13 = (bf16[256,3072]{1,0:T(8,128)(2,1)S(1)}, bf16[256,3072]{1,0:T(8,128)(2,1)S(1)}, u32[]{:S(2)}, u32[]{:S(2)}) collective-permute-start(bf16[256,3072]{1,0:T(8,128)(2,1)S(1)} %constant_dynamic-update-slice_fusion.4), channel_id=1, source_target_pairs={{0,1},{1,0},{2,3},{3,2},{4,5},{5,4},{6,7},{7,6},{8,9},{9,8},{10,11... | collective-permute-start | bytes 4718600 | tf_op jit(solution)/shard_map/ppermute | solution.py:24
  57.3 7.4 %project_qkv.1 = (bf16[1024,384]{1,0:T(8,128)(2,1)S(1)}, f32[1024,384]{1,0:T(8,128)S(1)}) custom-call(s32[1]{0:T(128)} %bitcast.2.place, bf16[512,768]{1,0:T(8,128)(2,1)S(1)} %get-tuple-element.129.refs_0_, bf16[512,768]{1,0:T(8,128)(2,1)S(1)} %get-tuple-element.130.refs_1_, bf16[512,768]{1,0:T(8,128)(2,1)S(1)} %get-tuple-element.131.refs_2_, ...), custom_call_target="tpu_custom_call" | custom-call | tf_op jit(solution)/shard_map/project_qkv/pallas_call | solution.py:168
  67.2 12.6 %collective-permute-done.11.refs_5_ = bf16[768,768]{1,0:T(8,128)(2,1)S(1)} collective-permute-done((bf16[768,768]{1,0:T(8,128)(2,1)S(1)}, bf16[768,768]{1,0:T(8,128)(2,1)S(1)}, u32[]{:S(2)}, u32[]{:S(2)}) %collective-permute-start.11) | collective-permute-done | bytes 1179680 | tf_op jit(solution)/shard_map/ppermute | solution.py:24
  85.4 11.5 %collective-permute-done.15.refs_6_ = bf16[384,768]{1,0:T(8,128)(2,1)S(1)} collective-permute-done((bf16[384,768]{1,0:T(8,128)(2,1)S(1)}, bf16[384,768]{1,0:T(8,128)(2,1)S(1)}, u32[]{:S(2)}, u32[]{:S(2)}) %collective-permute-start.15) | collective-permute-done | bytes 589856 | tf_op jit(solution)/shard_map/ppermute | solution.py:24
  103.7 5.4 %project_mlp.1 = f32[512,768]{1,0:T(8,128)} custom-call(bf16[512,768]{1,0:T(8,128)(2,1)S(1)} %get-tuple-element.129.refs_0_, bf16[512,768]{1,0:T(8,128)(2,1)S(1)} %get-tuple-element.130.refs_1_, bf16[512,768]{1,0:T(8,128)(2,1)S(1)} %get-tuple-element.131.refs_2_, bf16[512,768]{1,0:T(8,128)(2,1)S(1)} %get-tuple-element.132.refs_3_, ...), custom_call_target="tpu_custom_call" | custom-call | tf_op jit(solution)/shard_map/project_mlp/pallas_call | solution.py:194
  114.5 6.1 %collective-permute-done.20 = bf16[512,768]{1,0:T(8,128)(2,1)S(1)} collective-permute-done((bf16[512,768]{1,0:T(8,128)(2,1)S(1)}, bf16[512,768]{1,0:T(8,128)(2,1)S(1)}, u32[]{:S(2)}, u32[]{:S(2)}) %collective-permute-start.20) | collective-permute-done | bytes 786464 | tf_op jit(solution)/shard_map/ppermute | solution.py:24
  120.6 4.7 %fusion.2.refs_4_ = bf16[512,768]{1,0:T(8,128)(2,1)S(1)} fusion(f32[512,768]{1,0:T(8,128)} %project_mlp.1, bf16[512,768]{1,0:T(8,128)(2,1)S(1)} %collective-permute-done.20, f32[768]{0:T(1024)S(1)} %copy-done.27), kind=kLoop, calls=%fused_computation.6 | loop fusion | flops 26738688 | bytes 3148800 | tf_op jit(solution)/shard_map/convert_element_type | solution.py:393
  128.5 8.0 %attend.1 = bf16[1024,128]{1,0:T(8,128)(2,1)S(1)} custom-call(bf16[1024,128]{1,0:T(8,128)(2,1)S(1)} %get-tuple-element.139.q_ref, bf16[1024,256]{1,0:T(8,128)(2,1)S(1)} %pad_maximum_fusion.5.refs_0_, bf16[1024,256]{1,0:T(8,128)(2,1)S(1)} %collective-permute-done.18.refs_1_, bf16[1024,256]{1,0:T(8,128)(2,1)S(1)} %collective-permute-done.19.refs_2_, ...), custom_call_target="tpu_custom_call" | custom-call | tf_op jit(solution)/shard_map/attend/pallas_call | solution.py:121
  136.5 4.4 %collective-permute-done.23.refs_5_ = bf16[512,768]{1,0:T(8,128)(2,1)S(1)} collective-permute-done((bf16[512,768]{1,0:T(8,128)(2,1)S(1)}, bf16[512,768]{1,0:T(8,128)(2,1)S(1)}, u32[]{:S(2)}, u32[]{:S(2)}) %collective-permute-start.23) | collective-permute-done | bytes 786464 | tf_op jit(solution)/shard_map/ppermute | solution.py:24
  143.0 2.1 collective-permute-start.30
  145.3 2.2 collective-permute-done.26
  149.4 2.0 collective-permute-start.29
  153.5 2.8 collective-permute-done.27.refs_1_
  156.3 5.3 %collective-permute-done.28.refs_2_ = bf16[512,256]{1,0:T(8,128)(2,1)S(1)} collective-permute-done((bf16[512,256]{1,0:T(8,128)(2,1)S(1)}, bf16[512,256]{1,0:T(8,128)(2,1)S(1)}, u32[]{:S(2)}, u32[]{:S(2)}) %collective-permute-start.28) | collective-permute-done | bytes 262176 | tf_op jit(solution)/shard_map/ppermute | solution.py:24
  162.4 6.8 %project_out.3 = bf16[2,4,256,768]{3,2,1,0:T(8,128)(2,1)} custom-call(s32[1]{0:T(128)} %bitcast.2.place, bf16[512,256]{1,0:T(8,128)(2,1)} %copy-done.13, bf16[512,256]{1,0:T(8,128)(2,1)} %copy-done.18, bf16[512,256]{1,0:T(8,128)(2,1)} %copy-done.19, bf16[512,256]{1,0:T(8,128)(2,1)} %copy-done.20, bf16[512,768]{1,0:T(8,128)(2,1)} %copy-done.8, ...), custom_call_target="tpu_custom_call" | custom-call | tf_op jit(solution)/shard_map/project_out/pallas_call | solution.py:225
  169.1 7.0 %collective-permute-start.32 = (bf16[2,4,256,768]{3,2,1,0:T(8,128)(2,1)}, bf16[2,4,256,768]{3,2,1,0:T(8,128)(2,1)}, u32[]{:S(2)}, u32[]{:S(2)}) collective-permute-start(bf16[2,4,256,768]{3,2,1,0:T(8,128)(2,1)} %project_out.3), channel_id=1, source_target_pairs={{0,1},{1,0},{2,3},{3,2},{4,5},{5,4},{6,7},{7,6},{8,9},{9,8},{10,11... | collective-permute-start | bytes 9437192 | tf_op jit(solution)/shard_map/ppermute | solution.py:24
  176.2 6.8 %project_out.2 = bf16[2,4,256,768]{3,2,1,0:T(8,128)(2,1)} custom-call(s32[1]{0:T(128)} %bitcast.2.place, bf16[512,256]{1,0:T(8,128)(2,1)} %copy-done.13, bf16[512,256]{1,0:T(8,128)(2,1)} %copy-done.18, bf16[512,256]{1,0:T(8,128)(2,1)} %copy-done.19, bf16[512,256]{1,0:T(8,128)(2,1)} %copy-done.20, bf16[512,768]{1,0:T(8,128)(2,1)} %copy-done.8, ...), custom_call_target="tpu_custom_call" | custom-call | tf_op jit(solution)/shard_map/project_out/pallas_call | solution.py:225
  183.0 3.5 %add_bitcast_fusion = (f32[4,256,768]{2,1,0:T(8,128)S(1)}, f32[4,256,768]{2,1,0:T(8,128)S(1)}) fusion(bf16[2,4,256,768]{3,2,1,0:T(8,128)(2,1)} %project_out.2, bf16[2,4,256,768]{3,2,1,0:T(8,128)(2,1)} %collective-permute-done.32), kind=kLoop, calls=%fused_computation.1 | loop fusion | flops 4718592 | bytes 12582912 | tf_op jit(solution)/shard_map/add | solution.py:420
  187.9 2.1 collective-permute-start.34
  191.2 14.1 %all_to_all.5 = bf16[8,32,1152]{2,1,0:T(8,128)(2,1)S(1)} all-to-all(bf16[8,32,1152]{2,1,0:T(8,128)(2,1)S(1)} %copy.14), channel_id=1, replica_groups=mesh['xh'=2,'z'=4,'xl'=2,'y'=4,'c'=2] {'xh','z'}, dimensions={0} | all-to-all | bytes 1179648 | tf_op jit(solution)/shard_map/all_to_all | solution.py:418
  205.8 2.1 collective-permute-done.34
  209.8 2.0 collective-permute-start.35
  213.1 3.8 %collective-permute-done.37 = bf16[256,384]{1,0:T(8,128)(2,1)S(1)} collective-permute-done((bf16[256,384]{1,0:T(8,128)(2,1)S(1)}, bf16[256,384]{1,0:T(8,128)(2,1)S(1)}, u32[]{:S(2)}, u32[]{:S(2)}) %collective-permute-start.37) | collective-permute-done | bytes 196640 | tf_op jit(solution)/shard_map/ppermute | solution.py:24
  218.7 2.1 collective-permute-done.35
  228.6 5.9 %collective-permute-done.40 = bf16[4,32,768]{2,1,0:T(8,128)(2,1)S(1)} collective-permute-done((bf16[4,32,768]{2,1,0:T(8,128)(2,1)S(1)}, bf16[4,32,768]{2,1,0:T(8,128)(2,1)S(1)}, u32[]{:S(2)}, u32[]{:S(2)}) %collective-permute-start.40) | collective-permute-done | bytes 196640 | tf_op jit(solution)/shard_map/ppermute | solution.py:441
  238.9 8.9 %collective-permute-done.43 = bf16[256,768]{1,0:T(8,128)(2,1)S(1)} collective-permute-done((bf16[256,768]{1,0:T(8,128)(2,1)S(1)}, bf16[256,768]{1,0:T(8,128)(2,1)S(1)}, u32[]{:S(2)}, u32[]{:S(2)}) %collective-permute-start.43) | collective-permute-done | bytes 393248 | tf_op jit(solution)/shard_map/ppermute | solution.py:24
  247.7 3.9 %collective-permute-start.44 = (bf16[512,384]{1,0:T(8,128)(2,1)S(1)}, bf16[512,384]{1,0:T(8,128)(2,1)S(1)}, u32[]{:S(2)}, u32[]{:S(2)}) collective-permute-start(bf16[512,384]{1,0:T(8,128)(2,1)S(1)} %collective-permute-done.42), channel_id=1, source_target_pairs={{0,64},{64,0},{1,65},{65,1},{2,66},{66,2},{3,67},{67,3},{4,68},{68... | collective-permute-start | bytes 1179656 | tf_op jit(solution)/shard_map/ppermute | solution.py:24
  252.7 7.0 %collective-permute-start.47 = (bf16[512,1152]{1,0:T(8,128)(2,1)}, bf16[512,1152]{1,0:T(8,128)(2,1)}, u32[]{:S(2)}, u32[]{:S(2)}) collective-permute-start(bf16[512,1152]{1,0:T(8,128)(2,1)} %maximum_maximum_fusion.refs_5_), channel_id=1, source_target_pairs={{0,2},{2,0},{4,6},{6,4},{1,3},{3,1},{5,7},{7,5},{8,10},{10,8},{12,... | collective-permute-start | bytes 3538952 | tf_op jit(solution)/shard_map/ppermute | solution.py:24
  259.7 6.6 %collective-permute-start.48 = (bf16[512,1152]{1,0:T(8,128)(2,1)}, bf16[512,1152]{1,0:T(8,128)(2,1)}, u32[]{:S(2)}, u32[]{:S(2)}) collective-permute-start(bf16[512,1152]{1,0:T(8,128)(2,1)} %maximum_maximum_fusion.refs_5_), channel_id=1, source_target_pairs={{0,6},{2,4},{4,2},{6,0},{1,7},{3,5},{5,3},{7,1},{8,14},{10,12},{12... | collective-permute-start | bytes 3538952 | tf_op jit(solution)/shard_map/ppermute | solution.py:24
  266.5 9.7 %collective-permute-start.46 = (bf16[1024,384]{1,0:T(8,128)(2,1)S(1)}, bf16[1024,384]{1,0:T(8,128)(2,1)S(1)}, u32[]{:S(2)}, u32[]{:S(2)}) collective-permute-start(bf16[1024,384]{1,0:T(8,128)(2,1)S(1)} %constant_dynamic-update-slice_fusion.9.refs_0_), channel_id=1, source_target_pairs={{0,48},{16,32},{32,16},{48,0},{1,49},{17,33},{33,17},{49,1},{2,50}... | collective-permute-start | bytes 2359304 | tf_op jit(solution)/shard_map/ppermute | solution.py:24
  276.2 7.4 %collective-permute-done.47.refs_6_ = bf16[512,1152]{1,0:T(8,128)(2,1)} collective-permute-done((bf16[512,1152]{1,0:T(8,128)(2,1)}, bf16[512,1152]{1,0:T(8,128)(2,1)}, u32[]{:S(2)}, u32[]{:S(2)}) %collective-permute-start.47) | collective-permute-done | bytes 1179680 | tf_op jit(solution)/shard_map/ppermute | solution.py:24
  284.7 6.4 %collective-permute-done.48.refs_9_ = bf16[512,1152]{1,0:T(8,128)(2,1)} collective-permute-done((bf16[512,1152]{1,0:T(8,128)(2,1)}, bf16[512,1152]{1,0:T(8,128)(2,1)}, u32[]{:S(2)}, u32[]{:S(2)}) %collective-permute-start.48) | collective-permute-done | bytes 1179680 | tf_op jit(solution)/shard_map/ppermute | solution.py:24
  293.1 3.0 collective-permute-start.49
  296.8 3.1 collective-permute-start.53
  299.9 3.1 collective-permute-done.49.refs_2_
  303.0 3.2 collective-permute-start.54
  307.8 2.0 collective-permute-done.51.refs_7_
  309.7 3.6 %collective-permute-start.55 = (bf16[256,1152]{1,0:T(8,128)(2,1)}, bf16[256,1152]{1,0:T(8,128)(2,1)}, u32[]{:S(2)}, u32[]{:S(2)}) collective-permute-start(bf16[256,1152]{1,0:T(8,128)(2,1)} %collective-permute-done.51.refs_7_), channel_id=1, source_target_pairs={{0,1},{1,0},{2,3},{3,2},{4,5},{5,4},{6,7},{7,6},{8,9},{9,8},{10,11... | collective-permute-start | bytes 1769480 | tf_op jit(solution)/shard_map/ppermute | solution.py:24
  316.2 11.7 %moments.1 = (f32[384,768]{1,0:T(8,128)}, f32[384,384]{1,0:T(8,128)}) custom-call(s32[2]{0:T(128)} %pad_add_fusion.place, bf16[1024,384]{1,0:T(8,128)(2,1)} %copy-done.17, bf16[1024,384]{1,0:T(8,128)(2,1)} %copy-done.15, bf16[512,384]{1,0:T(8,128)(2,1)} %copy-done.24, bf16[512,384]{1,0:T(8,128)(2,1)} %copy-done.25, bf16[1024,384]{1,0:T(8,128)(2,1)} %copy-done.16, ...), custom_call_target="tpu_custom_call" | custom-call | tf_op jit(solution)/shard_map/moments/pallas_call | solution.py:290
  (233 shorter events, 82.8 us)
Async XLA Ops:
  0.7 32.7 %collective-permute-start.3 = (bf16[3,768,256]{2,1,0:T(8,128)(2,1)}, bf16[3,768,256]{2,1,0:T(8,128)(2,1)}, u32[]{:S(2)}, u32[]{:S(2)}) collective-permute-start(bf16[3,768,256]{2,1,0:T(8,128)(2,1)} %bitcast.63), channel_id=1, source_target_pairs={{0,16},{16,0},{32,48},{48,32},{1,17},{17,1},{33,49},{49,33},{2,18}... | collective-permute-start | bytes 3538952 | tf_op jit(solution)/shard_map/ppermute | solution.py:24
  3.2 30.1 %collective-permute-start.4 = (bf16[3,768,256]{2,1,0:T(8,128)(2,1)}, bf16[3,768,256]{2,1,0:T(8,128)(2,1)}, u32[]{:S(2)}, u32[]{:S(2)}) collective-permute-start(bf16[3,768,256]{2,1,0:T(8,128)(2,1)} %bitcast.64), channel_id=1, source_target_pairs={{0,48},{16,32},{32,16},{48,0},{1,49},{17,33},{33,17},{49,1},{2,50}... | collective-permute-start | bytes 3538952 | tf_op jit(solution)/shard_map/ppermute | solution.py:24
  8.1 11.9 %collective-permute-start = (bf16[64,3072]{1,0:T(8,128)(2,1)S(1)}, bf16[64,3072]{1,0:T(8,128)(2,1)S(1)}, u32[]{:S(2)}, u32[]{:S(2)}) collective-permute-start(bf16[64,3072]{1,0:T(8,128)(2,1)S(1)} %constant_dynamic-update-slice_fusion), channel_id=1, source_target_pairs={{0,64},{64,0},{1,65},{65,1},{2,66},{66,2},{3,67},{67,3},{4,68},{68... | collective-permute-start | bytes 1179656 | tf_op jit(solution)/shard_map/ppermute | solution.py:24
  20.0 9.3 %collective-permute-start.1 = (bf16[64,3072]{1,0:T(8,128)(2,1)S(1)}, bf16[64,3072]{1,0:T(8,128)(2,1)S(1)}, u32[]{:S(2)}, u32[]{:S(2)}) collective-permute-start(bf16[64,3072]{1,0:T(8,128)(2,1)S(1)} %collective-permute-done), channel_id=1, source_target_pairs={{0,2},{2,0},{4,6},{6,4},{1,3},{3,1},{5,7},{7,5},{8,10},{10,8},{12,... | collective-permute-start | bytes 1179656 | tf_op jit(solution)/shard_map/ppermute | solution.py:24
  21.4 10.1 %collective-permute-start.2 = (bf16[64,3072]{1,0:T(8,128)(2,1)S(1)}, bf16[64,3072]{1,0:T(8,128)(2,1)S(1)}, u32[]{:S(2)}, u32[]{:S(2)}) collective-permute-start(bf16[64,3072]{1,0:T(8,128)(2,1)S(1)} %collective-permute-done), channel_id=1, source_target_pairs={{0,6},{2,4},{4,2},{6,0},{1,7},{3,5},{5,3},{7,1},{8,14},{10,12},{12... | collective-permute-start | bytes 1179656 | tf_op jit(solution)/shard_map/ppermute | solution.py:24
  23.3 10.0 %collective-permute-start.5 = (bf16[256,768]{1,0:T(8,128)(2,1)S(1)}, bf16[256,768]{1,0:T(8,128)(2,1)S(1)}, u32[]{:S(2)}, u32[]{:S(2)}) collective-permute-start(bf16[256,768]{1,0:T(8,128)(2,1)S(1)} %copy-done.26), channel_id=1, source_target_pairs={{0,64},{64,0},{1,65},{65,1},{2,66},{66,2},{3,67},{67,3},{4,68},{68... | collective-permute-start | bytes 1179656 | tf_op jit(solution)/shard_map/ppermute | solution.py:24
  34.5 13.1 %collective-permute-start.8 = (bf16[3,384,256]{2,1,0:T(8,128)(2,1)S(1)}, bf16[3,384,256]{2,1,0:T(8,128)(2,1)S(1)}, u32[]{:S(2)}, u32[]{:S(2)}) collective-permute-start(bf16[3,384,256]{2,1,0:T(8,128)(2,1)S(1)} %slice.193), channel_id=1, source_target_pairs={{0,48},{16,32},{32,16},{48,0},{1,49},{17,33},{33,17},{49,1},{2,50}... | collective-permute-start | bytes 1769480 | tf_op jit(solution)/shard_map/ppermute | solution.py:24
  36.3 11.7 %collective-permute-start.9 = (bf16[3,384,256]{2,1,0:T(8,128)(2,1)S(1)}, bf16[3,384,256]{2,1,0:T(8,128)(2,1)S(1)}, u32[]{:S(2)}, u32[]{:S(2)}) collective-permute-start(bf16[3,384,256]{2,1,0:T(8,128)(2,1)S(1)} %slice.194), channel_id=1, source_target_pairs={{0,16},{16,0},{32,48},{48,32},{1,17},{17,1},{33,49},{49,33},{2,18}... | collective-permute-start | bytes 1769480 | tf_op jit(solution)/shard_map/ppermute | solution.py:24
  36.7 9.8 %collective-permute-start.10 = (bf16[256,768]{1,0:T(8,128)(2,1)S(1)}, bf16[256,768]{1,0:T(8,128)(2,1)S(1)}, u32[]{:S(2)}, u32[]{:S(2)}) collective-permute-start(bf16[256,768]{1,0:T(8,128)(2,1)S(1)} %get-tuple-element.103), channel_id=1, source_target_pairs={{0,64},{64,0},{1,65},{65,1},{2,66},{66,2},{3,67},{67,3},{4,68},{68... | collective-permute-start | bytes 1179656 | tf_op jit(solution)/shard_map/ppermute | solution.py:24
  52.2 27.5 %collective-permute-start.11 = (bf16[768,768]{1,0:T(8,128)(2,1)S(1)}, bf16[768,768]{1,0:T(8,128)(2,1)S(1)}, u32[]{:S(2)}, u32[]{:S(2)}) collective-permute-start(bf16[768,768]{1,0:T(8,128)(2,1)S(1)} %copy-done.2), channel_id=1, source_target_pairs={{0,16},{16,0},{32,48},{48,32},{1,17},{17,1},{33,49},{49,33},{2,18}... | collective-permute-start | bytes 3538952 | tf_op jit(solution)/shard_map/ppermute | solution.py:24
  52.7 28.4 %collective-permute-start.12 = (bf16[768,768]{1,0:T(8,128)(2,1)S(1)}, bf16[768,768]{1,0:T(8,128)(2,1)S(1)}, u32[]{:S(2)}, u32[]{:S(2)}) collective-permute-start(bf16[768,768]{1,0:T(8,128)(2,1)S(1)} %copy-done.2), channel_id=1, source_target_pairs={{0,48},{16,32},{32,16},{48,0},{1,49},{17,33},{33,17},{49,1},{2,50}... | collective-permute-start | bytes 3538952 | tf_op jit(solution)/shard_map/ppermute | solution.py:24
  54.5 11.5 %collective-permute-start.14 = (bf16[256,768]{1,0:T(8,128)(2,1)S(1)}, bf16[256,768]{1,0:T(8,128)(2,1)S(1)}, u32[]{:S(2)}, u32[]{:S(2)}) collective-permute-start(bf16[256,768]{1,0:T(8,128)(2,1)S(1)} %get-tuple-element.114), channel_id=1, source_target_pairs={{0,64},{64,0},{1,65},{65,1},{2,66},{66,2},{3,67},{67,3},{4,68},{68... | collective-permute-start | bytes 1179656 | tf_op jit(solution)/shard_map/ppermute | solution.py:24
  66.0 31.8 %collective-permute-start.17 = (bf16[1024,384]{1,0:T(8,128)(2,1)S(1)}, bf16[1024,384]{1,0:T(8,128)(2,1)S(1)}, u32[]{:S(2)}, u32[]{:S(2)}) collective-permute-start(bf16[1024,384]{1,0:T(8,128)(2,1)S(1)} %get-tuple-element.115), channel_id=1, source_target_pairs={{0,64},{64,0},{1,65},{65,1},{2,66},{66,2},{3,67},{67,3},{4,68},{68... | collective-permute-start | bytes 2359304 | tf_op jit(solution)/shard_map/ppermute | solution.py:24
  82.0 14.9 %collective-permute-start.15 = (bf16[384,768]{1,0:T(8,128)(2,1)S(1)}, bf16[384,768]{1,0:T(8,128)(2,1)S(1)}, u32[]{:S(2)}, u32[]{:S(2)}) collective-permute-start(bf16[384,768]{1,0:T(8,128)(2,1)S(1)} %slice.204), channel_id=1, source_target_pairs={{0,48},{16,32},{32,16},{48,0},{1,49},{17,33},{33,17},{49,1},{2,50}... | collective-permute-start | bytes 1769480 | tf_op jit(solution)/shard_map/ppermute | solution.py:24
  83.8 13.4 %collective-permute-start.16 = (bf16[384,768]{1,0:T(8,128)(2,1)S(1)}, bf16[384,768]{1,0:T(8,128)(2,1)S(1)}, u32[]{:S(2)}, u32[]{:S(2)}) collective-permute-start(bf16[384,768]{1,0:T(8,128)(2,1)S(1)} %slice.205), channel_id=1, source_target_pairs={{0,16},{16,0},{32,48},{48,32},{1,17},{17,1},{33,49},{49,33},{2,18}... | collective-permute-start | bytes 1769480 | tf_op jit(solution)/shard_map/ppermute | solution.py:24
  99.9 11.1 %collective-permute-start.18 = (bf16[1024,256]{1,0:T(8,128)(2,1)S(1)}, bf16[1024,256]{1,0:T(8,128)(2,1)S(1)}, u32[]{:S(2)}, u32[]{:S(2)}) collective-permute-start(bf16[1024,256]{1,0:T(8,128)(2,1)S(1)} %pad_maximum_fusion.5.refs_0_), channel_id=1, source_target_pairs={{0,16},{16,0},{32,48},{48,32},{1,17},{17,1},{33,49},{49,33},{2,18}... | collective-permute-start | bytes 1572872 | tf_op jit(solution)/shard_map/ppermute | solution.py:24
  100.2 12.2 %collective-permute-start.19 = (bf16[1024,256]{1,0:T(8,128)(2,1)S(1)}, bf16[1024,256]{1,0:T(8,128)(2,1)S(1)}, u32[]{:S(2)}, u32[]{:S(2)}) collective-permute-start(bf16[1024,256]{1,0:T(8,128)(2,1)S(1)} %pad_maximum_fusion.5.refs_0_), channel_id=1, source_target_pairs={{0,48},{16,32},{32,16},{48,0},{1,49},{17,33},{33,17},{49,1},{2,50}... | collective-permute-start | bytes 1572872 | tf_op jit(solution)/shard_map/ppermute | solution.py:24
  102.3 18.2 %collective-permute-start.20 = (bf16[512,768]{1,0:T(8,128)(2,1)S(1)}, bf16[512,768]{1,0:T(8,128)(2,1)S(1)}, u32[]{:S(2)}, u32[]{:S(2)}) collective-permute-start(bf16[512,768]{1,0:T(8,128)(2,1)S(1)} %add_convert_fusion), channel_id=1, source_target_pairs={{0,64},{64,0},{1,65},{65,1},{2,66},{66,2},{3,67},{67,3},{4,68},{68... | collective-permute-start | bytes 2359304 | tf_op jit(solution)/shard_map/ppermute | solution.py:24
  112.5 8.0 %collective-permute-start.21 = (bf16[512,256]{1,0:T(8,128)(2,1)S(1)}, bf16[512,256]{1,0:T(8,128)(2,1)S(1)}, u32[]{:S(2)}, u32[]{:S(2)}) collective-permute-start(bf16[512,256]{1,0:T(8,128)(2,1)S(1)} %slice.211), channel_id=1, source_target_pairs={{0,48},{16,32},{32,16},{48,0},{1,49},{17,33},{33,17},{49,1},{2,50}... | collective-permute-start | bytes 786440 | tf_op jit(solution)/shard_map/ppermute | solution.py:24
  125.3 15.5 %collective-permute-start.23 = (bf16[512,768]{1,0:T(8,128)(2,1)S(1)}, bf16[512,768]{1,0:T(8,128)(2,1)S(1)}, u32[]{:S(2)}, u32[]{:S(2)}) collective-permute-start(bf16[512,768]{1,0:T(8,128)(2,1)S(1)} %fusion.2.refs_4_), channel_id=1, source_target_pairs={{0,16},{16,0},{32,48},{48,32},{1,17},{17,1},{33,49},{49,33},{2,18}... | collective-permute-start | bytes 2359304 | tf_op jit(solution)/shard_map/ppermute | solution.py:24
  125.7 16.4 %collective-permute-start.24 = (bf16[512,768]{1,0:T(8,128)(2,1)S(1)}, bf16[512,768]{1,0:T(8,128)(2,1)S(1)}, u32[]{:S(2)}, u32[]{:S(2)}) collective-permute-start(bf16[512,768]{1,0:T(8,128)(2,1)S(1)} %fusion.2.refs_4_), channel_id=1, source_target_pairs={{0,48},{16,32},{32,16},{48,0},{1,49},{17,33},{33,17},{49,1},{2,50}... | collective-permute-start | bytes 2359304 | tf_op jit(solution)/shard_map/ppermute | solution.py:24
  126.6 9.8 %collective-permute-start.25 = (bf16[256,768]{1,0:T(8,128)(2,1)S(1)}, bf16[256,768]{1,0:T(8,128)(2,1)S(1)}, u32[]{:S(2)}, u32[]{:S(2)}) collective-permute-start(bf16[256,768]{1,0:T(8,128)(2,1)S(1)} %get-tuple-element.143), channel_id=1, source_target_pairs={{0,64},{64,0},{1,65},{65,1},{2,66},{66,2},{3,67},{67,3},{4,68},{68... | collective-permute-start | bytes 1179656 | tf_op jit(solution)/shard_map/ppermute | solution.py:24
  143.0 18.7 %collective-permute-start.30 = (bf16[256,768]{1,0:T(8,128)(2,1)S(1)}, bf16[256,768]{1,0:T(8,128)(2,1)}, u32[]{:S(2)}, u32[]{:S(2)}) collective-permute-start(bf16[256,768]{1,0:T(8,128)(2,1)S(1)} %slice.218), channel_id=1, source_target_pairs={{0,48},{16,32},{32,16},{48,0},{1,49},{17,33},{33,17},{49,1},{2,50}... | collective-permute-start | bytes 1179656 | tf_op jit(solution)/shard_map/ppermute | solution.py:24
  145.2 16.5 %collective-permute-start.31 = (bf16[256,768]{1,0:T(8,128)(2,1)S(1)}, bf16[256,768]{1,0:T(8,128)(2,1)}, u32[]{:S(2)}, u32[]{:S(2)}) collective-permute-start(bf16[256,768]{1,0:T(8,128)(2,1)S(1)} %slice.219), channel_id=1, source_target_pairs={{0,16},{16,0},{32,48},{48,32},{1,17},{17,1},{33,49},{49,33},{2,18}... | collective-permute-start | bytes 1179656 | tf_op jit(solution)/shard_map/ppermute | solution.py:24
  147.5 8.7 %collective-permute-start.27 = (bf16[512,256]{1,0:T(8,128)(2,1)S(1)}, bf16[512,256]{1,0:T(8,128)(2,1)S(1)}, u32[]{:S(2)}, u32[]{:S(2)}) collective-permute-start(bf16[512,256]{1,0:T(8,128)(2,1)S(1)} %pad_maximum_fusion.7.refs_0_), channel_id=1, source_target_pairs={{0,16},{16,0},{32,48},{48,32},{1,17},{17,1},{33,49},{49,33},{2,18}... | collective-permute-start | bytes 786440 | tf_op jit(solution)/shard_map/ppermute | solution.py:24
  147.6 13.9 %collective-permute-start.28 = (bf16[512,256]{1,0:T(8,128)(2,1)S(1)}, bf16[512,256]{1,0:T(8,128)(2,1)S(1)}, u32[]{:S(2)}, u32[]{:S(2)}) collective-permute-start(bf16[512,256]{1,0:T(8,128)(2,1)S(1)} %pad_maximum_fusion.7.refs_0_), channel_id=1, source_target_pairs={{0,32},{16,48},{32,0},{48,16},{1,33},{17,49},{33,1},{49,17},{2,34}... | collective-permute-start | bytes 786440 | tf_op jit(solution)/shard_map/ppermute | solution.py:24
  149.4 12.2 %collective-permute-start.29 = (bf16[512,256]{1,0:T(8,128)(2,1)S(1)}, bf16[512,256]{1,0:T(8,128)(2,1)S(1)}, u32[]{:S(2)}, u32[]{:S(2)}) collective-permute-start(bf16[512,256]{1,0:T(8,128)(2,1)S(1)} %pad_maximum_fusion.7.refs_0_), channel_id=1, source_target_pairs={{0,48},{16,32},{32,16},{48,0},{1,49},{17,33},{33,17},{49,1},{2,50}... | collective-permute-start | bytes 786440 | tf_op jit(solution)/shard_map/ppermute | solution.py:24
  169.1 13.8 %collective-permute-start.32 = (bf16[2,4,256,768]{3,2,1,0:T(8,128)(2,1)}, bf16[2,4,256,768]{3,2,1,0:T(8,128)(2,1)}, u32[]{:S(2)}, u32[]{:S(2)}) collective-permute-start(bf16[2,4,256,768]{3,2,1,0:T(8,128)(2,1)} %project_out.3), channel_id=1, source_target_pairs={{0,1},{1,0},{2,3},{3,2},{4,5},{5,4},{6,7},{7,6},{8,9},{9,8},{10,11... | collective-permute-start | bytes 9437192 | tf_op jit(solution)/shard_map/ppermute | solution.py:24
  186.6 19.2 %collective-permute-start.33 = (bf16[4,128,768]{2,1,0:T(8,128)(2,1)S(1)}, bf16[4,128,768]{2,1,0:T(8,128)(2,1)S(1)}, u32[]{:S(2)}, u32[]{:S(2)}) collective-permute-start(bf16[4,128,768]{2,1,0:T(8,128)(2,1)S(1)} %slice.365), channel_id=1, source_target_pairs={{0,2},{2,0},{4,6},{6,4},{1,3},{3,1},{5,7},{7,5},{8,10},{10,8},{12,... | collective-permute-start | bytes 2359304 | tf_op jit(solution)/shard_map/ppermute | solution.py:24
  187.9 20.1 %collective-permute-start.34 = (bf16[4,128,768]{2,1,0:T(8,128)(2,1)S(1)}, bf16[4,128,768]{2,1,0:T(8,128)(2,1)S(1)}, u32[]{:S(2)}, u32[]{:S(2)}) collective-permute-start(bf16[4,128,768]{2,1,0:T(8,128)(2,1)S(1)} %slice.364), channel_id=1, source_target_pairs={{0,6},{2,4},{4,2},{6,0},{1,7},{3,5},{5,3},{7,1},{8,14},{10,12},{12... | collective-permute-start | bytes 2359304 | tf_op jit(solution)/shard_map/ppermute | solution.py:24
  209.0 9.8 %collective-permute-start.36 = (bf16[4,64,768]{2,1,0:T(8,128)(2,1)}, bf16[4,64,768]{2,1,0:T(8,128)(2,1)}, u32[]{:S(2)}, u32[]{:S(2)}) collective-permute-start(bf16[4,64,768]{2,1,0:T(8,128)(2,1)} %fusion.12), channel_id=1, source_target_pairs={{0,2},{2,0},{4,6},{6,4},{1,3},{3,1},{5,7},{7,5},{8,10},{10,8},{12,... | collective-permute-start | bytes 1179656 | tf_op jit(solution)/shard_map/ppermute | solution.py:24
  209.8 11.0 %collective-permute-start.35 = (bf16[4,64,768]{2,1,0:T(8,128)(2,1)}, bf16[4,64,768]{2,1,0:T(8,128)(2,1)}, u32[]{:S(2)}, u32[]{:S(2)}) collective-permute-start(bf16[4,64,768]{2,1,0:T(8,128)(2,1)} %fusion.13), channel_id=1, source_target_pairs={{0,6},{2,4},{4,2},{6,0},{1,7},{3,5},{5,3},{7,1},{8,14},{10,12},{12... | collective-permute-start | bytes 1179656 | tf_op jit(solution)/shard_map/ppermute | solution.py:24
  223.7 10.9 %collective-permute-start.40 = (bf16[4,32,768]{2,1,0:T(8,128)(2,1)S(1)}, bf16[4,32,768]{2,1,0:T(8,128)(2,1)S(1)}, u32[]{:S(2)}, u32[]{:S(2)}) collective-permute-start(bf16[4,32,768]{2,1,0:T(8,128)(2,1)S(1)} %get-tuple-element.212), channel_id=1, source_target_pairs={{0,72},{8,64},{64,8},{72,0},{1,73},{9,65},{65,9},{73,1},{2,74},{10... | collective-permute-start | bytes 589832 | tf_op jit(solution)/shard_map/ppermute | solution.py:441
  226.7 8.0 %collective-permute-start.38 = (bf16[4,32,768]{2,1,0:T(8,128)(2,1)S(1)}, bf16[4,32,768]{2,1,0:T(8,128)(2,1)S(1)}, u32[]{:S(2)}, u32[]{:S(2)}) collective-permute-start(bf16[4,32,768]{2,1,0:T(8,128)(2,1)S(1)} %slice.367), channel_id=1, source_target_pairs={{0,8},{8,0},{1,9},{9,1},{2,10},{10,2},{3,11},{11,3},{4,12},{12,4},... | collective-permute-start | bytes 589832 | tf_op jit(solution)/shard_map/ppermute | solution.py:24
  237.1 10.7 %collective-permute-start.43 = (bf16[256,768]{1,0:T(8,128)(2,1)S(1)}, bf16[256,768]{1,0:T(8,128)(2,1)S(1)}, u32[]{:S(2)}, u32[]{:S(2)}) collective-permute-start(bf16[256,768]{1,0:T(8,128)(2,1)S(1)} %fusion.16), channel_id=1, source_target_pairs={{0,8},{8,0},{1,9},{9,1},{2,10},{10,2},{3,11},{11,3},{4,12},{12,4},... | collective-permute-start | bytes 1179656 | tf_op jit(solution)/shard_map/ppermute | solution.py:24
  238.2 9.6 %collective-permute-start.42 = (bf16[512,384]{1,0:T(8,128)(2,1)S(1)}, bf16[512,384]{1,0:T(8,128)(2,1)S(1)}, u32[]{:S(2)}, u32[]{:S(2)}) collective-permute-start(bf16[512,384]{1,0:T(8,128)(2,1)S(1)} %pad_maximum_fusion.6), channel_id=1, source_target_pairs={{0,0},{2,16},{4,32},{6,48},{8,64},{10,80},{12,96},{14,112},{16,2},... | collective-permute-start | bytes 1179656 | tf_op jit(solution)/shard_map/ppermute | solution.py:455
  247.7 18.6 %collective-permute-start.44 = (bf16[512,384]{1,0:T(8,128)(2,1)S(1)}, bf16[512,384]{1,0:T(8,128)(2,1)S(1)}, u32[]{:S(2)}, u32[]{:S(2)}) collective-permute-start(bf16[512,384]{1,0:T(8,128)(2,1)S(1)} %collective-permute-done.42), channel_id=1, source_target_pairs={{0,64},{64,0},{1,65},{65,1},{2,66},{66,2},{3,67},{67,3},{4,68},{68... | collective-permute-start | bytes 1179656 | tf_op jit(solution)/shard_map/ppermute | solution.py:24
  252.7 30.8 %collective-permute-start.47 = (bf16[512,1152]{1,0:T(8,128)(2,1)}, bf16[512,1152]{1,0:T(8,128)(2,1)}, u32[]{:S(2)}, u32[]{:S(2)}) collective-permute-start(bf16[512,1152]{1,0:T(8,128)(2,1)} %maximum_maximum_fusion.refs_5_), channel_id=1, source_target_pairs={{0,2},{2,0},{4,6},{6,4},{1,3},{3,1},{5,7},{7,5},{8,10},{10,8},{12,... | collective-permute-start | bytes 3538952 | tf_op jit(solution)/shard_map/ppermute | solution.py:24
  259.7 31.4 %collective-permute-start.48 = (bf16[512,1152]{1,0:T(8,128)(2,1)}, bf16[512,1152]{1,0:T(8,128)(2,1)}, u32[]{:S(2)}, u32[]{:S(2)}) collective-permute-start(bf16[512,1152]{1,0:T(8,128)(2,1)} %maximum_maximum_fusion.refs_5_), channel_id=1, source_target_pairs={{0,6},{2,4},{4,2},{6,0},{1,7},{3,5},{5,3},{7,1},{8,14},{10,12},{12... | collective-permute-start | bytes 3538952 | tf_op jit(solution)/shard_map/ppermute | solution.py:24
  266.4 25.8 %collective-permute-start.45 = (bf16[1024,384]{1,0:T(8,128)(2,1)S(1)}, bf16[1024,384]{1,0:T(8,128)(2,1)S(1)}, u32[]{:S(2)}, u32[]{:S(2)}) collective-permute-start(bf16[1024,384]{1,0:T(8,128)(2,1)S(1)} %constant_dynamic-update-slice_fusion.9.refs_0_), channel_id=1, source_target_pairs={{0,16},{16,0},{32,48},{48,32},{1,17},{17,1},{33,49},{49,33},{2,18}... | collective-permute-start | bytes 2359304 | tf_op jit(solution)/shard_map/ppermute | solution.py:24
  266.5 26.3 %collective-permute-start.46 = (bf16[1024,384]{1,0:T(8,128)(2,1)S(1)}, bf16[1024,384]{1,0:T(8,128)(2,1)S(1)}, u32[]{:S(2)}, u32[]{:S(2)}) collective-permute-start(bf16[1024,384]{1,0:T(8,128)(2,1)S(1)} %constant_dynamic-update-slice_fusion.9.refs_0_), channel_id=1, source_target_pairs={{0,48},{16,32},{32,16},{48,0},{1,49},{17,33},{33,17},{49,1},{2,50}... | collective-permute-start | bytes 2359304 | tf_op jit(solution)/shard_map/ppermute | solution.py:24
  293.1 9.9 %collective-permute-start.49 = (bf16[512,384]{1,0:T(8,128)(2,1)S(1)}, bf16[512,384]{1,0:T(8,128)(2,1)S(1)}, u32[]{:S(2)}, u32[]{:S(2)}) collective-permute-start(bf16[512,384]{1,0:T(8,128)(2,1)S(1)} %slice.250), channel_id=1, source_target_pairs={{0,48},{16,32},{32,16},{48,0},{1,49},{17,33},{33,17},{49,1},{2,50}... | collective-permute-start | bytes 1179656 | tf_op jit(solution)/shard_map/ppermute | solution.py:24
  296.1 10.0 %collective-permute-start.50 = (bf16[512,384]{1,0:T(8,128)(2,1)S(1)}, bf16[512,384]{1,0:T(8,128)(2,1)S(1)}, u32[]{:S(2)}, u32[]{:S(2)}) collective-permute-start(bf16[512,384]{1,0:T(8,128)(2,1)S(1)} %slice.251), channel_id=1, source_target_pairs={{0,16},{16,0},{32,48},{48,32},{1,17},{17,1},{33,49},{49,33},{2,18}... | collective-permute-start | bytes 1179656 | tf_op jit(solution)/shard_map/ppermute | solution.py:24
  296.2 13.5 %collective-permute-start.51 = (bf16[256,1152]{1,0:T(8,128)(2,1)S(1)}, bf16[256,1152]{1,0:T(8,128)(2,1)}, u32[]{:S(2)}, u32[]{:S(2)}) collective-permute-start(bf16[256,1152]{1,0:T(8,128)(2,1)S(1)} %slice.283), channel_id=1, source_target_pairs={{0,6},{2,4},{4,2},{6,0},{1,7},{3,5},{5,3},{7,1},{8,14},{10,12},{12... | collective-permute-start | bytes 1769480 | tf_op jit(solution)/shard_map/ppermute | solution.py:24
  296.8 13.0 %collective-permute-start.52 = (bf16[256,1152]{1,0:T(8,128)(2,1)S(1)}, bf16[256,1152]{1,0:T(8,128)(2,1)}, u32[]{:S(2)}, u32[]{:S(2)}) collective-permute-start(bf16[256,1152]{1,0:T(8,128)(2,1)S(1)} %slice.284), channel_id=1, source_target_pairs={{0,2},{2,0},{4,6},{6,4},{1,3},{3,1},{5,7},{7,5},{8,10},{10,8},{12,... | collective-permute-start | bytes 1769480 | tf_op jit(solution)/shard_map/ppermute | solution.py:24
  296.8 17.3 %collective-permute-start.53 = (bf16[512,1152]{1,0:T(8,128)(2,1)}, bf16[512,1152]{1,0:T(8,128)(2,1)}, u32[]{:S(2)}, u32[]{:S(2)}) collective-permute-start(bf16[512,1152]{1,0:T(8,128)(2,1)} %maximum_maximum_fusion.refs_5_), channel_id=1, source_target_pairs={{0,1},{1,0},{2,3},{3,2},{4,5},{5,4},{6,7},{7,6},{8,9},{9,8},{10,11... | collective-permute-start | bytes 3538952 | tf_op jit(solution)/shard_map/ppermute | solution.py:24
  303.0 13.2 %collective-permute-start.54 = (bf16[512,1152]{1,0:T(8,128)(2,1)}, bf16[512,1152]{1,0:T(8,128)(2,1)}, u32[]{:S(2)}, u32[]{:S(2)}) collective-permute-start(bf16[512,1152]{1,0:T(8,128)(2,1)} %collective-permute-done.47.refs_6_), channel_id=1, source_target_pairs={{0,1},{1,0},{2,3},{3,2},{4,5},{5,4},{6,7},{7,6},{8,9},{9,8},{10,11... | collective-permute-start | bytes 3538952 | tf_op jit(solution)/shard_map/ppermute | solution.py:24
  306.2 10.0 %collective-permute-start.57 = (bf16[512,1152]{1,0:T(8,128)(2,1)}, bf16[512,1152]{1,0:T(8,128)(2,1)}, u32[]{:S(2)}, u32[]{:S(2)}) collective-permute-start(bf16[512,1152]{1,0:T(8,128)(2,1)} %collective-permute-done.48.refs_9_), channel_id=1, source_target_pairs={{0,1},{1,0},{2,3},{3,2},{4,5},{5,4},{6,7},{7,6},{8,9},{9,8},{10,11... | collective-permute-start | bytes 3538952 | tf_op jit(solution)/shard_map/ppermute | solution.py:24
  (40 other events, 479.8 us)
